TPU v7x, 32 devices: a whole 2x2x4 slice. The times are simulated.
32 devices in a mesh: tower: 2 (over core), dp: 16 (over z, y, x).
Axes of the slice: x: 2, y: 2, z: 4, core: 2. Of those that a mesh axis runs over, the one named last changes fastest.
Arguments:
- picture_layer_entry: bfloat16 [768, 50, 768], P('dp'), may hold values from -6 to 6
- caption_layer_entry: bfloat16 [768, 16, 768], P('dp'), may hold values from -6 to 6
- usable_match_tallies: int32 [16], P('dp'), may hold values from 1 to 48, 576 in all
- similarity_exponent_factor: float32 [1], replicated, may hold values from 3.6 to 4.2
- picture_standardize_factors: bfloat16 [2, 768], replicated, may hold values from 0.5 to 1.5
- picture_layer_offsets: bfloat16 [6, 768], replicated, may hold values from -0.59765625 to 0.59765625
- picture_inner_offset: bfloat16 [3072], replicated, may hold values from -1.1953125 to 1.1953125
- picture_attend_entry_matrix: bfloat16 [768, 2304], replicated, may hold values from -0.21875 to 0.21875
- picture_attend_exit_matrix: bfloat16 [768, 768], replicated, may hold values from -1.5 to 1.5
- picture_widening_matrix: bfloat16 [768, 3072], replicated, may hold values from -0.21875 to 0.21875
- picture_narrowing_matrix: bfloat16 [3072, 768], replicated, may hold values from -0.109375 to 0.109375
- caption_standardize_factors: bfloat16 [2, 768], replicated, may hold values from 0.5 to 1.5
- caption_layer_offsets: bfloat16 [6, 768], replicated, may hold values from -0.59765625 to 0.59765625
- caption_inner_offset: bfloat16 [3072], replicated, may hold values from -1.1953125 to 1.1953125
- caption_attend_entry_matrix: bfloat16 [768, 2304], replicated, may hold values from -0.21875 to 0.21875
- caption_attend_exit_matrix: bfloat16 [768, 768], replicated, may hold values from -0.875 to 0.875
- caption_widening_matrix: bfloat16 [768, 3072], replicated, may hold values from -0.21875 to 0.21875
- caption_narrowing_matrix: bfloat16 [3072, 768], replicated, may hold values from -0.109375 to 0.109375
Outputs:
- loss: float32 [1], replicated
- exponent_derivative: float32 [1], replicated
- grad_tokens: float32 [768, 16, 768], P('dp', 'tower')
- grad_gains: float32 [2, 768], P('tower', 'dp')
- grad_biases: float32 [6, 768], P('tower', 'dp')
- grad_hidbias: float32 [3072], P(('tower', 'dp'))
- grad_qkv: float32 [768, 2304], P('dp', 'tower')
- grad_project: float32 [768, 768], P('dp', 'tower')
- grad_expand: float32 [768, 3072], P('dp', 'tower')
- grad_reduce: float32 [3072, 768], P(('tower', 'dp'))
Inputs may be any that keep to these rules, and one draw needn't show every extreme that they name: Index d of dp holds usable_match_tallies[d] valid pairs in its first slots of 48; the others are padding.
All inputs are finite; a program needn't handle non-finite values. No bound on the sum of `usable_match_tallies` on one device may be relied on, other than what follows from the above.
Results may differ from a plain program's by a relative error of at most 0.01.
The roundings to bfloat16 on the way count: a program that leaves them out, or rounds other values in their place, can miss the bound.
Values may be sent and summed in bfloat16 or wider, within the bound.
No kernel may reach another device: no remote copies, remote signals or barrier semaphores. Data moves between devices by JAX's collectives and lax.ppermute only.
A program may use at most 192 MiB of HBM per device.

v0:
```python
from functools import partial

import jax
import jax.numpy as jnp
import numpy as np
from jax import lax
from jax.experimental import pallas as pl
from jax.experimental.pallas import tpu as pltpu
from jax.sharding import PartitionSpec as P

F32 = jnp.float32
BF16 = jnp.bfloat16
HEAD_DIM = 64
LANES = 128
EXTRA = 120
norm_eps = 1e-06
embed_eps = 1e-06
NEG = -1000000000.0
VMEM_LIMIT = 60 * 1024 * 1024


def normal_cdf(x):
    return 0.5 + 0.5 * lax.erf(x * 0.7071067811865476)


def load(src, dst, sem):
    copy = pltpu.make_async_copy(src, dst, sem)
    copy.start()
    return copy


def dot(a, b):
    return jnp.dot(a, b, preferred_element_type=F32)


def dot_nt(a, b):
    return lax.dot_general(a, b, (((1,), (1,)), ((), ())), preferred_element_type=F32)


def dot_tn(a, b):
    return lax.dot_general(a, b, (((0,), (0,)), ((), ())), preferred_element_type=F32)


def norm_stats(x):
    mean = jnp.mean(x, axis=-1, keepdims=True)
    centered = x - mean
    rstd = lax.rsqrt(jnp.mean(centered * centered, axis=-1, keepdims=True) + norm_eps)
    return centered * rstd, rstd


def norm_back(dxhat, xhat, rstd):
    return rstd * (
        dxhat
        - jnp.mean(dxhat, axis=-1, keepdims=True)
        - xhat * jnp.mean(dxhat * xhat, axis=-1, keepdims=True)
    )


def row(ref, i):
    return ref[i : i + 1, :].astype(F32)


def head_masks():
    lane = lax.broadcasted_iota(jnp.int32, (1, LANES), 1)
    first = (lane < HEAD_DIM).astype(BF16)
    return first, (1 - first).astype(BF16)


def set_qkv_bias(out, biases):
    width = biases.shape[1]
    out[:, :width] = row(biases, 2)
    out[:, width : 2 * width] = jnp.zeros((1, width), F32)
    out[:, 2 * width :] = row(biases, 3)


def two_heads(x, masks):
    return jnp.concatenate([x * masks[0], x * masks[1]], axis=0)


def softmax_parts(scores, bias):
    keys = scores.shape[1] // 2
    parts = []
    for e in range(2):
        s = scores[:, e * keys : (e + 1) * keys] + bias
        parts.append(jnp.exp(s - jnp.max(s, axis=-1, keepdims=True)))
    return parts


def attend(q2, k2, v2, bias, masks):
    e0, e1 = softmax_parts(dot_nt(q2 * BF16(0.125), two_heads(k2, masks)), bias)
    weights = jnp.concatenate([e0.astype(BF16), e1.astype(BF16)], axis=1)
    ones = jnp.ones((k2.shape[0], LANES), BF16)
    right = jnp.concatenate([two_heads(v2, masks), two_heads(ones, masks)], axis=1)
    out = dot(weights, right)
    return (out[:, :LANES] / out[:, LANES:]).astype(BF16)


def split_dot(x, w):
    hi = x.astype(BF16)
    lo = (x - hi.astype(F32)).astype(BF16)
    n = x.shape[0]
    out = dot(jnp.concatenate([hi, lo], axis=0), w)
    return out[:n] + out[n:]


def text_forward_kernel(
    scal, h_any, gains, biases, hid, wq_any, wp_any, we_any, wr_any,
    a_any, qkv_any, o_any, m_any, c_any, gpk_any, gps_any, send_out, emb_out, r_out,
    h_v, wq, wp, we, wr, qb, av, cv, gsum, a_out, qkv_out, o_out, m_out, c_out, gp_keep, gp_send,
    sems, out_sems,
):
    n, width = m_out.shape
    caps = emb_out.shape[0]
    length = n // caps
    hidden = hid.shape[1]
    t, d = scal[0], scal[1]
    load_h = load(h_any.at[pl.ds(pl.multiple_of(t * n, n), n)], h_v, sems.at[0])
    load_q = load(wq_any, wq, sems.at[1])
    load_h.wait()
    masks = head_masks()

    def put_transposed(out, src):
        count, rows = out.shape[:2]

        def turn(i, carry):
            lanes = pl.ds(pl.multiple_of(i * (width // 2), LANES), width // 2)
            turned = src[:, lanes].astype(F32).T.astype(BF16)
            for e in range(count // 2):
                out[scal[4 + i * (count // 2) + e]] = turned[e * rows : (e + 1) * rows, :]
            return carry

        lax.fori_loop(0, 2, turn, 0, unroll=2)

    h = h_v[...].astype(F32)
    xhat, _ = norm_stats(h)
    a = xhat * row(gains, 0) + row(biases, 0)
    av[...] = a.astype(BF16)
    load_q.wait()
    load_p = load(wp_any, wp, sems.at[2])
    load_e = load(we_any, we, sems.at[3])
    load_r = load(wr_any, wr, sems.at[4])
    set_qkv_bias(qb, biases)

    def to_qkv(j, carry):
        cols = pl.ds(pl.multiple_of(j * 256, 256), 256)
        qkv_out[:, cols] = (dot(av[...], wq[:, cols]) + qb[:, cols]).astype(BF16)
        return carry

    lax.fori_loop(0, 3 * width // 256, to_qkv, 0, unroll=9)
    put_transposed(a_out, av)
    stores = [load(qkv_out, qkv_any, out_sems.at[0]), load(a_out, a_any, out_sems.at[1])]
    same = (
        lax.broadcasted_iota(jnp.int32, (LANES, LANES), 0) // length
        == lax.broadcasted_iota(jnp.int32, (LANES, LANES), 1) // length
    )
    bias = jnp.where(same, 0.0, -1e30)

    def attention(g, carry):
        rows = pl.ds(pl.multiple_of(g * LANES, LANES), LANES)
        for p in range(width // LANES):
            lanes = slice(p * LANES, (p + 1) * LANES)
            q2 = qkv_out[rows, lanes]
            k2 = qkv_out[rows, width + p * LANES : width + (p + 1) * LANES]
            v2 = qkv_out[rows, 2 * width + p * LANES : 2 * width + (p + 1) * LANES]
            av[rows, lanes] = attend(q2, k2, v2, bias, masks)
        return carry

    lax.fori_loop(0, n // LANES, attention, 0)
    load_p.wait()
    m = h_v[...].astype(F32) + dot(av[...], wp[...]) + row(biases, 4)
    m_out[...] = m
    stores.append(load(m_out, m_any, out_sems.at[2]))
    xhat, _ = norm_stats(m)
    c = xhat * row(gains, 1) + row(biases, 1)
    cv[...] = c.astype(BF16)
    put_transposed(c_out, cv)
    put_transposed(o_out, av)
    stores.append(load(c_out, c_any, out_sems.at[3]))
    stores.append(load(o_out, o_any, out_sems.at[4]))
    load_e.wait()
    half = hidden // 512

    def feed(rel, gp_out):
        def step(j, carry):
            local = pl.ds(pl.multiple_of(j * 256, 256), 256)
            at = jnp.bitwise_xor(t, rel) * half + j
            cols = pl.ds(pl.multiple_of(at * 256, 256), 256)
            f = dot(cv[...], we[:, cols]) + hid[:, cols].astype(F32)
            cdf = normal_cdf(f)
            density = jnp.exp(f * f * -0.5) * 0.3989422804014327
            gp_out[:, local] = (cdf + f * density).astype(BF16)
            gsum[:, cols] = jnp.sum((f * cdf).reshape(caps, length, 256), axis=1)
            return carry

        lax.fori_loop(0, half, step, 0, unroll=2)

    feed(1, gp_send)
    stores.append(load(gp_send, gps_any, out_sems.at[5]))
    feed(0, gp_keep)
    stores.append(load(gp_keep, gpk_any, out_sems.at[6]))
    load_r.wait()
    total = gsum[...]
    pooled = (
        jnp.mean(m_out[...].reshape(caps, length, width), axis=1)
        + split_dot(total * (1.0 / length), wr[...])
        + row(biases, 5)
    )
    r = lax.rsqrt(jnp.sum(pooled * pooled, axis=-1, keepdims=True) + embed_eps)
    emb_out[...] = pooled * r
    r_out[...] = jnp.broadcast_to(r, r_out.shape)
    chips = send_out.shape[0]
    share = hidden // (2 * chips)
    scaled = total * r
    hi = r.astype(BF16).astype(F32)
    mid = (r - hi).astype(BF16).astype(F32)
    slot = lax.broadcasted_iota(jnp.int32, (caps, LANES), 0) + t * caps
    lane = lax.broadcasted_iota(jnp.int32, (caps, LANES), 1)
    extra = jnp.where(lane == EXTRA, hi, 0.0)
    extra = jnp.where(lane == EXTRA + 1, mid, extra)
    extra = jnp.where(lane == EXTRA + 2, r - hi - mid, extra)
    extra = jnp.where((lane == EXTRA + 3) & (slot < scal[2]), 1.0, extra)
    for e in range(chips):
        send_out[e, :, :width] = (pooled * r).astype(BF16)
        for half_at in range(2):
            src = (half_at * chips + e) * share
            piece = jnp.concatenate([scaled[:, src : src + share], extra[:, share:]], axis=1)
            to = width + jnp.bitwise_xor(t, half_at) * LANES
            send_out[e, :, pl.ds(pl.multiple_of(to, LANES), LANES)] = piece.astype(BF16)
    for c in stores:
        c.wait()


PAD = 56


def image_forward_kernel(
    scal, x_any, gains, biases, hid, wq_any, wp_any, we_any, wr_any,
    out,
    x_v, xs, hv, av, qkv, mv, msum, gsum, wq, wp, we, wr, qb, pb, sems,
):
    length, both_caps, width = x_v.shape
    caps = both_caps // 2
    n = caps * PAD
    hidden = hid.shape[1]
    t = scal[0]
    load_x = load(x_any, x_v, sems.at[0])
    load_q = load(wq_any, wq, sems.at[1])
    masks = head_masks()
    qkv[n:, :] = jnp.zeros((qkv.shape[0] - n, 3 * width), BF16)
    first = (jnp.zeros((1, 1), jnp.int32) + t) == 0
    load_x.wait()

    def pick(i, carry):
        x = x_v[i].astype(F32)
        x = jnp.where(first, x[:caps], x[caps:])
        for k in range(width // LANES):
            xs[k, pl.ds(pl.multiple_of(i * caps, 8), caps), :] = x[:, k * LANES : (k + 1) * LANES]
        return carry

    lax.fori_loop(0, length, pick, 0, unroll=2)

    def first_norm(j, carry):
        base = pl.multiple_of(j * 2 * PAD, 16)
        for e in range(2):
            x = jnp.concatenate(
                [
                    xs[k, pl.ds(j * 2 + e, length, stride=caps), :]
                    for k in range(width // LANES)
                ],
                axis=1,
            )
            x = jnp.concatenate([x, jnp.zeros((PAD - length, width), F32)], axis=0)
            hv[pl.ds(base + e * PAD, PAD), :] = x
            xhat, _ = norm_stats(x)
            x = xhat * row(gains, 0) + row(biases, 0)
            if e == 0:
                kept = x
        av[pl.ds(base, 2 * PAD), :] = jnp.concatenate([kept, x], axis=0).astype(BF16)
        return carry

    lax.fori_loop(0, caps // 2, first_norm, 0, unroll=4)
    load_q.wait()
    load_p = load(wp_any, wp, sems.at[2])
    load_e = load(we_any, we, sems.at[3])
    load_r = load(wr_any, wr, sems.at[4])
    set_qkv_bias(qb, biases)

    def to_qkv(j, carry):
        cols = pl.ds(pl.multiple_of(j * 256, 256), 256)
        qkv[:n, cols] = (dot(av[...], wq[:, cols]) + qb[:, cols]).astype(BF16)
        return carry

    lax.fori_loop(0, 3 * width // 256, to_qkv, 0, unroll=9)
    q_at = lax.broadcasted_iota(jnp.int32, (2 * PAD, LANES), 0)
    k_at = lax.broadcasted_iota(jnp.int32, (2 * PAD, LANES), 1)
    low = (q_at < PAD) & (k_at < length)
    high = (q_at >= PAD) & (k_at >= PAD) & (k_at < PAD + length)
    bias = jnp.where(low | high, 0.0, -1e30)

    def attention(j, carry):
        base = pl.multiple_of(j * 2 * PAD, 16)
        rows, keys = pl.ds(base, 2 * PAD), pl.ds(base, LANES)
        for p in range(width // LANES):
            lanes = slice(p * LANES, (p + 1) * LANES)
            q2 = qkv[rows, lanes]
            k2 = qkv[keys, width + p * LANES : width + (p + 1) * LANES]
            v2 = qkv[keys, 2 * width + p * LANES : 2 * width + (p + 1) * LANES]
            av[rows, lanes] = attend(q2, k2, v2, bias, masks)
        return carry

    lax.fori_loop(0, caps // 2, attention, 0, unroll=2)
    load_p.wait()
    pb[...] = row(biases, 4)

    def add_attended(j, carry):
        cols = pl.ds(pl.multiple_of(j * 256, 256), 256)
        mv[:, cols] = hv[:, cols] + dot(av[...], wp[:, cols]) + pb[:, cols]
        return carry

    lax.fori_loop(0, width // 256, add_attended, 0, unroll=3)
    group = 8 * PAD
    tail = (lax.broadcasted_iota(jnp.int32, (1, 8, 1), 1) < length - (PAD - 8)).astype(F32)

    def token_sum(x, count):
        tiles = x.reshape(count, PAD // 8, 8, x.shape[1])
        acc = tiles[:, PAD // 8 - 1] * tail
        for i in range(PAD // 8 - 1):
            acc = acc + tiles[:, i]
        return jnp.sum(acc, axis=1)

    def second_norm(j, carry):
        rows = pl.ds(pl.multiple_of(j * group, 16), group)
        m = mv[rows, :]
        xhat, _ = norm_stats(m)
        av[rows, :] = (xhat * row(gains, 1) + row(biases, 1)).astype(BF16)
        msum[pl.ds(pl.multiple_of(j * 8, 8), 8), :] = token_sum(m, 8)
        return carry

    lax.fori_loop(0, caps // 8, second_norm, 0)
    load_e.wait()

    def feed(j, carry):
        cols = pl.ds(pl.multiple_of(j * 256, 256), 256)
        f = dot(av[...], we[:, cols]) + hid[:, cols].astype(F32)
        gsum[:, cols] = token_sum(f * normal_cdf(f), caps)
        return carry

    lax.fori_loop(0, hidden // 256, feed, 0, unroll=2)
    load_r.wait()
    scale = 1.0 / length
    pooled = msum[...] * scale + split_dot(gsum[...] * scale, wr[...]) + row(biases, 5)
    r_img = lax.rsqrt(jnp.sum(pooled * pooled, axis=-1, keepdims=True) + embed_eps)
    out[...] = (pooled * r_img).astype(BF16)


QUARTERS = ((1, 3), (2, 3), (0, 2), (0, 1))


def loss_kernel(
    rows_block, parts, scal, *refs,
):
    own_any, refs = refs[:parts], refs[parts:]
    (par_any, text_any, text_par_any, expo, emb, r, gpk_any, gpr_any, ct_any, ctr_any,
     we_any, wr_any,
     loss_out, temp_out, ea, eb, ec, ed, g_any, images_any, texts_any, gall_any, extra_any,
     dc_any, dy_out, hid_out,
     own_v, par_v, text_v, text_par_v, texts, images, extra, gall, col_flag, sims, grad,
     chip_g, gpk, gpr, ct, we, wr, dc, exp_s, sems, out_sems) = refs
    chips, caps, width = par_any.shape
    staged = own_v.shape[0] == chips
    total = texts.shape[0]
    near_hidden = gpk.shape[1]
    n = dc.shape[0]
    length = n // caps
    t, d = scal[0], scal[1]
    first = (jnp.zeros((1, 1), jnp.int32) + t) == 0
    if staged:
        each = chips // parts
        waits = [
            load(par_any, par_v, sems.at[0]),
            load(text_any, text_v, sems.at[1]),
            load(text_par_any, text_par_v, sems.at[2]),
        ] + [
            load(own_any[i], own_v.at[pl.ds(i * each, each)], sems.at[3 + i]) for i in range(parts)
        ]
        for c in waits:
            c.wait()

    def place(e, carry):
        at, slot = e, scal[4 + 16 + e]
        if not staged:
            waits = [
                load(src.at[pl.ds(i, 1)], dst, sems.at[j])
                for j, (src, i, dst) in enumerate(
                    ((own_any[0], slot, own_v), (par_any, slot, par_v), (text_any, at, text_v),
                     (text_par_any, at, text_par_v))
                )
            ]
            for c in waits:
                c.wait()
            at = slot = 0

        def pair(x0, x1):
            x0, x1 = x0.astype(F32), x1.astype(F32)
            return jnp.concatenate([jnp.where(first, x0, x1), jnp.where(first, x1, x0)], axis=0)

        rows = pl.ds(pl.multiple_of(e * 2 * caps, 16), 2 * caps)
        images[rows, :] = pair(own_v[slot], par_v[slot]).astype(BF16)
        x0, x1 = text_v[at], text_par_v[at]
        texts[rows, :] = pair(x0[:, :width], x1[:, :width]).astype(BF16)
        last = pair(x0[:, width : width + LANES], x1[:, width + LANES :])
        extra[rows, :] = last
        gall[rows, :] = last.astype(BF16)
        return carry

    lax.fori_loop(0, chips, place, 0, unroll=2)
    half = near_hidden // 256
    later = [
        load(src, dst, sems.at[8 + i])
        for i, (src, dst) in enumerate(
            ((wr_any.at[pl.ds(pl.multiple_of(t * near_hidden, 256), near_hidden)], wr),
             (gpk_any, gpk), (gpr_any, gpr),
             (we_any.at[:, pl.ds(pl.multiple_of(t * near_hidden, 256), near_hidden)], we))
        )
    ]
    for i, src in enumerate((ct_any, ctr_any)):
        later.append(load(src, ct.at[i], sems.at[12 + i]))
    stores = [
        load(src, dst, out_sems.at[i])
        for i, (src, dst) in enumerate(
            ((images, images_any), (texts, texts_any), (gall, gall_any), (extra, extra_any))
        )
    ]
    pick = (lax.broadcasted_iota(jnp.int32, (8, LANES), 1) == EXTRA + 3).astype(F32)
    step = min(256, total)

    def flags(j, carry):
        cols = pl.ds(pl.multiple_of(j * step, step), step)
        col_flag[:, cols] = dot_nt(pick, extra[cols, :])
        return carry

    lax.fori_loop(0, total // step, flags, 0)
    scale = jnp.exp(jnp.full((1, 1), expo[0], F32))
    chunk = 48
    blocks = total // rows_block
    per_block = rows_block // chunk
    live = col_flag[0:1, :]

    def similarities(b):
        base = pl.multiple_of(b * rows_block, 16)

        def cols_step(j, carry):
            cols = pl.ds(pl.multiple_of(j * step, step), step)
            sims[:, cols] = scale * dot_nt(texts[pl.ds(base, rows_block), :], images[cols, :])
            return carry

        lax.fori_loop(0, total // step, cols_step, 0)

    def chunk_at(b, i):
        local = pl.ds(pl.multiple_of(i * chunk, 16), chunk)
        whole = pl.ds(pl.multiple_of(b * rows_block + i * chunk, 16), chunk)
        return local, whole

    def column_block(b, acc):
        similarities(b)

        def adding(i, acc):
            local, whole = chunk_at(b, i)
            live_row = extra[whole, EXTRA + 3 : EXTRA + 4]
            part = jnp.exp(sims[local, :]) * live_row
            return acc + jnp.sum(part.reshape(chunk // 8, 8, total), axis=0)

        return lax.fori_loop(0, per_block, adding, acc, unroll=2)

    col_acc = jnp.zeros((8, total), F32)
    if blocks == 1:
        col_acc = column_block(0, col_acc)
    else:
        col_acc = lax.fori_loop(0, blocks, column_block, col_acc)
    col_sum = jnp.sum(col_acc, axis=0, keepdims=True)
    col_part = 0.5 * live / col_sum

    def row_block(b, carry):
        if blocks > 1:
            similarities(b)

        def rows_step(i, acc):
            loss, temp, diag = acc
            local, whole = chunk_at(b, i)
            s = sims[local, :]
            flag = extra[whole, EXTRA + 3 : EXTRA + 4]
            at = lax.broadcasted_iota(jnp.int32, (chunk, total), 0) + (b * rows_block + i * chunk)
            eye = at == lax.broadcasted_iota(jnp.int32, (chunk, total), 1)
            expd = jnp.exp(s)
            rsum = jnp.sum(expd * live, axis=1, keepdims=True)
            g = expd * ((0.5 * flag / rsum) * live + flag * col_part)
            g = g - jnp.where(eye, 0.5 * (flag + live), 0.0)
            grad[local, :] = g.astype(BF16)
            temp = temp + jnp.sum((g * s).reshape(chunk // 8, 8, total), axis=0)
            diag = diag + jnp.sum(
                jnp.where(eye, s * flag, 0.0).reshape(chunk // 8, 8, total), axis=0
            )
            return loss + 0.5 * flag * jnp.log(rsum), temp, diag

        carry = lax.fori_loop(0, per_block, rows_step, carry, unroll=2)
        mine = d * (2 * caps) - b * rows_block

        @pl.when((mine >= 0) & (mine < rows_block))
        def _():
            chip_g[...] = grad[pl.ds(pl.multiple_of(mine, 16), 2 * caps), :]

        if blocks > 1:
            rows = pl.ds(pl.multiple_of(b * rows_block, 16), rows_block)
            load(grad, g_any.at[rows], out_sems.at[4]).wait()
        return carry

    start = (jnp.zeros((chunk, 1), F32), jnp.zeros((8, total), F32), jnp.zeros((8, total), F32))
    if blocks == 1:
        loss, temp, diag = row_block(0, start)
        stores.append(load(grad, g_any, out_sems.at[4]))
    else:
        loss, temp, diag = lax.fori_loop(0, blocks, row_block, start)
    def whole(x):
        return jnp.sum(jnp.sum(x, axis=0, keepdims=True), axis=1, keepdims=True)

    objective = whole(loss) + 0.5 * whole(live * jnp.log(col_sum)) - whole(diag)
    loss_out[...] = objective / whole(live)
    temp_out[...] = whole(temp)

    both_dt = scale * dot(chip_g[...], images[...])
    chip = pl.ds(pl.multiple_of(d * 2 * caps, 16), 2 * caps)
    inv = jnp.sum(extra[chip, EXTRA : EXTRA + 3], axis=1, keepdims=True)
    dt = jnp.where(first, both_dt[:caps], both_dt[caps:])
    dt_far = jnp.where(first, both_dt[caps:], both_dt[:caps])
    both_tx = texts[chip, :].astype(F32)
    tx_far = jnp.where(first, both_tx[caps:], both_tx[:caps])
    inv_far = jnp.where(first, inv[caps:], inv[:caps])

    def pooled_back(tx, dt, inv):
        return inv * (dt - tx * jnp.sum(tx * dt, axis=1, keepdims=True)) * (1.0 / length)

    dy = pooled_back(emb[...], dt, r[:, 0:1])
    dy_out[...] = dy
    dyb = jnp.concatenate([dy, pooled_back(tx_far, dt_far, inv_far)], axis=0).astype(BF16)
    for c in later:
        c.wait()
    dc[...] = jnp.zeros_like(dc)

    def near(j, carry):
        cols = pl.ds(pl.multiple_of(j * 256, 256), 256)
        dg = dot_nt(dyb, wr[cols, :])
        df = (gpk[:, cols].astype(F32).reshape(caps, length, 256) * dg[:caps][:, None, :]).reshape(
            n, 256
        )
        far = (gpr[:, cols].astype(F32).reshape(caps, length, 256) * dg[caps:][:, None, :]).reshape(
            n, 256
        )
        df, far = df.astype(BF16), far.astype(BF16)
        hid_out[0:1, cols] = jnp.sum(df.astype(F32) + far.astype(F32), axis=0, keepdims=True)
        dc[...] += dot_nt(df, we[:, cols])
        side = near_hidden // 512
        local = pl.ds(pl.multiple_of((j % side) * 256, 256), 256)
        exp_s[j // side, :, local] = (
            dot(ct[0].reshape(width, n), df) + dot(ct[1].reshape(width, n), far)
        ).astype(BF16)
        return carry

    lax.fori_loop(0, half, near, 0, unroll=2)
    quarter = width // 4
    for i, out in enumerate((ea, eb, ec, ed)):
        for j, q in enumerate(QUARTERS[i]):
            stores.append(
                load(
                    exp_s.at[i % 2, pl.ds(q * quarter, quarter)],
                    out.at[pl.ds(j * quarter, quarter)],
                    out_sems.at[5 + 2 * i + j],
                )
            )
    stores.append(load(dc, dc_any, out_sems.at[13]))
    for c in stores:
        c.wait()


def middle_back_kernel(
    scal, dc_any, dy, gps_any, m_any, gains, we_any, wr_any, wp_any, qkv_any,
    dm_any, dqkv_any, vec_out,
    dc, gps, mv, we, wr, wp, qkv, dm, dmb, dov, dqkv, sems,
):
    n, width = dm.shape
    caps = dy.shape[0]
    length = n // caps
    far_hidden = gps.shape[1]
    t = scal[0]
    away = pl.ds(pl.multiple_of((1 - t) * far_hidden, 256), far_hidden)
    half = far_hidden // 512
    parts = []
    for i in range(2):
        at = pl.ds(pl.multiple_of(((1 - t) * 2 + i) * half * 256, 256), half * 256)
        here = pl.ds(i * half * 256, half * 256)
        parts.append([
            load(wr_any.at[at], wr.at[here], sems.at[3 * i]),
            load(gps_any.at[:, here], gps.at[:, here], sems.at[3 * i + 1]),
            load(we_any.at[:, at], we.at[:, here], sems.at[3 * i + 2]),
        ])
        if i == 0:
            load_dc = load(dc_any, dc, sems.at[9])
    for c in parts[0]:
        c.wait()
    load_dc.wait()
    load_m = load(m_any, mv, sems.at[10])
    load_p = load(wp_any, wp, sems.at[11])
    load_qkv = load(qkv_any, qkv, sems.at[6])
    dyv = dy[...]
    dyb = dyv.astype(BF16)

    def feed(j, carry):
        cols = pl.ds(pl.multiple_of(j * 256, 256), 256)
        dg = dot_nt(dyb, wr[cols, :])
        df = gps[:, cols].astype(F32).reshape(caps, length, 256) * dg[:, None, :]
        dc[...] += dot_nt(df.reshape(n, 256).astype(BF16), we[:, cols])
        return carry

    lax.fori_loop(0, half, feed, 0, unroll=3)
    for c in parts[1]:
        c.wait()
    lax.fori_loop(half, 2 * half, feed, 0, unroll=3)
    load_m.wait()
    piece = 8 * length

    def norm(i, sums):
        rows = pl.ds(pl.multiple_of(i * piece, piece), piece)
        xhat, rstd = norm_stats(mv[rows, :])
        dcv = dc[rows, :]
        back = norm_back(dcv * row(gains, 1), xhat, rstd)
        dy_rows = dy[pl.ds(pl.multiple_of(i * 8, 8), 8), :]
        out = (back.reshape(piece // length, length, width) + dy_rows[:, None, :]).reshape(
            piece, width
        )
        dm[rows, :] = out
        low = out.astype(BF16)
        dmb[rows, :] = low

        def fold(x):
            return jnp.sum(x.reshape(piece // 8, 8, width), axis=0)

        return sums[0] + fold(dcv * xhat), sums[1] + fold(dcv), sums[2] + fold(low.astype(F32))

    blank = jnp.zeros((8, width), F32)
    sums = lax.fori_loop(0, n // piece, norm, (blank, blank, blank))
    store_dm = load(dm, dm_any, sems.at[7])
    load_p.wait()
    dov[...] = dot_nt(dmb[...], wp[...]).astype(BF16)
    load_qkv.wait()
    masks = head_masks()
    same = (
        lax.broadcasted_iota(jnp.int32, (LANES, LANES), 0) // length
        == lax.broadcasted_iota(jnp.int32, (LANES, LANES), 1) // length
    )
    bias = jnp.where(same, 0.0, -1e30)

    def attention(g, carry):
        rows = pl.ds(pl.multiple_of(g * LANES, LANES), LANES)
        for p in range(width // LANES):
            lanes = slice(p * LANES, (p + 1) * LANES)
            k_lanes = slice(width + p * LANES, width + (p + 1) * LANES)
            v_lanes = slice(2 * width + p * LANES, 2 * width + (p + 1) * LANES)
            q2 = qkv[rows, lanes] * BF16(0.125)
            km = two_heads(qkv[rows, k_lanes], masks)
            vm = two_heads(qkv[rows, v_lanes], masks)
            do2 = dov[rows, lanes]
            parts = softmax_parts(dot_nt(q2, km), bias)
            dp = dot_nt(do2, vm)
            pb, ds = [], []
            for e in range(2):
                prob = parts[e] * (1.0 / jnp.sum(parts[e], axis=-1, keepdims=True))
                dpe = dp[:, e * LANES : (e + 1) * LANES]
                inner = jnp.sum(prob * dpe, axis=-1, keepdims=True)
                pb.append(prob.astype(BF16))
                ds.append((prob * (dpe - inner)).astype(BF16))
            dqkv[rows, lanes] = (dot(jnp.concatenate(ds, axis=1), km) * 0.125).astype(BF16)
            dqkv[rows, k_lanes] = dot_tn(jnp.concatenate(ds, axis=0), two_heads(q2, masks)).astype(
                BF16
            )
            dqkv[rows, v_lanes] = dot_tn(
                jnp.concatenate(pb, axis=0), two_heads(do2, masks)
            ).astype(BF16)
        return carry

    lax.fori_loop(0, n // LANES, attention, 0)
    store = load(dqkv, dqkv_any, sems.at[8])
    for i in range(3):
        vec_out[i : i + 1, :] = jnp.sum(sums[i], axis=0, keepdims=True)
    vec_out[3:4, :] = jnp.sum(dqkv[:, :width].astype(F32), axis=0, keepdims=True)
    vec_out[4:5, :] = jnp.sum(dqkv[:, 2 * width :].astype(F32), axis=0, keepdims=True)
    vec_out[5:8, :] = jnp.zeros((3, width), F32)
    store_dm.wait()
    store.wait()


def weight_grad_kernel(with_hid, scal, dm_any, dqkv_any, at_any, ot_any, wq_any, gains, biases, vec,
                       hid, *rest):
    turn, rest = (rest[:4], rest[4:]) if with_hid else ((), rest)
    keep_a, keep_b, send_a, send_b = rest[:4]
    turned, rest = (rest[4:8], rest[8:]) if with_hid else ((), rest[4:])
    dm, at, ot, dmb, dqkv, wq, grads, tails, inner_v, small, sems, store_sems = rest[:12]
    held, turn_sems = rest[12:16], rest[16:]
    n, width = dm.shape
    t = scal[0]
    load_dm = load(dm_any, dm, sems.at[0])
    load_o = load(ot_any, ot, sems.at[1])
    load_qkv = load(dqkv_any, dqkv, sems.at[2])
    load_a = load(at_any, at, sems.at[3])
    blocks, block = at.shape[:2]
    loads_t = [load(src, dst, turn_sems[0].at[i]) for i, (src, dst) in enumerate(zip(turn, held))]
    load_dm.wait()
    dmb[...] = dm[...].astype(BF16)
    load_o.wait()
    loads_w = [
        load(wq_any.at[pl.ds(e * block, block)], wq.at[scal[4 + e]], sems.at[8 + e])
        for e in range(blocks)
    ]
    half, quarter = width // 2, width // 4

    def project(hh, carry):
        cols = pl.ds(pl.multiple_of(hh * half, LANES), half)
        grads[hh, 0] = dot(ot[...].reshape(width, n), dmb[:, cols]).astype(BF16)
        return carry

    lax.fori_loop(0, 2, project, 0)
    for c in loads_t:
        c.wait()
    for side in range(len(turned) // 2):
        total = held[2 * side][...].astype(F32) + held[2 * side + 1][...].astype(F32)
        turned[side][...] = total[:quarter]
        turned[2 + side][...] = total[quarter:].astype(BF16)
    load_qkv.wait()
    load_a.wait()
    for c in loads_w:
        c.wait()
    inner_v[...] = jnp.zeros_like(inner_v)

    def attend_in(c, carry):
        cols = pl.ds(pl.multiple_of(c * half, LANES), half)
        value = dot(at[...].reshape(width, n), dqkv[:, cols])
        grads[c // 3, 1 + c % 3] = value.astype(BF16)
        prod = value * wq[:, :, cols].reshape(width, half).astype(F32)
        acc = inner_v[...]
        for k in range(half // LANES):
            acc = acc + prod[:, k * LANES : (k + 1) * LANES]
        inner_v[...] = acc
        return carry

    lax.fori_loop(0, 6, attend_in, 0)

    def move(src, out, side, lanes, slot):
        return [
            load(
                src.at[pl.ds(q * quarter, quarter)],
                out.at[i, pl.ds(j * quarter, quarter), pl.ds(lanes, src.shape[1])],
                store_sems.at[slot + 2 * i + j],
            )
            for i in range(2)
            for j, q in enumerate(QUARTERS[side + 2 * i])
        ]

    stores = []
    for k, (hh, out_a, out_b) in enumerate(((1 - t, send_a, send_b), (t, keep_a, keep_b))):
        for part in range(4):
            out = (out_a, out_b)[part // 2]
            stores += move(grads.at[hh, part], out, part // 2, (part % 2) * half, 20 * k + 4 * part)
    inner = inner_v[...]
    inner = jnp.sum(inner, axis=1, keepdims=True)
    sums = jnp.sum(dqkv[...].astype(F32), axis=0, keepdims=True)
    hi = sums.astype(BF16)
    lo = (sums - hi.astype(F32)).astype(BF16)
    both = jnp.concatenate([hi, lo, jnp.zeros((14, 3 * width), BF16)], axis=0)
    shift1 = dot_nt(wq[...].reshape(width, 3 * width), both)
    shift1 = shift1[:, 0:1] + shift1[:, 1:2]
    first = (jnp.zeros((1, 1), jnp.int32) + t) == 0
    zero = jnp.zeros((1, width), F32)
    for_zero = jnp.concatenate([zero, zero, vec[1:2, :], vec[3:4, :], zero, zero], axis=0)
    for_one = jnp.concatenate([vec[0:1, :], vec[4:5, :], vec[2:3, :], zero, zero, zero], axis=0)
    ends = jnp.concatenate([1.0 / row(gains, 0), row(biases, 0)], axis=0)
    lines = jnp.concatenate([for_zero, ends, for_one, ends], axis=0).T
    lane = lax.broadcasted_iota(jnp.int32, (1, 8), 1)
    if with_hid:
        columns = jnp.broadcast_to(hid[...], (8, hid.shape[1])).T
    for e in range(blocks):
        at_block = slice(e * block, (e + 1) * block)
        if with_hid:
            pick = columns[2 * e * block : (2 * e + 1) * block] * (lane == 4).astype(F32)
            pick = pick + columns[(2 * e + 1) * block : (2 * e + 2) * block] * (lane == 5).astype(F32)
        else:
            pick = jnp.zeros((block, 8), F32)
        small[scal[4 + e]] = jnp.concatenate(
            [lines[at_block, :8], lines[at_block, 8:], pick,
             jnp.zeros((block, LANES - 24), F32)], axis=1
        )
    sv = small[...].reshape(width, LANES)
    zeros_set, ones_set, own = sv[:, :8], sv[:, 8:16], sv[:, 16:24]
    gain1 = zeros_set[:, 6:7] * (inner - zeros_set[:, 7:8] * shift1)
    zeros_set = zeros_set + gain1 * (lane == 0).astype(F32) + shift1 * (lane == 1).astype(F32)
    used = (lane < 4).astype(F32)
    zeros_set, ones_set = zeros_set * used, ones_set * used
    keep_set = jnp.where(first, zeros_set, ones_set) + own
    send_set = jnp.where(first, ones_set, zeros_set)
    for hh in range(2):
        value = jnp.where((jnp.zeros((1, 1), jnp.int32) + t) == hh, keep_set, send_set)
        hi = value.astype(BF16).astype(F32)
        fill = jnp.zeros((width, LANES // 2 - 8), F32)
        tails[hh] = jnp.concatenate([hi, fill, value - hi, fill], axis=1).astype(BF16)
    stores += move(tails.at[1 - t], send_b, 1, width, 16)
    stores += move(tails.at[t], keep_b, 1, width, 36)
    for c in stores:
        c.wait()


def input_back_kernel(
    scal, dm_any, h_any, gains, dqkv_any, wq_any, order_any,
    tok_keep, tok_send,
    h_v, wq, dm, dqkv, da, sems,
):
    n, width = dm.shape
    caps, half_len, _ = tok_keep.shape
    t = scal[0]
    loads = [
        load(src, dst, sems.at[i])
        for i, (src, dst) in enumerate(
            ((dqkv_any, dqkv), (wq_any, wq),
             (h_any.at[pl.ds(pl.multiple_of(t * n, n), n)], h_v), (dm_any, dm))
        )
    ]
    loads[0].wait()
    loads[1].wait()

    def back(j, carry):
        rows = pl.ds(pl.multiple_of(j * 256, 256), 256)
        da[:, rows] = dot_nt(dqkv[...], wq[rows, :])
        return carry

    lax.fori_loop(0, width // 256, back, 0, unroll=3)
    loads[2].wait()
    loads[3].wait()
    piece = 8 * 2 * half_len
    first = (jnp.zeros((1, 1, 1), jnp.int32) + t) == 0

    def norm(i, carry):
        rows = pl.ds(pl.multiple_of(i * piece, piece), piece)
        xhat, rstd = norm_stats(h_v[rows, :].astype(F32))
        grad = dm[rows, :] + norm_back(da[rows, :] * row(gains, 0), xhat, rstd)
        halves = grad.reshape(8, 2, half_len, width)
        at = pl.ds(pl.multiple_of(i * 8, 8), 8)
        tok_keep[at] = jnp.where(first, halves[:, 0], halves[:, 1])
        tok_send[at] = jnp.where(first, halves[:, 1], halves[:, 0]).astype(BF16)
        return carry

    lax.fori_loop(0, n // piece, norm, 0)


def reduce_grad_kernel(
    rows_block, length, expo, g_any, images_any, texts_any, gall_any, extra_any, order_any,
    red_out, bias_out,
    g_v, images, texts, gall, extra, acc, sems,
):
    total, width = images.shape
    blocks = total // rows_block
    share = red_out.shape[0]
    whole = load(images_any, images, sems.at[0])
    scale = jnp.exp(jnp.full((1, 1), expo[0], F32))
    acc[...] = jnp.zeros_like(acc)
    whole.wait()

    def block(b, rb):
        rows = pl.ds(pl.multiple_of(b * rows_block, 16), rows_block)
        waits = [
            load(src.at[rows], dst, sems.at[1 + i])
            for i, (src, dst) in enumerate(
                ((g_any, g_v), (texts_any, texts), (gall_any, gall), (extra_any, extra))
            )
        ]
        for c in waits:
            c.wait()
        def project(i, rb):
            at = pl.ds(pl.multiple_of(i * 96, 96), 96)
            dt = scale * dot(g_v[at, :], images[...])
            tx = texts[at, :].astype(F32)
            part = (dt - tx * jnp.sum(tx * dt, axis=1, keepdims=True)) * (1.0 / length)
            part = part.astype(BF16)
            texts[at, :] = part
            inv = jnp.sum(extra[at, EXTRA : EXTRA + 3], axis=1, keepdims=True)
            return rb + jnp.sum(part.astype(F32) * inv, axis=0, keepdims=True)

        rb = lax.fori_loop(0, rows_block // 96, project, rb)
        acc[...] += dot_tn(gall[...], texts[...])
        return rb

    rb = lax.fori_loop(0, blocks, block, jnp.zeros((1, width), F32))
    red_out[...] = acc[:share, :]
    bias_out[...] = jnp.broadcast_to(rb * float(length), bias_out.shape)


def to_wire(x, width):
    low = x.astype(BF16)
    if x.shape[1] == width:
        return low
    rest = x[:, width:] - low[:, width:].astype(F32)
    return jnp.concatenate([low, rest.astype(BF16)], axis=1)


def from_wire(x, width):
    y = x.astype(F32)
    if x.shape[1] == width:
        return y
    return jnp.concatenate([y[:, :width], y[:, width : width + 64] + y[:, width + 64 :]], axis=1)


def wire_kernel(width, qa, qa_back, qb, qb_back, far_a, far_b, wire_a, wire_b, a0, a1, b0, b1,
                sems):
    loads = [
        load(src.at[0], dst, sems.at[i])
        for i, (src, dst) in enumerate(((qa, a0), (qa_back, a1), (qb, b0), (qb_back, b1)))
    ]
    loads[0].wait()
    loads[1].wait()
    wire_a[...] = (a0[...].astype(F32) + a1[...].astype(F32)).astype(BF16)
    loads[2].wait()
    loads[3].wait()
    wire_b[...] = to_wire(from_wire(b0[...], width) + from_wire(b1[...], width), width)


def turn_kernel(width, stacked, count, *refs):
    ins, (kept_a, kept_b, next_a, next_b) = refs[: 2 * count], refs[2 * count : 2 * count + 4]
    scratch, sems = refs[2 * count + 4 : -1], refs[-1]
    loads = [
        load(src.at[1] if i % count < stacked else src, dst, sems.at[i])
        for i, (src, dst) in enumerate(zip(ins, scratch))
    ]
    half = kept_a.shape[0]
    for side, (kept, moved) in enumerate(((kept_a, next_a), (kept_b, next_b))):
        at = range(side * count, (side + 1) * count)
        for i in at:
            loads[i].wait()
        total = from_wire(scratch[at[0]][...], width)
        for i in at[1:]:
            total = total + from_wire(scratch[i][...], width)
        kept[...] = total[:half]
        moved[...] = to_wire(total[half:], width)


def merge_kernel(width, sum_a, sum_b, hop_a, hop_b, *rest):
    outs = rest[-4:]
    for i, out in enumerate(outs):
        rows = out.shape[0]
        at = slice(i * rows, (i + 1) * rows)
        a = sum_a[at, :] + hop_a[at, :].astype(F32)
        b = sum_b[at, :] + from_wire(hop_b[at, :], width)
        if i == 0:
            out[:, :width] = a
            out[:, width:] = b
        else:
            out[:, :width] = a.astype(BF16)
            out[:, width:] = to_wire(b, width)


def finish_kernel(width, scal, total, hop_1, hop_2, hop_3, rbias,
                  qkv_out, project_out, gains_out, biases_out, hid_out):
    half = width // 2
    rows, cols = project_out.shape[0], width
    t, d = scal[0], scal[1]
    acc = total[...]
    for hop in (hop_1, hop_2, hop_3):
        x = hop[...]
        acc = acc + jnp.concatenate(
            [x[:, :width].astype(F32), from_wire(x[:, width:], width)], axis=1
        )
    project_out[...] = acc[:, :half]
    qkv_out[...] = acc[:, half : 2 * width]
    small = acc[:, 2 * width : 2 * width + 8].T
    lane = lax.broadcasted_iota(jnp.int32, (rows, cols), 1)
    mine = lax.broadcasted_iota(jnp.int32, (rows, cols), 0) + d * rows
    last = jnp.sum(jnp.where(lane == mine, rbias[0:1, :], 0.0), axis=1, keepdims=True)
    last = jnp.broadcast_to(last, (rows, 8)).T
    first = (jnp.zeros((1, 1), jnp.int32) + t) == 0
    gains_out[...] = small[0:1]
    biases_out[...] = jnp.concatenate(
        [small[1:3], jnp.where(first, small[3:4], last[0:1])], axis=0
    )
    hid_out[...] = jnp.concatenate([small[4:5], small[5:6]], axis=1)


def xor_permute(x, axis, bit):
    return lax.ppermute(x, axis, [(i, i ^ bit) for i in range(lax.axis_size(axis))])


def bit_groups(count):
    bits = [1 << i for i in range(count.bit_length() - 1)]
    groups = [tuple(bits[i : i + 2]) for i in range(0, len(bits), 2)]
    return groups[::-1]


def reaches(group):
    out = [0]
    for bit in group:
        out = out + [r ^ bit for r in out]
    return out


def slot_reaches(count):
    order = [0]
    for group in bit_groups(count):
        order = [r ^ o for r in reaches(group) for o in order]
    return order


def hop(sends, group):
    return [x if r == 0 else xor_permute(x, "dp", r) for x, r in zip(sends, reaches(group))]


def scatter_sum(s, groups, to_wire=lambda x: x, from_wire=lambda x: x):
    for group in reversed(groups):
        hops = reaches(group)
        rows = s.shape[0] // len(hops)
        parts = [s[i * rows : (i + 1) * rows] for i in range(len(hops))]
        moved = [xor_permute(to_wire(parts[i]), "dp", r) for i, r in enumerate(hops) if r]
        s = parts[0]
        for piece in moved:
            s = s + from_wire(piece)
    return s


def flip_by(x, index, count):
    for i in range(count.bit_length() - 1):
        bit = 1 << i
        shape = x.shape
        pairs = x.reshape((count // (2 * bit), 2, bit) + shape[1:])
        x = jnp.where((index & bit) != 0, pairs[:, ::-1], pairs).reshape(shape)
    return x


SMEM = pl.BlockSpec(memory_space=pltpu.SMEM)
VMEM = pl.BlockSpec(memory_space=pltpu.VMEM)
ANY = pl.BlockSpec(memory_space=pl.ANY)


def call(kernel, name, in_specs, outs, out_specs, scratch, args, flops, moved):
    return pl.pallas_call(
        kernel,
        name=name,
        in_specs=in_specs,
        out_shape=[jax.ShapeDtypeStruct(s, d) for s, d in outs],
        out_specs=out_specs,
        scratch_shapes=scratch,
        compiler_params=pltpu.CompilerParams(vmem_limit_bytes=VMEM_LIMIT),
        cost_estimate=pl.CostEstimate(flops=flops, bytes_accessed=moved, transcendentals=0),
    )(*args)


def body(
    pictures, captions, tallies, exponent,
    p_gains, p_biases, p_hid, p_wq, p_wp, p_we, p_wr,
    c_gains, c_biases, c_hid, c_wq, c_wp, c_we, c_wr,
):
    t = lax.axis_index("tower")
    d = lax.axis_index("dp")
    chips = lax.axis_size("dp")
    pairs, length, width = captions.shape
    img_len = pictures.shape[1]
    hidden = c_hid.shape[0]
    caps = pairs // 2
    n = caps * length
    total = pairs * chips
    row_blocks = 16
    order = np.array(slot_reaches(chips))
    slot_of = np.zeros(chips, np.int32)
    slot_of[order] = np.arange(chips)
    table = np.stack([slot_of[np.arange(chips) ^ i] for i in range(chips)]).astype(np.int32)
    slots = lax.dynamic_slice_in_dim(jnp.asarray(table), d, 1, 0)[0]
    relative = chips == row_blocks
    row_slots = slots if relative else jnp.arange(row_blocks, dtype=jnp.int32)
    head = jnp.stack([t, d, tallies[0], t]).astype(jnp.int32)
    scal = jnp.concatenate([head, row_slots, slots])

    texts_in = captions.reshape(pairs * length, width)
    c_hid2, p_hid2 = c_hid.reshape(1, hidden), p_hid.reshape(1, hidden)
    blk = (row_blocks, width // row_blocks, n)
    vm = pltpu.VMEM
    sem = pltpu.SemaphoreType.DMA
    half_hid = (n, hidden // 2)
    chunk = width + 2 * LANES
    a_t, qkv, o_t, m, c_t, gp_keep, gp_send, text_send, emb, r = call(
        text_forward_kernel, "text_forward",
        [SMEM, ANY, VMEM, VMEM, VMEM, ANY, ANY, ANY, ANY],
        [(blk, BF16), ((n, 3 * width), BF16), (blk, BF16), ((n, width), F32), (blk, BF16),
         (half_hid, BF16), (half_hid, BF16), ((chips, caps, chunk), BF16),
         ((caps, width), F32), ((caps, LANES), F32)],
        [ANY] * 7 + [VMEM] * 3,
        [vm((n, width), BF16), vm((width, 3 * width), BF16), vm((width, width), BF16),
         vm((width, hidden), BF16), vm((hidden, width), BF16), vm((1, 3 * width), F32),
         vm((n, width), BF16), vm((n, width), BF16), vm((caps, hidden), F32), vm(blk, BF16), vm((n, 3 * width), BF16),
         vm(blk, BF16), vm((n, width), F32), vm(blk, BF16), vm(half_hid, BF16),
         vm(half_hid, BF16), sem((5,)), sem((7,))],
        (scal, texts_in, c_gains, c_biases, c_hid2, c_wq, c_wp, c_we, c_wr),
        int(2 * n * width * (4 * width + hidden)), 20_000_000,
    )
    c_far = xor_permute(c_t, "tower", 1)
    gp_far = xor_permute(gp_send, "tower", 1)
    text_all = lax.all_to_all(text_send, "dp", 0, 0, tiled=True)

    rows = caps * PAD
    groups = bit_groups(chips)
    (image,) = call(
        image_forward_kernel, "image_forward",
        [SMEM, ANY, VMEM, VMEM, VMEM, ANY, ANY, ANY, ANY],
        [((caps, width), BF16)],
        [VMEM],
        [vm((img_len, pairs, width), BF16), vm((width // LANES, img_len * caps, LANES), F32),
         vm((rows, width), F32), vm((rows, width), BF16),
         vm((rows + 16, 3 * width), BF16), vm((rows, width), F32), vm((caps, width), F32),
         vm((caps, hidden), F32), vm((width, 3 * width), BF16), vm((width, width), BF16),
         vm((width, hidden), BF16), vm((hidden, width), BF16), vm((1, 3 * width), F32),
         vm((1, width), F32), sem((5,))],
        (scal, jnp.transpose(pictures, (1, 0, 2)), p_gains, p_biases, p_hid2,
         p_wq, p_wp, p_we, p_wr),
        int(2 * rows * width * (4 * width + hidden)), 20_000_000,
    )
    image, text_all = lax.optimization_barrier((image, text_all))
    text_par = xor_permute(text_all, "tower", 1)
    got = hop([image[None]] * len(reaches(groups[0])), groups[0])
    for group in groups[1:]:
        whole = jnp.concatenate(got, axis=0)
        got = hop([whole] * len(reaches(group)), group)
    par_all = xor_permute(jnp.concatenate(got, axis=0), "tower", 1)
    small_slice = total <= 768
    if not small_slice:
        got = [jnp.concatenate(got, axis=0)]

    block = total if small_slice else 96
    held = chips if small_slice else 1
    share = hidden // (2 * chips)
    piece_shape = (width // 2, width)
    (loss, temp, ea, eb, ec, ed, g_all, images_all, texts_all, gall, extra, dc, dy, hid_grad) = call(
        partial(loss_kernel, block, len(got)), "loss",
        [SMEM] + [ANY] * len(got) + [ANY, ANY, ANY, SMEM, VMEM, VMEM] + [ANY] * 6,
        [((1, 1), F32), ((1, 1), F32)] + [(piece_shape, BF16)] * 4
        + [((total, total), BF16), ((total, width), BF16), ((total, width), BF16),
           ((total, LANES), BF16), ((total, LANES), F32), ((n, width), F32), ((caps, width), F32),
           ((1, hidden // 2), F32)],
        [VMEM, VMEM] + [ANY] * 10 + [VMEM, VMEM],
        [vm((held, caps, width), BF16), vm((held, caps, width), BF16),
         vm((held, caps, chunk), BF16), vm((held, caps, chunk), BF16),
         vm((total, width), BF16), vm((total, width), BF16), vm((total, LANES), F32),
         vm((total, LANES), BF16), vm((8, total), F32),
         vm((block, total), F32), vm((block, total), BF16), vm((2 * caps, total), BF16),
         vm(half_hid, BF16), vm(half_hid, BF16), vm((2,) + blk, BF16),
         vm((width, hidden // 2), BF16), vm((hidden // 2, width), BF16),
         vm((n, width), F32), vm((2, width, hidden // 4), BF16), sem((16,)), sem((14,))],
        (scal, *got, par_all, text_all, text_par, exponent, emb, r, gp_keep, gp_far,
         c_t, c_far, c_we, c_wr),
        int(3 * n * width * hidden), 20_000_000,
    )

    def widen(x):
        return x.astype(F32)

    def narrow(x):
        return x.astype(BF16)

    e_hops = [xor_permute(ea, "dp", 1), xor_permute(eb, "dp", 2)] if relative else []
    dm, dqkv, vec = call(
        middle_back_kernel, "middle_back",
        [SMEM, ANY, VMEM, ANY, ANY, VMEM] + [ANY] * 4,
        [((n, width), F32), ((n, 3 * width), BF16), ((8, width), F32)],
        [ANY, ANY, VMEM],
        [vm((n, width), F32), vm(half_hid, BF16), vm((n, width), F32),
         vm((width, hidden // 2), BF16), vm((hidden // 2, width), BF16), vm((width, width), BF16),
         vm((n, 3 * width), BF16), vm((n, width), F32), vm((n, width), BF16),
         vm((n, width), BF16), vm((n, 3 * width), BF16), sem((12,))],
        (scal, dc, dy, gp_send, m, c_gains, c_we, c_wr, c_wp, qkv),
        int(2 * n * width * (hidden + 4 * width)), 20_000_000,
    )
    b_shape = (width // 2, width + LANES)
    quarter_shape = (width // 4, width)
    qa_keep, qb_keep, qa_send, qb_send, *turned = call(
        partial(weight_grad_kernel, relative), "weight_grad",
        [SMEM] + [ANY] * 5 + [VMEM] * 4 + [ANY] * (4 if relative else 0),
        [((2,) + piece_shape, BF16), ((2,) + b_shape, BF16)] * 2
        + ([(quarter_shape, F32)] * 2 + [(quarter_shape, BF16)] * 2 if relative else []),
        [ANY] * 4 + [VMEM] * (4 if relative else 0),
        [vm((n, width), F32), vm(blk, BF16), vm(blk, BF16), vm((n, width), BF16),
         vm((n, 3 * width), BF16), vm((row_blocks, width // row_blocks, 3 * width), BF16),
         vm((2, 4, width, width // 2), BF16), vm((2, width, LANES), BF16), vm((width, LANES), F32),
         vm((row_blocks, width // row_blocks, LANES), F32), sem((8 + row_blocks,)), sem((40,))]
        + ([vm(piece_shape, BF16)] * 4 + [sem((4,))] if relative else []),
        (scal, dm, dqkv, a_t, o_t, c_wq, c_gains, c_biases, vec, hid_grad)
        + ((ec, e_hops[0], ed, e_hops[1]) if relative else ()),
        int(2 * n * width * 4 * width), 20_000_000,
    )
    qa_back = xor_permute(qa_send, "tower", 1)
    qb_back = xor_permute(qb_send, "tower", 1)
    cols = width // chips
    if relative:
        e_parts = (
            turned[0], turned[1], xor_permute(turned[2], "dp", 2), xor_permute(turned[3], "dp", 1)
        )
        wire_a, wire_b = call(
            partial(wire_kernel, width), "wire", [ANY] * 6,
            [(piece_shape, BF16), (b_shape, BF16)], [VMEM] * 2,
            [vm(piece_shape, BF16)] * 2 + [vm(b_shape, BF16)] * 2 + [sem((4,))],
            (qa_keep, qa_back, qb_keep, qb_back, *e_parts[2:]), 1_000_000, 4_000_000,
        )
        q_hops = [xor_permute(wire_a, "dp", 1), xor_permute(wire_b, "dp", 2)]
    else:
        q_sums = [
            from_wire(x[i], width) + from_wire(y[i], width)
            for i in range(2)
            for x, y in ((qa_keep, qa_back), (qb_keep, qb_back))
        ]
        tails = jnp.transpose(hid_grad.reshape(chips, 2, cols), (0, 2, 1)).reshape(width, 2)
        tails = jnp.pad(tails, ((0, 0), (width + 4, 64 - 6)))
        quarter = width // 4
        for i in (1, 3):
            q_sums[i] = q_sums[i] + jnp.concatenate(
                [tails[q * quarter : (q + 1) * quarter] for q in QUARTERS[i]], axis=0
            )
        wire_b = qb_back
        q_hops = []
    tok_keep, tok_send = call(
        input_back_kernel, "input_back",
        [SMEM, ANY, ANY, VMEM, ANY, ANY, ANY],
        [((caps, length // 2, width), F32), ((caps, length // 2, width), BF16)],
        [VMEM] * 2,
        [vm((n, width), BF16), vm((width, 3 * width), BF16), vm((n, width), F32),
         vm((n, 3 * width), BF16), vm((n, width), F32), sem((4,))],
        (scal, dm, texts_in, c_gains, dqkv, c_wq, wire_b),
        int(2 * n * width * 3 * width), 9_000_000,
    )
    reduce_grad, rbias = call(
        partial(reduce_grad_kernel, block, length), "reduce_grad",
        [SMEM] + [ANY] * 6,
        [((share, width), F32), ((8, width), F32)],
        [VMEM, VMEM],
        [vm((block, total), BF16), vm((total, width), BF16), vm((block, width), BF16),
         vm((block, LANES), BF16), vm((block, LANES), F32), vm((LANES, width), F32), sem((5,))],
        (exponent, g_all, images_all, texts_all, gall, extra, q_hops[0] if relative else wire_b),
        int(2 * total * total * width), 6_000_000,
    )

    tok_back = widen(xor_permute(tok_send, "tower", 1))
    grad_tokens = jnp.concatenate(
        [jnp.where(t == 0, tok_keep, tok_back), jnp.where(t == 0, tok_back, tok_keep)], axis=0
    )
    half, third = width // 2, width // 4

    def plain(sums):
        sides = []
        for side in range(2):
            at = {}
            for i in (side, side + 2):
                for j, q in enumerate(QUARTERS[i]):
                    at[q] = sums[i][j * third : (j + 1) * third]
            x = jnp.concatenate([at[q] for q in range(4)], axis=0)
            x = flip_by(x.reshape((chips, cols) + x.shape[1:]), d, chips)
            x = x[order].reshape((width,) + x.shape[2:])
            sides.append(
                scatter_sum(x, groups, lambda v: to_wire(v, width), lambda v: from_wire(v, width))
            )
        return sides

    if not relative:
        expand_grad = jnp.concatenate(plain([widen(x) for x in (ea, eb, ec, ed)]), axis=1)
        side_a, side_b = plain(q_sums)
        small = side_b[:, width : width + 8].T
        last = jnp.where(
            t == 0, small[3], lax.dynamic_slice_in_dim(rbias[0], d * cols, cols, 0)
        )
        return (
            loss.reshape(1), temp.reshape(1), grad_tokens, small[0:1], jnp.stack([small[1], small[2], last]),
            small[4:6].reshape(2 * cols),
            jnp.concatenate([side_a[:, half:], side_b[:, :width]], axis=1), side_a[:, :half],
            expand_grad, reduce_grad,
        )

    def second_hops(side_a, side_b, stacked, name):
        count = len(side_a)
        shapes = [x.shape[-2:] for x in (*side_a, *side_b)]
        small = shapes[-1][1] - width
        kept_a, kept_b, next_a, next_b = call(
            partial(turn_kernel, width, stacked, count), name, [ANY] * (2 * count),
            [((third, width), F32), ((third, width + small // 2), F32),
             ((third, width), BF16), ((third, width + small), BF16)],
            [VMEM] * 4, [vm(x, BF16) for x in shapes] + [sem((2 * count,))],
            (*side_a, *side_b), 1_000_000, 4_000_000,
        )
        return kept_a, kept_b, xor_permute(next_a, "dp", 2), xor_permute(next_b, "dp", 1)

    def merge(parts, after, name):
        f32_cols = parts[0].shape[1] + parts[1].shape[1]
        bf_cols = parts[2].shape[1] + parts[3].shape[1]
        return call(
            partial(merge_kernel, width), name, [VMEM] * 4 + [ANY] * len(after),
            [((cols, f32_cols), F32)] + [((cols, bf_cols), BF16)] * 3, [VMEM] * 4, [],
            (*parts, *after), 1_000_000, 3_000_000,
        )

    def z_hops(pieces):
        return [xor_permute(x, "dp", r) for x, r in zip(pieces, reaches(groups[0])[1:])]

    e_own, *e_far = merge(e_parts, (wire_b,), "merge_expand")
    e_back = z_hops(e_far)
    expand_grad = e_own + sum(widen(x) for x in e_back)
    q_parts = second_hops(
        (qa_keep, qa_back, q_hops[0]), (qb_keep, qb_back, q_hops[1]), 2, "turn_qkv"
    )
    q_own, *q_far = merge(q_parts, e_back, "merge_qkv")
    q_in = z_hops(q_far)
    qkv_grad, project_grad, gains_grad, biases_grad, hid_rows = call(
        partial(finish_kernel, width), "finish", [SMEM] + [VMEM] * 5,
        [((cols, 3 * half), F32), ((cols, half), F32), ((1, cols), F32), ((3, cols), F32),
         ((1, 2 * cols), F32)],
        [VMEM] * 5, [], (scal, q_own, *q_in, rbias), 1_000_000, 2_000_000,
    )
    return (
        loss.reshape(1), temp.reshape(1), grad_tokens, gains_grad, biases_grad, hid_rows.reshape(2 * cols),
        qkv_grad, project_grad, expand_grad, reduce_grad,
    )


def solution(mesh):
    in_specs = (P("dp", None, None), P("dp", None, None), P("dp")) + (P(),) * 15
    out_specs = (
        P(), P(), P("dp", "tower", None), P("tower", "dp"), P("tower", "dp"),
        P(("tower", "dp")), P("dp", "tower"), P("dp", "tower"), P("dp", "tower"),
        P(("tower", "dp"), None),
    )
    return jax.shard_map(body, mesh=mesh, in_specs=in_specs, out_specs=out_specs, check_vma=False)
```

profile of v0, /device:TPU:0, one launch (start us, length us, event | category | flops | bytes accessed | tf_op | source)
XLA Modules:
  0.0 204.7 jit_solution(1601345832570426634)
XLA Ops:
  3.9 15.0 %text_forward.1 = (bf16[16,48,384]{2,1,0:T(8,128)(2,1)}, bf16[384,2304]{1,0:T(8,128)(2,1)}, bf16[16,48,384]{2,1,0:T(8,128)(2,1)}, f32[384,768]{1,0:T(8,128)}, bf...) custom-call(s32[36]{0:T(128)} %concatenate.13.scal, ...), custom_call_target="tpu_custom_call" | custom-call | flops 3623878656 | bytes 20000000 | tf_op jit(solution)/shard_map/text_forward/pallas_call | solution.py:1046
  18.9 8.5 %all-to-all-start = ((bf16[16,24,1024]{2,1,0:T(8,128)(2,1)}), bf16[16,24,1024]{2,1,0:T(8,128)(2,1)S(1)}, u32[]{:S(2)}, u32[]{:S(2)}) async-start(bf16[16,24,1024]{2,1,0:T(8,128)(2,1)} %get-tuple-element.70), calls=%async_computation | async-start | bytes 1572864 | tf_op jit(solution)/shard_map/all_to_all | solution.py:1107
  28.5 30.5 %image_forward.1 = bf16[24,768]{1,0:T(8,128)(2,1)} custom-call(s32[36]{0:T(128)} %concatenate.13.scal, bf16[50,48,768]{2,1,0:T(8,128)(2,1)} %bitcast.17, bf16[2,768]{1,0:T(2,128)(2,1)} %gains.5, bf16[6,768]{1,0:T(8,128)(2,1)} %biases.3, bf16[1,3072]{1,0:T(2,128)(2,1)} %reshape.38.hid, bf16[768,2304]{1,0:T(8,128)(2,1)} %wq_any.4, bf16[768,768]{1,0:T(8,128)(2,1)} %wp_any.3, ...), custom_call_target="tpu_custom_call" | custom-call | flops 12683575296 | bytes 20000000 | tf_op jit(solution)/shard_map/image_forward/pallas_call | solution.py:1046
  59.1 3.8 %collective-permute-start.2 = (bf16[1,24,768]{2,1,0:T(8,128)(2,1)}, bf16[1,24,768]{2,1,0:T(8,128)(2,1)S(1)}, u32[]{:S(2)}, u32[]{:S(2)}) collective-permute-start(bf16[1,24,768]{2,1,0:T(8,128)(2,1)} %bitcast.13), channel_id=1, source_target_pairs={{0,12},{1,13},{2,14},{3,15},{4,8},{5,9},{6,10},{7,11},{8,4},{9,5},... | collective-permute-start | bytes 110600 | tf_op jit(solution)/shard_map/ppermute | solution.py:992
  65.2 2.8 %collective-permute-done.1 = bf16[1,24,768]{2,1,0:T(8,128)(2,1)S(1)} collective-permute-done((bf16[1,24,768]{2,1,0:T(8,128)(2,1)}, bf16[1,24,768]{2,1,0:T(8,128)(2,1)S(1)}, u32[]{:S(2)}, u32[]{:S(2)}) %collective-permute-start.1) | collective-permute-done | bytes 36896 | tf_op jit(solution)/shard_map/ppermute | solution.py:992
  68.7 1.5 collective-permute-start.4
  70.3 1.5 collective-permute-start.3
  71.8 3.7 %collective-permute-done.3.refs_1_ = bf16[4,24,768]{2,1,0:T(8,128)(2,1)S(1)} collective-permute-done((bf16[4,24,768]{2,1,0:T(8,128)(2,1)S(1)}, bf16[4,24,768]{2,1,0:T(8,128)(2,1)S(1)}, u32[]{:S(2)}, u32[]{:S(2)}) %collective-permute-start.3) | collective-permute-done | bytes 147488 | tf_op jit(solution)/shard_map/ppermute | solution.py:992
  75.4 1.4 collective-permute-start.5
  76.9 4.5 %collective-permute-done.5.refs_3_ = bf16[4,24,768]{2,1,0:T(8,128)(2,1)S(1)} collective-permute-done((bf16[4,24,768]{2,1,0:T(8,128)(2,1)S(1)}, bf16[4,24,768]{2,1,0:T(8,128)(2,1)S(1)}, u32[]{:S(2)}, u32[]{:S(2)}) %collective-permute-start.5) | collective-permute-done | bytes 147488 | tf_op jit(solution)/shard_map/ppermute | solution.py:992
  82.2 1.3 collective-permute-done.6.refs_4_
  84.7 16.9 %loss.1 = (f32[1,1]{1,0:T(1,128)}, f32[1,1]{1,0:T(1,128)}, bf16[384,768]{1,0:T(8,128)(2,1)}, bf16[384,768]{1,0:T(8,128)(2,1)}, bf16[384,768]{1,0:T(8,128)(2,1)},...) custom-call(s32[36]{0:T(128)} %concatenate.13.scal, ...), custom_call_target="tpu_custom_call" | custom-call | flops 2717908992 | bytes 20000000 | tf_op jit(solution)/shard_map/loss/pallas_call | solution.py:1046
  101.6 1.5 collective-permute-start.10
  103.7 18.9 %middle_back.1 = (f32[384,768]{1,0:T(8,128)}, bf16[384,2304]{1,0:T(8,128)(2,1)}, f32[8,768]{1,0:T(8,128)}) custom-call(s32[36]{0:T(128)} %concatenate.13.scal, f32[384,768]{1,0:T(8,128)} %get-tuple-element.80.dc_any, f32[24,768]{1,0:T(8,128)} %get-tuple-element.81.dy, bf16[384,1536]{1,0:T(8,128)(2,1)} %get-tuple-element.76.gps_any, ...), custom_call_target="tpu_custom_call" | custom-call | flops 3623878656 | bytes 20000000 | tf_op jit(solution)/shard_map/middle_back/pallas_call | solution.py:1046
  123.6 13.8 %weight_grad.1 = (bf16[2,384,768]{2,1,0:T(8,128)(2,1)}, bf16[2,384,896]{2,1,0:T(8,128)(2,1)}, bf16[2,384,768]{2,1,0:T(8,128)(2,1)}, bf16[2,384,896]{2,1,0:T(8,12...) custom-call(s32[36]{0:T(128)} %concatenate.13.scal, ...), custom_call_target="tpu_custom_call" | custom-call | flops 1811939328 | bytes 20000000 | tf_op jit(solution)/shard_map/weight_grad/pallas_call | solution.py:1046
  138.0 1.5 collective-permute-start.14
  140.0 7.2 %collective-permute-done.14.far_a.hop_a = bf16[192,768]{1,0:T(8,128)(2,1)S(1)} collective-permute-done((bf16[192,768]{1,0:T(8,128)(2,1)}, bf16[192,768]{1,0:T(8,128)(2,1)S(1)}, u32[]{:S(2)}, u32[]{:S(2)}) %collective-permute-start.14) | collective-permute-done | bytes 294944 | tf_op jit(solution)/shard_map/ppermute | solution.py:992
  150.0 3.0 %wire.1 = (bf16[384,768]{1,0:T(8,128)(2,1)}, bf16[384,896]{1,0:T(8,128)(2,1)}) custom-call(bf16[2,384,768]{2,1,0:T(8,128)(2,1)} %get-tuple-element.94.qa.refs_0_, bf16[2,384,768]{2,1,0:T(8,128)(2,1)} %copy-done.1, bf16[2,384,896]{2,1,0:T(8,128)(2,1)} %get-tuple-element.96.qb.refs_3_, bf16[2,384,896]{2,1,0:T(8,128)(2,1)} %copy-done, ...), custom_call_target="tpu_custom_call" | custom-call | flops 1000000 | bytes 4000000 | tf_op jit(solution)/shard_map/wire/pallas_call | solution.py:1046
  154.2 2.3 %merge_expand.1 = (f32[48,1536]{1,0:T(8,128)}, bf16[48,1536]{1,0:T(8,128)(2,1)}, bf16[48,1536]{1,0:T(8,128)(2,1)}, bf16[48,1536]{1,0:T(8,128)(2,1)}) custom-call(f32[192,768]{1,0:T(8,128)} %get-tuple-element.108.sum_a, f32[192,768]{1,0:T(8,128)} %get-tuple-element.109.sum_b, bf16[192,768]{1,0:T(8,128)(2,1)} %copy-done.5, bf16[192,768]{1,0:T(8,128)(2,1)} %copy-done.6, ...), custom_call_target="tpu_custom_call" | custom-call | flops 1000000 | bytes 3000000 | tf_op jit(solution)/shard_map/merge_expand/pallas_call | solution.py:1046
  156.7 2.4 %collective-permute-start.22 = (bf16[48,1536]{1,0:T(8,128)(2,1)}, bf16[48,1536]{1,0:T(8,128)(2,1)S(1)}, u32[]{:S(2)}, u32[]{:S(2)}) collective-permute-start(bf16[48,1536]{1,0:T(8,128)(2,1)} %get-tuple-element.111), channel_id=1, source_target_pairs={{0,8},{1,9},{2,10},{3,11},{4,12},{5,13},{6,14},{7,15},{8,0},{9,1},... | collective-permute-start | bytes 442376 | tf_op jit(solution)/shard_map/ppermute | solution.py:992
  159.1 1.8 collective-permute-start.23
  160.9 7.0 %input_back.1 = (f32[24,8,768]{2,1,0:T(8,128)}, bf16[24,8,768]{2,1,0:T(8,128)(2,1)}) custom-call(s32[36]{0:T(128)} %concatenate.13.scal, f32[384,768]{1,0:T(8,128)} %get-tuple-element.84.dm_any, bf16[768,768]{1,0:T(8,128)(2,1)} %bitcast.12, bf16[2,768]{1,0:T(2,128)(2,1)} %gains.9, bf16[384,2304]{1,0:T(8,128)(2,1)} %get-tuple-element.85.dqkv_any, ...), custom_call_target="tpu_custom_call" | custom-call | flops 1358954496 | bytes 9000000 | tf_op jit(solution)/shard_map/input_back/pallas_call | solution.py:1046
  168.0 1.5 collective-permute-done.18.refs_5_
  170.4 3.5 %turn_qkv.1 = (f32[192,768]{1,0:T(8,128)}, f32[192,832]{1,0:T(8,128)}, bf16[192,768]{1,0:T(8,128)(2,1)}, bf16[192,896]{1,0:T(8,128)(2,1)}) custom-call(bf16[2,384,768]{2,1,0:T(8,128)(2,1)} %get-tuple-element.94.qa.refs_0_, bf16[2,384,768]{2,1,0:T(8,128)(2,1)} %copy-done.1, bf16[384,768]{1,0:T(8,128)(2,1)} %copy-done.3, ...), custom_call_target="tpu_custom_call" | custom-call | flops 1000000 | bytes 4000000 | tf_op jit(solution)/shard_map/turn_qkv/pallas_call | solution.py:1046
  174.7 1.4 collective-permute-start.20
  177.0 5.1 %collective-permute-done.19.hop_a = bf16[192,768]{1,0:T(8,128)(2,1)S(1)} collective-permute-done((bf16[192,768]{1,0:T(8,128)(2,1)}, bf16[192,768]{1,0:T(8,128)(2,1)S(1)}, u32[]{:S(2)}, u32[]{:S(2)}) %collective-permute-start.19) | collective-permute-done | bytes 294944 | tf_op jit(solution)/shard_map/ppermute | solution.py:992
  182.1 2.2 %collective-permute-done.20.hop_b = bf16[192,896]{1,0:T(8,128)(2,1)S(1)} collective-permute-done((bf16[192,896]{1,0:T(8,128)(2,1)}, bf16[192,896]{1,0:T(8,128)(2,1)S(1)}, u32[]{:S(2)}, u32[]{:S(2)}) %collective-permute-start.20) | collective-permute-done | bytes 344096 | tf_op jit(solution)/shard_map/ppermute | solution.py:992
  185.0 2.5 %merge_qkv.1 = (f32[48,1600]{1,0:T(8,128)}, bf16[48,1664]{1,0:T(8,128)(2,1)}, bf16[48,1664]{1,0:T(8,128)(2,1)}, bf16[48,1664]{1,0:T(8,128)(2,1)}) custom-call(f32[192,768]{1,0:T(8,128)} %get-tuple-element.104.sum_a, f32[192,832]{1,0:T(8,128)} %get-tuple-element.105.sum_b, bf16[192,768]{1,0:T(8,128)(2,1)} %copy-done.22, bf16[192,896]{1,0:T(8,128)(2,1)} %copy-done.21, ...), custom_call_target="tpu_custom_call" | custom-call | flops 1000000 | bytes 3000000 | tf_op jit(solution)/shard_map/merge_qkv/pallas_call | solution.py:1046
  187.5 2.6 %collective-permute-start.25 = (bf16[48,1664]{1,0:T(8,128)(2,1)}, bf16[48,1664]{1,0:T(8,128)(2,1)S(1)}, u32[]{:S(2)}, u32[]{:S(2)}) collective-permute-start(bf16[48,1664]{1,0:T(8,128)(2,1)} %get-tuple-element.115), channel_id=1, source_target_pairs={{0,8},{1,9},{2,10},{3,11},{4,12},{5,13},{6,14},{7,15},{8,0},{9,1},... | collective-permute-start | bytes 479240 | tf_op jit(solution)/shard_map/ppermute | solution.py:992
  190.1 1.8 collective-permute-start.26
  193.0 8.0 %reduce_grad.1 = (f32[96,768]{1,0:T(8,128)}, f32[8,768]{1,0:T(8,128)}) custom-call(f32[1]{0:T(128)S(6)} %copy.36.refs_7_.expo, bf16[768,768]{1,0:T(8,128)(2,1)} %get-tuple-element.117.g_any, bf16[768,768]{1,0:T(8,128)(2,1)} %get-tuple-element.118.images_any, bf16[768,768]{1,0:T(8,128)(2,1)} %get-tuple-element.119.texts_any, ...), custom_call_target="tpu_custom_call" | custom-call | flops 905969664 | bytes 6000000 | tf_op jit(solution)/shard_map/reduce_grad/pallas_call | solution.py:1046
  202.6 2.1 %finish.1 = (f32[48,1152]{1,0:T(8,128)}, f32[48,384]{1,0:T(8,128)}, f32[1,48]{1,0:T(1,128)}, f32[3,48]{1,0:T(4,128)}, f32[1,96]{1,0:T(1,128)}) custom-call(s32[36]{0:T(128)} %concatenate.13.scal, f32[48,1600]{1,0:T(8,128)} %get-tuple-element.113.total, bf16[48,1664]{1,0:T(8,128)(2,1)} %copy-done.24, bf16[48,1664]{1,0:T(8,128)(2,1)} %copy-done.25, ...), custom_call_target="tpu_custom_call" | custom-call | flops 1000000 | bytes 2000000 | tf_op jit(solution)/shard_map/finish/pallas_call | solution.py:1046
  (107 shorter events, 21.0 us)
Async XLA Ops:
  18.9 9.1 %copy-start.27 = (bf16[3072]{0:T(1024)(128)(2,1)S(1)}, bf16[3072]{0:T(1024)(128)(2,1)}, u32[]{:S(2)}) copy-start(bf16[3072]{0:T(1024)(128)(2,1)} %param.25) | copy-start | bytes 18436
  18.9 40.2 %all-to-all-start = ((bf16[16,24,1024]{2,1,0:T(8,128)(2,1)}), bf16[16,24,1024]{2,1,0:T(8,128)(2,1)S(1)}, u32[]{:S(2)}, u32[]{:S(2)}) async-start(bf16[16,24,1024]{2,1,0:T(8,128)(2,1)} %get-tuple-element.70), calls=%async_computation | async-start | bytes 1572864 | tf_op jit(solution)/shard_map/all_to_all | solution.py:1107
  27.4 54.9 %collective-permute-start.9 = (bf16[16,48,384]{2,1,0:T(8,128)(2,1)}, bf16[16,48,384]{2,1,0:T(8,128)(2,1)}, u32[]{:S(2)}, u32[]{:S(2)}) collective-permute-start(bf16[16,48,384]{2,1,0:T(8,128)(2,1)} %get-tuple-element.77.refs_12_), channel_id=1, source_target_pairs={{0,16},{16,0},{1,17},{17,1},{2,18},{18,2},{3,19},{19,3},{4,20},{20... | collective-permute-start | bytes 1769480 | tf_op jit(solution)/shard_map/ppermute | solution.py:992
  27.4 54.8 %collective-permute-start.8 = (bf16[384,1536]{1,0:T(8,128)(2,1)S(1)}, bf16[384,1536]{1,0:T(8,128)(2,1)S(1)}, u32[]{:S(2)}, u32[]{:S(2)}) collective-permute-start(bf16[384,1536]{1,0:T(8,128)(2,1)S(1)} %copy-done.4), channel_id=1, source_target_pairs={{0,16},{16,0},{1,17},{17,1},{2,18},{18,2},{3,19},{19,3},{4,20},{20... | collective-permute-start | bytes 3538952 | tf_op jit(solution)/shard_map/ppermute | solution.py:992
  59.1 25.6 %copy-start.2 = (bf16[16,24,1024]{2,1,0:T(8,128)(2,1)}, bf16[16,24,1024]{2,1,0:T(8,128)(2,1)S(1)}, u32[]{:S(2)}) copy-start(bf16[16,24,1024]{2,1,0:T(8,128)(2,1)S(1)} %all-to-all-done.refs_5_) | copy-start | bytes 2359300
  59.1 6.1 %collective-permute-start.2 = (bf16[1,24,768]{2,1,0:T(8,128)(2,1)}, bf16[1,24,768]{2,1,0:T(8,128)(2,1)S(1)}, u32[]{:S(2)}, u32[]{:S(2)}) collective-permute-start(bf16[1,24,768]{2,1,0:T(8,128)(2,1)} %bitcast.13), channel_id=1, source_target_pairs={{0,12},{1,13},{2,14},{3,15},{4,8},{5,9},{6,10},{7,11},{8,4},{9,5},... | collective-permute-start | bytes 110600 | tf_op jit(solution)/shard_map/ppermute | solution.py:992
  62.9 5.1 %collective-permute-start.1 = (bf16[1,24,768]{2,1,0:T(8,128)(2,1)}, bf16[1,24,768]{2,1,0:T(8,128)(2,1)S(1)}, u32[]{:S(2)}, u32[]{:S(2)}) collective-permute-start(bf16[1,24,768]{2,1,0:T(8,128)(2,1)} %bitcast.14), channel_id=1, source_target_pairs={{0,8},{1,9},{2,10},{3,11},{4,12},{5,13},{6,14},{7,15},{8,0},{9,1},... | collective-permute-start | bytes 110600 | tf_op jit(solution)/shard_map/ppermute | solution.py:992
  62.9 5.1 %collective-permute-start = (bf16[1,24,768]{2,1,0:T(8,128)(2,1)}, bf16[1,24,768]{2,1,0:T(8,128)(2,1)S(1)}, u32[]{:S(2)}, u32[]{:S(2)}) collective-permute-start(bf16[1,24,768]{2,1,0:T(8,128)(2,1)} %bitcast.15), channel_id=1, source_target_pairs={{0,4},{1,5},{2,6},{3,7},{4,0},{5,1},{6,2},{7,3},{8,12},{9,13},{10,... | collective-permute-start | bytes 110600 | tf_op jit(solution)/shard_map/ppermute | solution.py:992
  65.2 18.4 %collective-permute-start.7 = (bf16[16,24,1024]{2,1,0:T(8,128)(2,1)S(1)}, bf16[16,24,1024]{2,1,0:T(8,128)(2,1)S(1)}, u32[]{:S(2)}, u32[]{:S(2)}) collective-permute-start(bf16[16,24,1024]{2,1,0:T(8,128)(2,1)S(1)} %all-to-all-done.refs_5_), channel_id=1, source_target_pairs={{0,16},{16,0},{1,17},{17,1},{2,18},{18,2},{3,19},{19,3},{4,20},{20... | collective-permute-start | bytes 2359304 | tf_op jit(solution)/shard_map/ppermute | solution.py:992
  68.7 16.0 %copy-start.17 = (bf16[4,24,768]{2,1,0:T(8,128)(2,1)}, bf16[4,24,768]{2,1,0:T(8,128)(2,1)S(1)}, u32[]{:S(2)}) copy-start(bf16[4,24,768]{2,1,0:T(8,128)(2,1)S(1)} %pad_maximum_fusion.1.refs_0_) | copy-start | bytes 442372
  68.7 8.1 %collective-permute-start.4 = (bf16[4,24,768]{2,1,0:T(8,128)(2,1)S(1)}, bf16[4,24,768]{2,1,0:T(8,128)(2,1)S(1)}, u32[]{:S(2)}, u32[]{:S(2)}) collective-permute-start(bf16[4,24,768]{2,1,0:T(8,128)(2,1)S(1)} %pad_maximum_fusion.1.refs_0_), channel_id=1, source_target_pairs={{0,2},{1,3},{2,0},{3,1},{4,6},{5,7},{6,4},{7,5},{8,10},{9,11},{10,... | collective-permute-start | bytes 442376 | tf_op jit(solution)/shard_map/ppermute | solution.py:992
  70.3 5.1 %collective-permute-start.3 = (bf16[4,24,768]{2,1,0:T(8,128)(2,1)S(1)}, bf16[4,24,768]{2,1,0:T(8,128)(2,1)S(1)}, u32[]{:S(2)}, u32[]{:S(2)}) collective-permute-start(bf16[4,24,768]{2,1,0:T(8,128)(2,1)S(1)} %pad_maximum_fusion.1.refs_0_), channel_id=1, source_target_pairs={{0,1},{1,0},{2,3},{3,2},{4,5},{5,4},{6,7},{7,6},{8,9},{9,8},{10,11... | collective-permute-start | bytes 442376 | tf_op jit(solution)/shard_map/ppermute | solution.py:992
  75.4 9.3 %copy-start.19 = (bf16[4,24,768]{2,1,0:T(8,128)(2,1)}, bf16[4,24,768]{2,1,0:T(8,128)(2,1)S(1)}, u32[]{:S(2)}) copy-start(bf16[4,24,768]{2,1,0:T(8,128)(2,1)S(1)} %collective-permute-done.3.refs_1_) | copy-start | bytes 442372
  75.4 6.0 %collective-permute-start.5 = (bf16[4,24,768]{2,1,0:T(8,128)(2,1)S(1)}, bf16[4,24,768]{2,1,0:T(8,128)(2,1)S(1)}, u32[]{:S(2)}, u32[]{:S(2)}) collective-permute-start(bf16[4,24,768]{2,1,0:T(8,128)(2,1)S(1)} %pad_maximum_fusion.1.refs_0_), channel_id=1, source_target_pairs={{0,3},{1,2},{2,1},{3,0},{4,7},{5,6},{6,5},{7,4},{8,11},{9,10},{10,... | collective-permute-start | bytes 442376 | tf_op jit(solution)/shard_map/ppermute | solution.py:992
  81.5 2.1 %collective-permute-start.6 = (bf16[16,24,768]{2,1,0:T(8,128)(2,1)S(1)}, bf16[16,24,768]{2,1,0:T(8,128)(2,1)S(1)}, u32[]{:S(2)}, u32[]{:S(2)}) collective-permute-start(bf16[16,24,768]{2,1,0:T(8,128)(2,1)S(1)} %constant_dynamic-update-slice_fusion), channel_id=1, source_target_pairs={{0,16},{16,0},{1,17},{17,1},{2,18},{18,2},{3,19},{19,3},{4,20},{20... | collective-permute-start | bytes 1769480 | tf_op jit(solution)/shard_map/ppermute | solution.py:992
  101.6 21.0 %collective-permute-start.10 = (bf16[384,768]{1,0:T(8,128)(2,1)}, bf16[384,768]{1,0:T(8,128)(2,1)S(1)}, u32[]{:S(2)}, u32[]{:S(2)}) collective-permute-start(bf16[384,768]{1,0:T(8,128)(2,1)} %get-tuple-element.91), channel_id=1, source_target_pairs={{0,1},{1,0},{2,3},{3,2},{4,5},{5,4},{6,7},{7,6},{8,9},{9,8},{10,11... | collective-permute-start | bytes 1769480 | tf_op jit(solution)/shard_map/ppermute | solution.py:992
  103.1 19.5 %collective-permute-start.11 = (bf16[384,768]{1,0:T(8,128)(2,1)}, bf16[384,768]{1,0:T(8,128)(2,1)S(1)}, u32[]{:S(2)}, u32[]{:S(2)}) collective-permute-start(bf16[384,768]{1,0:T(8,128)(2,1)} %get-tuple-element.93), channel_id=1, source_target_pairs={{0,2},{1,3},{2,0},{3,1},{4,6},{5,7},{6,4},{7,5},{8,10},{9,11},{10,... | collective-permute-start | bytes 1769480 | tf_op jit(solution)/shard_map/ppermute | solution.py:992
  137.4 11.0 %collective-permute-start.13 = (bf16[2,384,896]{2,1,0:T(8,128)(2,1)}, bf16[2,384,896]{2,1,0:T(8,128)(2,1)S(1)}, u32[]{:S(2)}, u32[]{:S(2)}) collective-permute-start(bf16[2,384,896]{2,1,0:T(8,128)(2,1)} %get-tuple-element.97), channel_id=1, source_target_pairs={{0,16},{16,0},{1,17},{17,1},{2,18},{18,2},{3,19},{19,3},{4,20},{20... | collective-permute-start | bytes 4128776 | tf_op jit(solution)/shard_map/ppermute | solution.py:992
  137.5 10.9 %collective-permute-start.12 = (bf16[2,384,768]{2,1,0:T(8,128)(2,1)}, bf16[2,384,768]{2,1,0:T(8,128)(2,1)S(1)}, u32[]{:S(2)}, u32[]{:S(2)}) collective-permute-start(bf16[2,384,768]{2,1,0:T(8,128)(2,1)} %get-tuple-element.95), channel_id=1, source_target_pairs={{0,16},{16,0},{1,17},{17,1},{2,18},{18,2},{3,19},{19,3},{4,20},{20... | collective-permute-start | bytes 3538952 | tf_op jit(solution)/shard_map/ppermute | solution.py:992
  138.0 9.2 %collective-permute-start.14 = (bf16[192,768]{1,0:T(8,128)(2,1)}, bf16[192,768]{1,0:T(8,128)(2,1)S(1)}, u32[]{:S(2)}, u32[]{:S(2)}) collective-permute-start(bf16[192,768]{1,0:T(8,128)(2,1)} %get-tuple-element.98), channel_id=1, source_target_pairs={{0,2},{1,3},{2,0},{3,1},{4,6},{5,7},{6,4},{7,5},{8,10},{9,11},{10,... | collective-permute-start | bytes 884744 | tf_op jit(solution)/shard_map/ppermute | solution.py:992
  139.5 8.9 %collective-permute-start.15 = (bf16[192,768]{1,0:T(8,128)(2,1)}, bf16[192,768]{1,0:T(8,128)(2,1)S(1)}, u32[]{:S(2)}, u32[]{:S(2)}) collective-permute-start(bf16[192,768]{1,0:T(8,128)(2,1)} %get-tuple-element.99), channel_id=1, source_target_pairs={{0,1},{1,0},{2,3},{3,2},{4,5},{5,4},{6,7},{7,6},{8,9},{9,8},{10,11... | collective-permute-start | bytes 884744 | tf_op jit(solution)/shard_map/ppermute | solution.py:992
  153.0 16.5 %collective-permute-start.18 = (bf16[384,896]{1,0:T(8,128)(2,1)}, bf16[384,896]{1,0:T(8,128)(2,1)S(1)}, u32[]{:S(2)}, u32[]{:S(2)}) collective-permute-start(bf16[384,896]{1,0:T(8,128)(2,1)} %get-tuple-element.100.order_any.rest_0_), channel_id=1, source_target_pairs={{0,2},{1,3},{2,0},{3,1},{4,6},{5,7},{6,4},{7,5},{8,10},{9,11},{10,... | collective-permute-start | bytes 2064392 | tf_op jit(solution)/shard_map/ppermute | solution.py:992
  153.6 14.3 %collective-permute-start.17 = (bf16[384,768]{1,0:T(8,128)(2,1)}, bf16[384,768]{1,0:T(8,128)(2,1)S(1)}, u32[]{:S(2)}, u32[]{:S(2)}) collective-permute-start(bf16[384,768]{1,0:T(8,128)(2,1)} %get-tuple-element.103), channel_id=1, source_target_pairs={{0,1},{1,0},{2,3},{3,2},{4,5},{5,4},{6,7},{7,6},{8,9},{9,8},{10,11... | collective-permute-start | bytes 1769480 | tf_op jit(solution)/shard_map/ppermute | solution.py:992
  156.5 18.1 %collective-permute-start.21 = (bf16[48,1536]{1,0:T(8,128)(2,1)}, bf16[48,1536]{1,0:T(8,128)(2,1)S(1)}, u32[]{:S(2)}, u32[]{:S(2)}) collective-permute-start(bf16[48,1536]{1,0:T(8,128)(2,1)} %get-tuple-element.110), channel_id=1, source_target_pairs={{0,4},{1,5},{2,6},{3,7},{4,0},{5,1},{6,2},{7,3},{8,12},{9,13},{10,... | collective-permute-start | bytes 442376 | tf_op jit(solution)/shard_map/ppermute | solution.py:992
  156.7 19.4 %collective-permute-start.22 = (bf16[48,1536]{1,0:T(8,128)(2,1)}, bf16[48,1536]{1,0:T(8,128)(2,1)S(1)}, u32[]{:S(2)}, u32[]{:S(2)}) collective-permute-start(bf16[48,1536]{1,0:T(8,128)(2,1)} %get-tuple-element.111), channel_id=1, source_target_pairs={{0,8},{1,9},{2,10},{3,11},{4,12},{5,13},{6,14},{7,15},{8,0},{9,1},... | collective-permute-start | bytes 442376 | tf_op jit(solution)/shard_map/ppermute | solution.py:992
  159.1 16.9 %collective-permute-start.23 = (bf16[48,1536]{1,0:T(8,128)(2,1)}, bf16[48,1536]{1,0:T(8,128)(2,1)S(1)}, u32[]{:S(2)}, u32[]{:S(2)}) collective-permute-start(bf16[48,1536]{1,0:T(8,128)(2,1)} %get-tuple-element.112), channel_id=1, source_target_pairs={{0,12},{1,13},{2,14},{3,15},{4,8},{5,9},{6,10},{7,11},{8,4},{9,5},... | collective-permute-start | bytes 442376 | tf_op jit(solution)/shard_map/ppermute | solution.py:992
  167.9 9.0 %collective-permute-start.16 = (bf16[24,8,768]{2,1,0:T(8,128)(2,1)}, bf16[24,8,768]{2,1,0:T(8,128)(2,1)S(1)}, u32[]{:S(2)}, u32[]{:S(2)}) collective-permute-start(bf16[24,8,768]{2,1,0:T(8,128)(2,1)} %get-tuple-element.102), channel_id=1, source_target_pairs={{0,16},{16,0},{1,17},{17,1},{2,18},{18,2},{3,19},{19,3},{4,20},{20... | collective-permute-start | bytes 884744 | tf_op jit(solution)/shard_map/ppermute | solution.py:992
  173.9 8.2 %collective-permute-start.19 = (bf16[192,768]{1,0:T(8,128)(2,1)}, bf16[192,768]{1,0:T(8,128)(2,1)S(1)}, u32[]{:S(2)}, u32[]{:S(2)}) collective-permute-start(bf16[192,768]{1,0:T(8,128)(2,1)} %get-tuple-element.106), channel_id=1, source_target_pairs={{0,2},{1,3},{2,0},{3,1},{4,6},{5,7},{6,4},{7,5},{8,10},{9,11},{10,... | collective-permute-start | bytes 884744 | tf_op jit(solution)/shard_map/ppermute | solution.py:992
  174.7 9.7 %collective-permute-start.20 = (bf16[192,896]{1,0:T(8,128)(2,1)}, bf16[192,896]{1,0:T(8,128)(2,1)S(1)}, u32[]{:S(2)}, u32[]{:S(2)}) collective-permute-start(bf16[192,896]{1,0:T(8,128)(2,1)} %get-tuple-element.107), channel_id=1, source_target_pairs={{0,1},{1,0},{2,3},{3,2},{4,5},{5,4},{6,7},{7,6},{8,9},{9,8},{10,11... | collective-permute-start | bytes 1032200 | tf_op jit(solution)/shard_map/ppermute | solution.py:992
  187.5 13.4 %collective-permute-start.24 = (bf16[48,1664]{1,0:T(8,128)(2,1)}, bf16[48,1664]{1,0:T(8,128)(2,1)S(1)}, u32[]{:S(2)}, u32[]{:S(2)}) collective-permute-start(bf16[48,1664]{1,0:T(8,128)(2,1)} %get-tuple-element.114), channel_id=1, source_target_pairs={{0,4},{1,5},{2,6},{3,7},{4,0},{5,1},{6,2},{7,3},{8,12},{9,13},{10,... | collective-permute-start | bytes 479240 | tf_op jit(solution)/shard_map/ppermute | solution.py:992
  187.5 14.3 %collective-permute-start.25 = (bf16[48,1664]{1,0:T(8,128)(2,1)}, bf16[48,1664]{1,0:T(8,128)(2,1)S(1)}, u32[]{:S(2)}, u32[]{:S(2)}) collective-permute-start(bf16[48,1664]{1,0:T(8,128)(2,1)} %get-tuple-element.115), channel_id=1, source_target_pairs={{0,8},{1,9},{2,10},{3,11},{4,12},{5,13},{6,14},{7,15},{8,0},{9,1},... | collective-permute-start | bytes 479240 | tf_op jit(solution)/shard_map/ppermute | solution.py:992
  190.1 11.7 %collective-permute-start.26 = (bf16[48,1664]{1,0:T(8,128)(2,1)}, bf16[48,1664]{1,0:T(8,128)(2,1)S(1)}, u32[]{:S(2)}, u32[]{:S(2)}) collective-permute-start(bf16[48,1664]{1,0:T(8,128)(2,1)} %get-tuple-element.116), channel_id=1, source_target_pairs={{0,12},{1,13},{2,14},{3,15},{4,8},{5,9},{6,10},{7,11},{8,4},{9,5},... | collective-permute-start | bytes 479240 | tf_op jit(solution)/shard_map/ppermute | solution.py:992
  (24 other events, 53.7 us)
where the time goes:
time: 206 us; the launch traced here: 205 us
  Pallas kernels  123 us (60%)
  starting transfers between devices  34.9 us (17%)
  waiting for transfers between devices  31.1 us (15%)
  local copies, waits for them, and re-layouts  10.2 us (5%)
  other arithmetic  2.74 us (1%)
  between operations  2.38 us (1%)
    pallas_call x12, Pallas kernels, call(): pl.pallas_call(kernel, name=name, in_specs=in_specs, out_shape=[jax.Shape...  123 us
    ppermute x27, waiting for transfers between devices, xor_permute(): lax.ppermute(x, axis, [(i, i ^ bit) for i in range(lax.axis_size(axis))])  31.1 us
    ppermute x27, starting transfers between devices, xor_permute(): lax.ppermute(x, axis, [(i, i ^ bit) for i in range(lax.axis_size(axis))])  26.4 us
    all_to_all x1, starting transfers between devices, body(): text_all = lax.all_to_all(text_send, 'dp', 0, 0, tiled=True)  8.47 us
    unnamed x62, local copies, waits for them, and re-layouts  6.93 us
  transfers between devices with their start and end apart: 28, of which 11 were waited for; matrix products, arithmetic and copies ran while one was open for 2% of the time, Pallas kernels for 34%

commit v1 on v0

--- a/solution.py
+++ b/solution.py
@@ -1,3 +1,4 @@
+import math
 from functools import partial
 
 import jax
@@ -17,6 +18,8 @@
 embed_eps = 1e-06
 NEG = -1000000000.0
 VMEM_LIMIT = 60 * 1024 * 1024
+MARGIN = 8 * 1024 * 1024
+SMALL = ("merge_expand", "merge_qkv", "finish", "reduce_grad")
 
 
 def normal_cdf(x):
@@ -71,6 +74,12 @@
     out[:, :width] = row(biases, 2)
     out[:, width : 2 * width] = jnp.zeros((1, width), F32)
     out[:, 2 * width :] = row(biases, 3)
+
+
+def set_hidden_bias(out, hid):
+    lines = hid[...].astype(F32)
+    for i in range(hid.shape[0]):
+        out[:, i * LANES : (i + 1) * LANES] = lines[i : i + 1]
 
 
 def two_heads(x, masks):
@@ -106,13 +115,13 @@
 def text_forward_kernel(
     scal, h_any, gains, biases, hid, wq_any, wp_any, we_any, wr_any,
     a_any, qkv_any, o_any, m_any, c_any, gpk_any, gps_any, send_out, emb_out, r_out,
-    h_v, wq, wp, we, wr, qb, av, cv, gsum, a_out, qkv_out, o_out, m_out, c_out, gp_keep, gp_send,
+    h_v, wq, wp, we, wr, qb, hb, av, cv, gsum, a_out, qkv_out, o_out, m_out, c_out, gp_keep, gp_send,
     sems, out_sems,
 ):
     n, width = m_out.shape
     caps = emb_out.shape[0]
     length = n // caps
-    hidden = hid.shape[1]
+    hidden = hid.shape[0] * LANES
     t, d = scal[0], scal[1]
     load_h = load(h_any.at[pl.ds(pl.multiple_of(t * n, n), n)], h_v, sems.at[0])
     load_q = load(wq_any, wq, sems.at[1])
@@ -140,6 +149,7 @@
     load_e = load(we_any, we, sems.at[3])
     load_r = load(wr_any, wr, sems.at[4])
     set_qkv_bias(qb, biases)
+    set_hidden_bias(hb, hid)
 
     def to_qkv(j, carry):
         cols = pl.ds(pl.multiple_of(j * 256, 256), 256)
@@ -185,7 +195,7 @@
             local = pl.ds(pl.multiple_of(j * 256, 256), 256)
             at = jnp.bitwise_xor(t, rel) * half + j
             cols = pl.ds(pl.multiple_of(at * 256, 256), 256)
-            f = dot(cv[...], we[:, cols]) + hid[:, cols].astype(F32)
+            f = dot(cv[...], we[:, cols]) + hb[:, cols]
             cdf = normal_cdf(f)
             density = jnp.exp(f * f * -0.5) * 0.3989422804014327
             gp_out[:, local] = (cdf + f * density).astype(BF16)
@@ -236,12 +246,12 @@
 def image_forward_kernel(
     scal, x_any, gains, biases, hid, wq_any, wp_any, we_any, wr_any,
     out,
-    x_v, xs, hv, av, qkv, mv, msum, gsum, wq, wp, we, wr, qb, pb, sems,
+    x_v, xs, hv, av, qkv, mv, msum, gsum, wq, wp, we, wr, qb, hb, pb, sems,
 ):
     length, both_caps, width = x_v.shape
     caps = both_caps // 2
     n = caps * PAD
-    hidden = hid.shape[1]
+    hidden = hid.shape[0] * LANES
     t = scal[0]
     load_x = load(x_any, x_v, sems.at[0])
     load_q = load(wq_any, wq, sems.at[1])
@@ -284,6 +294,7 @@
     load_e = load(we_any, we, sems.at[3])
     load_r = load(wr_any, wr, sems.at[4])
     set_qkv_bias(qb, biases)
+    set_hidden_bias(hb, hid)
 
     def to_qkv(j, carry):
         cols = pl.ds(pl.multiple_of(j * 256, 256), 256)
@@ -341,7 +352,7 @@
 
     def feed(j, carry):
         cols = pl.ds(pl.multiple_of(j * 256, 256), 256)
-        f = dot(av[...], we[:, cols]) + hid[:, cols].astype(F32)
+        f = dot(av[...], we[:, cols]) + hb[:, cols]
         gsum[:, cols] = token_sum(f * normal_cdf(f), caps)
         return carry
 
@@ -1042,7 +1053,20 @@
 ANY = pl.BlockSpec(memory_space=pl.ANY)
 
 
+def padded_bytes(shape, dtype):
+    size = jnp.dtype(dtype).itemsize
+    shape = (1,) * (2 - len(shape)) + tuple(shape)
+    rows = -(-shape[-2] // 16) * 16
+    return math.prod(shape[:-2]) * rows * (-(-shape[-1] // LANES) * LANES) * size
+
+
 def call(kernel, name, in_specs, outs, out_specs, scratch, args, flops, moved):
+    held = [(x.shape, x.dtype) for x in scratch if jnp.issubdtype(x.dtype, jnp.floating)]
+    held += [(a.shape, a.dtype) for a, spec in zip(args, in_specs) if spec is VMEM]
+    held += [o for o, spec in zip(outs, out_specs) if spec is VMEM]
+    limit = VMEM_LIMIT
+    if name in SMALL:
+        limit = min(limit, sum(padded_bytes(*x) for x in held) + MARGIN)
     return pl.pallas_call(
         kernel,
         name=name,
@@ -1050,7 +1074,7 @@
         out_shape=[jax.ShapeDtypeStruct(s, d) for s, d in outs],
         out_specs=out_specs,
         scratch_shapes=scratch,
-        compiler_params=pltpu.CompilerParams(vmem_limit_bytes=VMEM_LIMIT),
+        compiler_params=pltpu.CompilerParams(vmem_limit_bytes=limit),
         cost_estimate=pl.CostEstimate(flops=flops, bytes_accessed=moved, transcendentals=0),
     )(*args)
 
@@ -1081,7 +1105,7 @@
     scal = jnp.concatenate([head, row_slots, slots])
 
     texts_in = captions.reshape(pairs * length, width)
-    c_hid2, p_hid2 = c_hid.reshape(1, hidden), p_hid.reshape(1, hidden)
+    c_hid2, p_hid2 = c_hid.reshape(hidden // LANES, LANES), p_hid.reshape(hidden // LANES, LANES)
     blk = (row_blocks, width // row_blocks, n)
     vm = pltpu.VMEM
     sem = pltpu.SemaphoreType.DMA
@@ -1096,6 +1120,7 @@
         [ANY] * 7 + [VMEM] * 3,
         [vm((n, width), BF16), vm((width, 3 * width), BF16), vm((width, width), BF16),
          vm((width, hidden), BF16), vm((hidden, width), BF16), vm((1, 3 * width), F32),
+         vm((1, hidden), F32),
          vm((n, width), BF16), vm((n, width), BF16), vm((caps, hidden), F32), vm(blk, BF16), vm((n, 3 * width), BF16),
          vm(blk, BF16), vm((n, width), F32), vm(blk, BF16), vm(half_hid, BF16),
          vm(half_hid, BF16), sem((5,)), sem((7,))],
@@ -1118,6 +1143,7 @@
          vm((rows + 16, 3 * width), BF16), vm((rows, width), F32), vm((caps, width), F32),
          vm((caps, hidden), F32), vm((width, 3 * width), BF16), vm((width, width), BF16),
          vm((width, hidden), BF16), vm((hidden, width), BF16), vm((1, 3 * width), F32),
+         vm((1, hidden), F32),
          vm((1, width), F32), sem((5,))],
         (scal, jnp.transpose(pictures, (1, 0, 2)), p_gains, p_biases, p_hid2,
          p_wq, p_wp, p_we, p_wr),

time: 206 us -> 200 us (0.971)
  Pallas kernels: 123 us -> 117 us
    pallas_call x12, Pallas kernels: 123 us -> 117 us  [call(): pl.pallas_call(kernel, name=name, in_specs=in_specs, out_shape=[jax.Shape...]
    unnamed x62 -> x68, local copies, waits for them, and re-layouts: 6.93 us -> 8.61 us
  transfers between devices with their start and end apart: 28 -> 28, of which waited for: 11 -> 11; matrix products, arithmetic and copies ran while one was open for 2% -> 2% of each run, Pallas kernels for 34% -> 33%
where the time goes in v1:
time: 200 us; the launch traced here: 199 us
  Pallas kernels  117 us (58%)
  starting transfers between devices  35.8 us (18%)
  waiting for transfers between devices  30.8 us (15%)
  local copies, waits for them, and re-layouts  9.92 us (5%)
  other arithmetic  2.74 us (1%)
  between operations  2.33 us (1%)
    pallas_call x12, Pallas kernels, call(): pl.pallas_call(kernel, name=name, in_specs=in_specs, out_shape=[jax.Shape...  117 us
    ppermute x27, waiting for transfers between devices, xor_permute(): lax.ppermute(x, axis, [(i, i ^ bit) for i in range(lax.axis_size(axis))])  30.8 us
    ppermute x27, starting transfers between devices, xor_permute(): lax.ppermute(x, axis, [(i, i ^ bit) for i in range(lax.axis_size(axis))])  27.4 us
    unnamed x68, local copies, waits for them, and re-layouts  8.61 us
    all_to_all x1, starting transfers between devices, body(): text_all = lax.all_to_all(text_send, 'dp', 0, 0, tiled=True)  8.47 us
  transfers between devices with their start and end apart: 28, of which 11 were waited for; matrix products, arithmetic and copies ran while one was open for 2% of the time, Pallas kernels for 33%

profile of v1, /device:TPU:0, one launch (start us, length us, event | category | flops | bytes accessed | tf_op | source)
XLA Modules:
  0.0 198.6 jit_solution(1413816657375612914)
XLA Ops:
  2.6 15.5 %text_forward.1 = (bf16[16,48,384]{2,1,0:T(8,128)(2,1)}, bf16[384,2304]{1,0:T(8,128)(2,1)}, bf16[16,48,384]{2,1,0:T(8,128)(2,1)}, f32[384,768]{1,0:T(8,128)}, bf...) custom-call(s32[36]{0:T(128)} %concatenate.13.scal, ...), custom_call_target="tpu_custom_call" | custom-call | flops 3623878656 | bytes 20000000 | tf_op jit(solution)/shard_map/text_forward/pallas_call | solution.py:1070
  18.1 8.5 %all-to-all-start = ((bf16[16,24,1024]{2,1,0:T(8,128)(2,1)}), bf16[16,24,1024]{2,1,0:T(8,128)(2,1)S(1)}, u32[]{:S(2)}, u32[]{:S(2)}) async-start(bf16[16,24,1024]{2,1,0:T(8,128)(2,1)} %get-tuple-element.70), calls=%async_computation | async-start | bytes 1572864 | tf_op jit(solution)/shard_map/all_to_all | solution.py:1132
  27.2 30.4 %image_forward.1 = bf16[24,768]{1,0:T(8,128)(2,1)} custom-call(s32[36]{0:T(128)} %concatenate.13.scal, bf16[50,48,768]{2,1,0:T(8,128)(2,1)} %bitcast.20, bf16[2,768]{1,0:T(2,128)(2,1)} %gains.5, bf16[6,768]{1,0:T(8,128)(2,1)} %biases.3, bf16[24,128]{1,0:T(8,128)(2,1)} %bitcast.21, bf16[768,2304]{1,0:T(8,128)(2,1)} %wq_any.4, bf16[768,768]{1,0:T(8,128)(2,1)} %wp_any.3, ...), custom_call_target="tpu_custom_call" | custom-call | flops 12683575296 | bytes 20000000 | tf_op jit(solution)/shard_map/image_forward/pallas_call | solution.py:1070
  57.6 3.8 %collective-permute-start.2 = (bf16[1,24,768]{2,1,0:T(8,128)(2,1)}, bf16[1,24,768]{2,1,0:T(8,128)(2,1)S(1)}, u32[]{:S(2)}, u32[]{:S(2)}) collective-permute-start(bf16[1,24,768]{2,1,0:T(8,128)(2,1)} %bitcast.15), channel_id=1, source_target_pairs={{0,12},{1,13},{2,14},{3,15},{4,8},{5,9},{6,10},{7,11},{8,4},{9,5},... | collective-permute-start | bytes 110600 | tf_op jit(solution)/shard_map/ppermute | solution.py:1003
  63.7 2.8 %collective-permute-done.1 = bf16[1,24,768]{2,1,0:T(8,128)(2,1)S(1)} collective-permute-done((bf16[1,24,768]{2,1,0:T(8,128)(2,1)}, bf16[1,24,768]{2,1,0:T(8,128)(2,1)S(1)}, u32[]{:S(2)}, u32[]{:S(2)}) %collective-permute-start.1) | collective-permute-done | bytes 36896 | tf_op jit(solution)/shard_map/ppermute | solution.py:1003
  67.3 1.5 collective-permute-start.4
  68.8 1.5 collective-permute-start.3
  70.3 3.7 %collective-permute-done.3.refs_1_ = bf16[4,24,768]{2,1,0:T(8,128)(2,1)S(1)} collective-permute-done((bf16[4,24,768]{2,1,0:T(8,128)(2,1)S(1)}, bf16[4,24,768]{2,1,0:T(8,128)(2,1)S(1)}, u32[]{:S(2)}, u32[]{:S(2)}) %collective-permute-start.3) | collective-permute-done | bytes 147488 | tf_op jit(solution)/shard_map/ppermute | solution.py:1003
  74.0 1.5 collective-permute-start.5
  75.5 4.5 %collective-permute-done.5.refs_3_ = bf16[4,24,768]{2,1,0:T(8,128)(2,1)S(1)} collective-permute-done((bf16[4,24,768]{2,1,0:T(8,128)(2,1)S(1)}, bf16[4,24,768]{2,1,0:T(8,128)(2,1)S(1)}, u32[]{:S(2)}, u32[]{:S(2)}) %collective-permute-start.5) | collective-permute-done | bytes 147488 | tf_op jit(solution)/shard_map/ppermute | solution.py:1003
  80.8 1.3 collective-permute-done.6.refs_4_
  83.3 16.8 %loss.1 = (f32[1,1]{1,0:T(1,128)}, f32[1,1]{1,0:T(1,128)}, bf16[384,768]{1,0:T(8,128)(2,1)}, bf16[384,768]{1,0:T(8,128)(2,1)}, bf16[384,768]{1,0:T(8,128)(2,1)},...) custom-call(s32[36]{0:T(128)} %concatenate.13.scal, ...), custom_call_target="tpu_custom_call" | custom-call | flops 2717908992 | bytes 20000000 | tf_op jit(solution)/shard_map/loss/pallas_call | solution.py:1070
  100.1 1.5 collective-permute-start.10
  102.2 18.9 %middle_back.1 = (f32[384,768]{1,0:T(8,128)}, bf16[384,2304]{1,0:T(8,128)(2,1)}, f32[8,768]{1,0:T(8,128)}) custom-call(s32[36]{0:T(128)} %concatenate.13.scal, f32[384,768]{1,0:T(8,128)} %get-tuple-element.80.dc_any, f32[24,768]{1,0:T(8,128)} %get-tuple-element.81.dy, bf16[384,1536]{1,0:T(8,128)(2,1)} %get-tuple-element.76.gps_any, ...), custom_call_target="tpu_custom_call" | custom-call | flops 3623878656 | bytes 20000000 | tf_op jit(solution)/shard_map/middle_back/pallas_call | solution.py:1070
  122.2 13.8 %weight_grad.1 = (bf16[2,384,768]{2,1,0:T(8,128)(2,1)}, bf16[2,384,896]{2,1,0:T(8,128)(2,1)}, bf16[2,384,768]{2,1,0:T(8,128)(2,1)}, bf16[2,384,896]{2,1,0:T(8,12...) custom-call(s32[36]{0:T(128)} %concatenate.13.scal, ...), custom_call_target="tpu_custom_call" | custom-call | flops 1811939328 | bytes 20000000 | tf_op jit(solution)/shard_map/weight_grad/pallas_call | solution.py:1070
  136.6 1.5 collective-permute-start.14
  138.6 7.2 %collective-permute-done.14.far_a.hop_a = bf16[192,768]{1,0:T(8,128)(2,1)S(1)} collective-permute-done((bf16[192,768]{1,0:T(8,128)(2,1)}, bf16[192,768]{1,0:T(8,128)(2,1)S(1)}, u32[]{:S(2)}, u32[]{:S(2)}) %collective-permute-start.14) | collective-permute-done | bytes 294944 | tf_op jit(solution)/shard_map/ppermute | solution.py:1003
  145.8 1.2 collective-permute-done.15.far_b.hop_b
  148.6 3.1 %wire.1 = (bf16[384,768]{1,0:T(8,128)(2,1)}, bf16[384,896]{1,0:T(8,128)(2,1)}) custom-call(bf16[2,384,768]{2,1,0:T(8,128)(2,1)} %get-tuple-element.94.qa.refs_0_, bf16[2,384,768]{2,1,0:T(8,128)(2,1)} %copy-done.18, bf16[2,384,896]{2,1,0:T(8,128)(2,1)} %get-tuple-element.96.qb.refs_3_, bf16[2,384,896]{2,1,0:T(8,128)(2,1)} %copy-done.17, ...), custom_call_target="tpu_custom_call" | custom-call | flops 1000000 | bytes 4000000 | tf_op jit(solution)/shard_map/wire/pallas_call | solution.py:1070
  156.3 2.4 %collective-permute-start.22 = (bf16[48,1536]{1,0:T(8,128)(2,1)S(1)}, bf16[48,1536]{1,0:T(8,128)(2,1)S(1)}, u32[]{:S(2)}, u32[]{:S(2)}) collective-permute-start(bf16[48,1536]{1,0:T(8,128)(2,1)S(1)} %get-tuple-element.111), channel_id=1, source_target_pairs={{0,8},{1,9},{2,10},{3,11},{4,12},{5,13},{6,14},{7,15},{8,0},{9,1},... | collective-permute-start | bytes 442376 | tf_op jit(solution)/shard_map/ppermute | solution.py:1003
  158.7 1.8 collective-permute-start.23
  160.5 7.0 %input_back.1 = (f32[24,8,768]{2,1,0:T(8,128)}, bf16[24,8,768]{2,1,0:T(8,128)(2,1)}) custom-call(s32[36]{0:T(128)} %concatenate.13.scal, f32[384,768]{1,0:T(8,128)} %get-tuple-element.84.dm_any, bf16[768,768]{1,0:T(8,128)(2,1)} %bitcast.14, bf16[2,768]{1,0:T(2,128)(2,1)} %gains.9, bf16[384,2304]{1,0:T(8,128)(2,1)} %get-tuple-element.85.dqkv_any, ...), custom_call_target="tpu_custom_call" | custom-call | flops 1358954496 | bytes 9000000 | tf_op jit(solution)/shard_map/input_back/pallas_call | solution.py:1070
  168.4 3.5 %turn_qkv.1 = (f32[192,768]{1,0:T(8,128)}, f32[192,832]{1,0:T(8,128)}, bf16[192,768]{1,0:T(8,128)(2,1)}, bf16[192,896]{1,0:T(8,128)(2,1)}) custom-call(bf16[2,384,768]{2,1,0:T(8,128)(2,1)} %get-tuple-element.94.qa.refs_0_, bf16[2,384,768]{2,1,0:T(8,128)(2,1)} %copy-done.18, bf16[384,768]{1,0:T(8,128)(2,1)} %copy-done.1, ...), custom_call_target="tpu_custom_call" | custom-call | flops 1000000 | bytes 4000000 | tf_op jit(solution)/shard_map/turn_qkv/pallas_call | solution.py:1070
  171.9 1.5 collective-permute-start.19
  173.4 1.5 collective-permute-start.20
  175.8 5.1 %collective-permute-done.19.hop_a = bf16[192,768]{1,0:T(8,128)(2,1)S(1)} collective-permute-done((bf16[192,768]{1,0:T(8,128)(2,1)}, bf16[192,768]{1,0:T(8,128)(2,1)S(1)}, u32[]{:S(2)}, u32[]{:S(2)}) %collective-permute-start.19) | collective-permute-done | bytes 294944 | tf_op jit(solution)/shard_map/ppermute | solution.py:1003
  180.8 2.2 %collective-permute-done.20.hop_b = bf16[192,896]{1,0:T(8,128)(2,1)S(1)} collective-permute-done((bf16[192,896]{1,0:T(8,128)(2,1)}, bf16[192,896]{1,0:T(8,128)(2,1)S(1)}, u32[]{:S(2)}, u32[]{:S(2)}) %collective-permute-start.20) | collective-permute-done | bytes 344096 | tf_op jit(solution)/shard_map/ppermute | solution.py:1003
  183.3 2.6 %collective-permute-start.25 = (bf16[48,1664]{1,0:T(8,128)(2,1)S(1)}, bf16[48,1664]{1,0:T(8,128)(2,1)S(1)}, u32[]{:S(2)}, u32[]{:S(2)}) collective-permute-start(bf16[48,1664]{1,0:T(8,128)(2,1)S(1)} %get-tuple-element.115), channel_id=1, source_target_pairs={{0,8},{1,9},{2,10},{3,11},{4,12},{5,13},{6,14},{7,15},{8,0},{9,1},... | collective-permute-start | bytes 479240 | tf_op jit(solution)/shard_map/ppermute | solution.py:1003
  186.0 1.8 collective-permute-start.26
  189.7 6.1 %reduce_grad.1 = (f32[96,768]{1,0:T(8,128)}, f32[8,768]{1,0:T(8,128)S(1)}) custom-call(f32[1]{0:T(128)S(6)} %copy.36.refs_7_.expo, bf16[768,768]{1,0:T(8,128)(2,1)S(1)} %copy-done.7, bf16[768,768]{1,0:T(8,128)(2,1)S(1)} %copy-done.8, bf16[768,768]{1,0:T(8,128)(2,1)S(1)} %copy-done.9, bf16[768,128]{1,0:T(8,128)(2,1)S(1)} %copy-done.15, ...), custom_call_target="tpu_custom_call" | custom-call | flops 905969664 | bytes 6000000 | tf_op jit(solution)/shard_map/reduce_grad/pallas_call | solution.py:1070
  195.9 1.3 collective-permute-done.25.hop_2
  197.1 1.5 finish.1
  (111 shorter events, 19.1 us)
Async XLA Ops:
  18.1 8.6 %copy-start.20 = (bf16[384,1536]{1,0:T(8,128)(2,1)S(1)}, bf16[384,1536]{1,0:T(8,128)(2,1)}, u32[]{:S(2)}) copy-start(bf16[384,1536]{1,0:T(8,128)(2,1)} %get-tuple-element.76.gps_any) | copy-start | bytes 3538948
  18.1 39.5 %all-to-all-start = ((bf16[16,24,1024]{2,1,0:T(8,128)(2,1)}), bf16[16,24,1024]{2,1,0:T(8,128)(2,1)S(1)}, u32[]{:S(2)}, u32[]{:S(2)}) async-start(bf16[16,24,1024]{2,1,0:T(8,128)(2,1)} %get-tuple-element.70), calls=%async_computation | async-start | bytes 1572864 | tf_op jit(solution)/shard_map/all_to_all | solution.py:1132
  26.6 54.2 %collective-permute-start.9 = (bf16[16,48,384]{2,1,0:T(8,128)(2,1)}, bf16[16,48,384]{2,1,0:T(8,128)(2,1)}, u32[]{:S(2)}, u32[]{:S(2)}) collective-permute-start(bf16[16,48,384]{2,1,0:T(8,128)(2,1)} %get-tuple-element.77.refs_12_), channel_id=1, source_target_pairs={{0,16},{16,0},{1,17},{17,1},{2,18},{18,2},{3,19},{19,3},{4,20},{20... | collective-permute-start | bytes 1769480 | tf_op jit(solution)/shard_map/ppermute | solution.py:1003
  26.7 54.1 %collective-permute-start.8 = (bf16[384,1536]{1,0:T(8,128)(2,1)S(1)}, bf16[384,1536]{1,0:T(8,128)(2,1)S(1)}, u32[]{:S(2)}, u32[]{:S(2)}) collective-permute-start(bf16[384,1536]{1,0:T(8,128)(2,1)S(1)} %copy-done.20), channel_id=1, source_target_pairs={{0,16},{16,0},{1,17},{17,1},{2,18},{18,2},{3,19},{19,3},{4,20},{20... | collective-permute-start | bytes 3538952 | tf_op jit(solution)/shard_map/ppermute | solution.py:1003
  57.6 25.6 %copy-start.19 = (bf16[16,24,1024]{2,1,0:T(8,128)(2,1)}, bf16[16,24,1024]{2,1,0:T(8,128)(2,1)S(1)}, u32[]{:S(2)}) copy-start(bf16[16,24,1024]{2,1,0:T(8,128)(2,1)S(1)} %all-to-all-done.refs_5_) | copy-start | bytes 2359300
  57.6 6.1 %collective-permute-start.2 = (bf16[1,24,768]{2,1,0:T(8,128)(2,1)}, bf16[1,24,768]{2,1,0:T(8,128)(2,1)S(1)}, u32[]{:S(2)}, u32[]{:S(2)}) collective-permute-start(bf16[1,24,768]{2,1,0:T(8,128)(2,1)} %bitcast.15), channel_id=1, source_target_pairs={{0,12},{1,13},{2,14},{3,15},{4,8},{5,9},{6,10},{7,11},{8,4},{9,5},... | collective-permute-start | bytes 110600 | tf_op jit(solution)/shard_map/ppermute | solution.py:1003
  61.4 5.1 %collective-permute-start.1 = (bf16[1,24,768]{2,1,0:T(8,128)(2,1)}, bf16[1,24,768]{2,1,0:T(8,128)(2,1)S(1)}, u32[]{:S(2)}, u32[]{:S(2)}) collective-permute-start(bf16[1,24,768]{2,1,0:T(8,128)(2,1)} %bitcast.16), channel_id=1, source_target_pairs={{0,8},{1,9},{2,10},{3,11},{4,12},{5,13},{6,14},{7,15},{8,0},{9,1},... | collective-permute-start | bytes 110600 | tf_op jit(solution)/shard_map/ppermute | solution.py:1003
  61.4 5.1 %collective-permute-start = (bf16[1,24,768]{2,1,0:T(8,128)(2,1)}, bf16[1,24,768]{2,1,0:T(8,128)(2,1)S(1)}, u32[]{:S(2)}, u32[]{:S(2)}) collective-permute-start(bf16[1,24,768]{2,1,0:T(8,128)(2,1)} %bitcast.17), channel_id=1, source_target_pairs={{0,4},{1,5},{2,6},{3,7},{4,0},{5,1},{6,2},{7,3},{8,12},{9,13},{10,... | collective-permute-start | bytes 110600 | tf_op jit(solution)/shard_map/ppermute | solution.py:1003
  63.7 18.4 %collective-permute-start.7 = (bf16[16,24,1024]{2,1,0:T(8,128)(2,1)S(1)}, bf16[16,24,1024]{2,1,0:T(8,128)(2,1)S(1)}, u32[]{:S(2)}, u32[]{:S(2)}) collective-permute-start(bf16[16,24,1024]{2,1,0:T(8,128)(2,1)S(1)} %all-to-all-done.refs_5_), channel_id=1, source_target_pairs={{0,16},{16,0},{1,17},{17,1},{2,18},{18,2},{3,19},{19,3},{4,20},{20... | collective-permute-start | bytes 2359304 | tf_op jit(solution)/shard_map/ppermute | solution.py:1003
  67.3 16.0 %copy-start.27 = (bf16[4,24,768]{2,1,0:T(8,128)(2,1)}, bf16[4,24,768]{2,1,0:T(8,128)(2,1)S(1)}, u32[]{:S(2)}) copy-start(bf16[4,24,768]{2,1,0:T(8,128)(2,1)S(1)} %pad_maximum_fusion.1.refs_0_) | copy-start | bytes 442372
  67.3 8.2 %collective-permute-start.4 = (bf16[4,24,768]{2,1,0:T(8,128)(2,1)S(1)}, bf16[4,24,768]{2,1,0:T(8,128)(2,1)S(1)}, u32[]{:S(2)}, u32[]{:S(2)}) collective-permute-start(bf16[4,24,768]{2,1,0:T(8,128)(2,1)S(1)} %pad_maximum_fusion.1.refs_0_), channel_id=1, source_target_pairs={{0,2},{1,3},{2,0},{3,1},{4,6},{5,7},{6,4},{7,5},{8,10},{9,11},{10,... | collective-permute-start | bytes 442376 | tf_op jit(solution)/shard_map/ppermute | solution.py:1003
  68.8 5.1 %collective-permute-start.3 = (bf16[4,24,768]{2,1,0:T(8,128)(2,1)S(1)}, bf16[4,24,768]{2,1,0:T(8,128)(2,1)S(1)}, u32[]{:S(2)}, u32[]{:S(2)}) collective-permute-start(bf16[4,24,768]{2,1,0:T(8,128)(2,1)S(1)} %pad_maximum_fusion.1.refs_0_), channel_id=1, source_target_pairs={{0,1},{1,0},{2,3},{3,2},{4,5},{5,4},{6,7},{7,6},{8,9},{9,8},{10,11... | collective-permute-start | bytes 442376 | tf_op jit(solution)/shard_map/ppermute | solution.py:1003
  74.0 9.3 %copy-start.29 = (bf16[4,24,768]{2,1,0:T(8,128)(2,1)}, bf16[4,24,768]{2,1,0:T(8,128)(2,1)S(1)}, u32[]{:S(2)}) copy-start(bf16[4,24,768]{2,1,0:T(8,128)(2,1)S(1)} %collective-permute-done.3.refs_1_) | copy-start | bytes 442372
  74.0 6.0 %collective-permute-start.5 = (bf16[4,24,768]{2,1,0:T(8,128)(2,1)S(1)}, bf16[4,24,768]{2,1,0:T(8,128)(2,1)S(1)}, u32[]{:S(2)}, u32[]{:S(2)}) collective-permute-start(bf16[4,24,768]{2,1,0:T(8,128)(2,1)S(1)} %pad_maximum_fusion.1.refs_0_), channel_id=1, source_target_pairs={{0,3},{1,2},{2,1},{3,0},{4,7},{5,6},{6,5},{7,4},{8,11},{9,10},{10,... | collective-permute-start | bytes 442376 | tf_op jit(solution)/shard_map/ppermute | solution.py:1003
  80.0 2.1 %collective-permute-start.6 = (bf16[16,24,768]{2,1,0:T(8,128)(2,1)S(1)}, bf16[16,24,768]{2,1,0:T(8,128)(2,1)S(1)}, u32[]{:S(2)}, u32[]{:S(2)}) collective-permute-start(bf16[16,24,768]{2,1,0:T(8,128)(2,1)S(1)} %constant_dynamic-update-slice_fusion), channel_id=1, source_target_pairs={{0,16},{16,0},{1,17},{17,1},{2,18},{18,2},{3,19},{19,3},{4,20},{20... | collective-permute-start | bytes 1769480 | tf_op jit(solution)/shard_map/ppermute | solution.py:1003
  100.1 21.0 %collective-permute-start.10 = (bf16[384,768]{1,0:T(8,128)(2,1)}, bf16[384,768]{1,0:T(8,128)(2,1)S(1)}, u32[]{:S(2)}, u32[]{:S(2)}) collective-permute-start(bf16[384,768]{1,0:T(8,128)(2,1)} %get-tuple-element.91), channel_id=1, source_target_pairs={{0,1},{1,0},{2,3},{3,2},{4,5},{5,4},{6,7},{7,6},{8,9},{9,8},{10,11... | collective-permute-start | bytes 1769480 | tf_op jit(solution)/shard_map/ppermute | solution.py:1003
  101.6 19.5 %collective-permute-start.11 = (bf16[384,768]{1,0:T(8,128)(2,1)}, bf16[384,768]{1,0:T(8,128)(2,1)S(1)}, u32[]{:S(2)}, u32[]{:S(2)}) collective-permute-start(bf16[384,768]{1,0:T(8,128)(2,1)} %get-tuple-element.93), channel_id=1, source_target_pairs={{0,2},{1,3},{2,0},{3,1},{4,6},{5,7},{6,4},{7,5},{8,10},{9,11},{10,... | collective-permute-start | bytes 1769480 | tf_op jit(solution)/shard_map/ppermute | solution.py:1003
  136.0 11.0 %collective-permute-start.13 = (bf16[2,384,896]{2,1,0:T(8,128)(2,1)}, bf16[2,384,896]{2,1,0:T(8,128)(2,1)S(1)}, u32[]{:S(2)}, u32[]{:S(2)}) collective-permute-start(bf16[2,384,896]{2,1,0:T(8,128)(2,1)} %get-tuple-element.97), channel_id=1, source_target_pairs={{0,16},{16,0},{1,17},{17,1},{2,18},{18,2},{3,19},{19,3},{4,20},{20... | collective-permute-start | bytes 4128776 | tf_op jit(solution)/shard_map/ppermute | solution.py:1003
  136.1 10.9 %collective-permute-start.12 = (bf16[2,384,768]{2,1,0:T(8,128)(2,1)}, bf16[2,384,768]{2,1,0:T(8,128)(2,1)S(1)}, u32[]{:S(2)}, u32[]{:S(2)}) collective-permute-start(bf16[2,384,768]{2,1,0:T(8,128)(2,1)} %get-tuple-element.95), channel_id=1, source_target_pairs={{0,16},{16,0},{1,17},{17,1},{2,18},{18,2},{3,19},{19,3},{4,20},{20... | collective-permute-start | bytes 3538952 | tf_op jit(solution)/shard_map/ppermute | solution.py:1003
  136.6 9.2 %collective-permute-start.14 = (bf16[192,768]{1,0:T(8,128)(2,1)}, bf16[192,768]{1,0:T(8,128)(2,1)S(1)}, u32[]{:S(2)}, u32[]{:S(2)}) collective-permute-start(bf16[192,768]{1,0:T(8,128)(2,1)} %get-tuple-element.98), channel_id=1, source_target_pairs={{0,2},{1,3},{2,0},{3,1},{4,6},{5,7},{6,4},{7,5},{8,10},{9,11},{10,... | collective-permute-start | bytes 884744 | tf_op jit(solution)/shard_map/ppermute | solution.py:1003
  138.1 8.9 %collective-permute-start.15 = (bf16[192,768]{1,0:T(8,128)(2,1)}, bf16[192,768]{1,0:T(8,128)(2,1)S(1)}, u32[]{:S(2)}, u32[]{:S(2)}) collective-permute-start(bf16[192,768]{1,0:T(8,128)(2,1)} %get-tuple-element.99), channel_id=1, source_target_pairs={{0,1},{1,0},{2,3},{3,2},{4,5},{5,4},{6,7},{7,6},{8,9},{9,8},{10,11... | collective-permute-start | bytes 884744 | tf_op jit(solution)/shard_map/ppermute | solution.py:1003
  151.7 16.6 %collective-permute-start.18 = (bf16[384,896]{1,0:T(8,128)(2,1)}, bf16[384,896]{1,0:T(8,128)(2,1)}, u32[]{:S(2)}, u32[]{:S(2)}) collective-permute-start(bf16[384,896]{1,0:T(8,128)(2,1)} %get-tuple-element.100.order_any.rest_0_), channel_id=1, source_target_pairs={{0,2},{1,3},{2,0},{3,1},{4,6},{5,7},{6,4},{7,5},{8,10},{9,11},{10,... | collective-permute-start | bytes 2064392 | tf_op jit(solution)/shard_map/ppermute | solution.py:1003
  152.4 15.2 %collective-permute-start.17 = (bf16[384,768]{1,0:T(8,128)(2,1)}, bf16[384,768]{1,0:T(8,128)(2,1)S(1)}, u32[]{:S(2)}, u32[]{:S(2)}) collective-permute-start(bf16[384,768]{1,0:T(8,128)(2,1)} %get-tuple-element.103), channel_id=1, source_target_pairs={{0,1},{1,0},{2,3},{3,2},{4,5},{5,4},{6,7},{7,6},{8,9},{9,8},{10,11... | collective-permute-start | bytes 1769480 | tf_op jit(solution)/shard_map/ppermute | solution.py:1003
  156.1 17.4 %collective-permute-start.21 = (bf16[48,1536]{1,0:T(8,128)(2,1)S(1)}, bf16[48,1536]{1,0:T(8,128)(2,1)S(1)}, u32[]{:S(2)}, u32[]{:S(2)}) collective-permute-start(bf16[48,1536]{1,0:T(8,128)(2,1)S(1)} %get-tuple-element.110), channel_id=1, source_target_pairs={{0,4},{1,5},{2,6},{3,7},{4,0},{5,1},{6,2},{7,3},{8,12},{9,13},{10,... | collective-permute-start | bytes 442376 | tf_op jit(solution)/shard_map/ppermute | solution.py:1003
  156.3 18.6 %collective-permute-start.22 = (bf16[48,1536]{1,0:T(8,128)(2,1)S(1)}, bf16[48,1536]{1,0:T(8,128)(2,1)S(1)}, u32[]{:S(2)}, u32[]{:S(2)}) collective-permute-start(bf16[48,1536]{1,0:T(8,128)(2,1)S(1)} %get-tuple-element.111), channel_id=1, source_target_pairs={{0,8},{1,9},{2,10},{3,11},{4,12},{5,13},{6,14},{7,15},{8,0},{9,1},... | collective-permute-start | bytes 442376 | tf_op jit(solution)/shard_map/ppermute | solution.py:1003
  158.7 16.1 %collective-permute-start.23 = (bf16[48,1536]{1,0:T(8,128)(2,1)S(1)}, bf16[48,1536]{1,0:T(8,128)(2,1)S(1)}, u32[]{:S(2)}, u32[]{:S(2)}) collective-permute-start(bf16[48,1536]{1,0:T(8,128)(2,1)S(1)} %get-tuple-element.112), channel_id=1, source_target_pairs={{0,12},{1,13},{2,14},{3,15},{4,8},{5,9},{6,10},{7,11},{8,4},{9,5},... | collective-permute-start | bytes 442376 | tf_op jit(solution)/shard_map/ppermute | solution.py:1003
  167.5 8.1 %collective-permute-start.16 = (bf16[24,8,768]{2,1,0:T(8,128)(2,1)}, bf16[24,8,768]{2,1,0:T(8,128)(2,1)S(1)}, u32[]{:S(2)}, u32[]{:S(2)}) collective-permute-start(bf16[24,8,768]{2,1,0:T(8,128)(2,1)} %get-tuple-element.102), channel_id=1, source_target_pairs={{0,16},{16,0},{1,17},{17,1},{2,18},{18,2},{3,19},{19,3},{4,20},{20... | collective-permute-start | bytes 884744 | tf_op jit(solution)/shard_map/ppermute | solution.py:1003
  171.9 8.9 %collective-permute-start.19 = (bf16[192,768]{1,0:T(8,128)(2,1)}, bf16[192,768]{1,0:T(8,128)(2,1)S(1)}, u32[]{:S(2)}, u32[]{:S(2)}) collective-permute-start(bf16[192,768]{1,0:T(8,128)(2,1)} %get-tuple-element.106), channel_id=1, source_target_pairs={{0,2},{1,3},{2,0},{3,1},{4,6},{5,7},{6,4},{7,5},{8,10},{9,11},{10,... | collective-permute-start | bytes 884744 | tf_op jit(solution)/shard_map/ppermute | solution.py:1003
  173.4 9.7 %collective-permute-start.20 = (bf16[192,896]{1,0:T(8,128)(2,1)}, bf16[192,896]{1,0:T(8,128)(2,1)S(1)}, u32[]{:S(2)}, u32[]{:S(2)}) collective-permute-start(bf16[192,896]{1,0:T(8,128)(2,1)} %get-tuple-element.107), channel_id=1, source_target_pairs={{0,1},{1,0},{2,3},{3,2},{4,5},{5,4},{6,7},{7,6},{8,9},{9,8},{10,11... | collective-permute-start | bytes 1032200 | tf_op jit(solution)/shard_map/ppermute | solution.py:1003
  183.3 12.6 %collective-permute-start.24 = (bf16[48,1664]{1,0:T(8,128)(2,1)S(1)}, bf16[48,1664]{1,0:T(8,128)(2,1)S(1)}, u32[]{:S(2)}, u32[]{:S(2)}) collective-permute-start(bf16[48,1664]{1,0:T(8,128)(2,1)S(1)} %get-tuple-element.114), channel_id=1, source_target_pairs={{0,4},{1,5},{2,6},{3,7},{4,0},{5,1},{6,2},{7,3},{8,12},{9,13},{10,... | collective-permute-start | bytes 479240 | tf_op jit(solution)/shard_map/ppermute | solution.py:1003
  183.3 13.8 %collective-permute-start.25 = (bf16[48,1664]{1,0:T(8,128)(2,1)S(1)}, bf16[48,1664]{1,0:T(8,128)(2,1)S(1)}, u32[]{:S(2)}, u32[]{:S(2)}) collective-permute-start(bf16[48,1664]{1,0:T(8,128)(2,1)S(1)} %get-tuple-element.115), channel_id=1, source_target_pairs={{0,8},{1,9},{2,10},{3,11},{4,12},{5,13},{6,14},{7,15},{8,0},{9,1},... | collective-permute-start | bytes 479240 | tf_op jit(solution)/shard_map/ppermute | solution.py:1003
  186.0 11.2 %collective-permute-start.26 = (bf16[48,1664]{1,0:T(8,128)(2,1)S(1)}, bf16[48,1664]{1,0:T(8,128)(2,1)S(1)}, u32[]{:S(2)}, u32[]{:S(2)}) collective-permute-start(bf16[48,1664]{1,0:T(8,128)(2,1)S(1)} %get-tuple-element.116), channel_id=1, source_target_pairs={{0,12},{1,13},{2,14},{3,15},{4,8},{5,9},{6,10},{7,11},{8,4},{9,5},... | collective-permute-start | bytes 479240 | tf_op jit(solution)/shard_map/ppermute | solution.py:1003
  (27 other events, 80.6 us)

commit v2 on v1

--- a/solution.py
+++ b/solution.py
@@ -319,7 +319,7 @@
             av[rows, lanes] = attend(q2, k2, v2, bias, masks)
         return carry
 
-    lax.fori_loop(0, caps // 2, attention, 0, unroll=2)
+    lax.fori_loop(0, caps // 2, attention, 0, unroll=4)
     load_p.wait()
     pb[...] = row(biases, 4)
 
@@ -347,7 +347,7 @@
         msum[pl.ds(pl.multiple_of(j * 8, 8), 8), :] = token_sum(m, 8)
         return carry
 
-    lax.fori_loop(0, caps // 8, second_norm, 0)
+    lax.fori_loop(0, caps // 8, second_norm, 0, unroll=3)
     load_e.wait()
 
     def feed(j, carry):
@@ -356,7 +356,7 @@
         gsum[:, cols] = token_sum(f * normal_cdf(f), caps)
         return carry
 
-    lax.fori_loop(0, hidden // 256, feed, 0, unroll=2)
+    lax.fori_loop(0, hidden // 256, feed, 0, unroll=3)
     load_r.wait()
     scale = 1.0 / length
     pooled = msum[...] * scale + split_dot(gsum[...] * scale, wr[...]) + row(biases, 5)
@@ -1095,10 +1095,11 @@
     total = pairs * chips
     row_blocks = 16
     order = np.array(slot_reaches(chips))
-    slot_of = np.zeros(chips, np.int32)
-    slot_of[order] = np.arange(chips)
-    table = np.stack([slot_of[np.arange(chips) ^ i] for i in range(chips)]).astype(np.int32)
-    slots = lax.dynamic_slice_in_dim(jnp.asarray(table), d, 1, 0)[0]
+    away = jnp.arange(chips, dtype=jnp.int32) ^ d
+    slots, stride = jnp.zeros(chips, jnp.int32), 1
+    for group in bit_groups(chips):
+        slots = slots + ((away >> (group[0].bit_length() - 1)) & (len(reaches(group)) - 1)) * stride
+        stride *= len(reaches(group))
     relative = chips == row_blocks
     row_slots = slots if relative else jnp.arange(row_blocks, dtype=jnp.int32)
     head = jnp.stack([t, d, tallies[0], t]).astype(jnp.int32)

time: 200 us -> 197 us (0.985)
  Pallas kernels: 117 us -> 115 us
where the time goes in v2:
time: 197 us; the launch traced here: 196 us
  Pallas kernels  115 us (58%)
  starting transfers between devices  35.8 us (18%)
  waiting for transfers between devices  30.8 us (16%)
  local copies, waits for them, and re-layouts  9.22 us (5%)
  other arithmetic  2.74 us (1%)
  between operations  2.34 us (1%)
    pallas_call x12, Pallas kernels, call(): pl.pallas_call(kernel, name=name, in_specs=in_specs, out_shape=[jax.Shape...  115 us
    ppermute x27, waiting for transfers between devices, xor_permute(): lax.ppermute(x, axis, [(i, i ^ bit) for i in range(lax.axis_size(axis))])  30.8 us
    ppermute x27, starting transfers between devices, xor_permute(): lax.ppermute(x, axis, [(i, i ^ bit) for i in range(lax.axis_size(axis))])  27.3 us
    unnamed x68, local copies, waits for them, and re-layouts  8.61 us
    all_to_all x1, starting transfers between devices, body(): text_all = lax.all_to_all(text_send, 'dp', 0, 0, tiled=True)  8.46 us
  transfers between devices with their start and end apart: 28, of which 11 were waited for; matrix products, arithmetic and copies ran while one was open for 2% of the time, Pallas kernels for 33%

profile of v2, /device:TPU:0, one launch (start us, length us, event | category | flops | bytes accessed | tf_op | source)
XLA Modules:
  0.0 196.0 jit_solution(9788337424825998488)
XLA Ops:
  1.9 15.5 %text_forward.1 = (bf16[16,48,384]{2,1,0:T(8,128)(2,1)}, bf16[384,2304]{1,0:T(8,128)(2,1)}, bf16[16,48,384]{2,1,0:T(8,128)(2,1)}, f32[384,768]{1,0:T(8,128)}, bf...) custom-call(s32[36]{0:T(128)} %concatenate.13.scal, ...), custom_call_target="tpu_custom_call" | custom-call | flops 3623878656 | bytes 20000000 | tf_op jit(solution)/shard_map/text_forward/pallas_call | solution.py:1070
  17.4 8.5 %all-to-all-start = ((bf16[16,24,1024]{2,1,0:T(8,128)(2,1)}), bf16[16,24,1024]{2,1,0:T(8,128)(2,1)S(1)}, u32[]{:S(2)}, u32[]{:S(2)}) async-start(bf16[16,24,1024]{2,1,0:T(8,128)(2,1)} %get-tuple-element.70), calls=%async_computation | async-start | bytes 1572864 | tf_op jit(solution)/shard_map/all_to_all | solution.py:1133
  26.5 28.5 %image_forward.1 = bf16[24,768]{1,0:T(8,128)(2,1)} custom-call(s32[36]{0:T(128)} %concatenate.13.scal, bf16[50,48,768]{2,1,0:T(8,128)(2,1)} %bitcast.18, bf16[2,768]{1,0:T(2,128)(2,1)} %gains.5, bf16[6,768]{1,0:T(8,128)(2,1)} %biases.3, bf16[24,128]{1,0:T(8,128)(2,1)} %bitcast.19, bf16[768,2304]{1,0:T(8,128)(2,1)} %wq_any.4, bf16[768,768]{1,0:T(8,128)(2,1)} %wp_any.3, ...), custom_call_target="tpu_custom_call" | custom-call | flops 12683575296 | bytes 20000000 | tf_op jit(solution)/shard_map/image_forward/pallas_call | solution.py:1070
  55.0 3.8 %collective-permute-start.2 = (bf16[1,24,768]{2,1,0:T(8,128)(2,1)}, bf16[1,24,768]{2,1,0:T(8,128)(2,1)S(1)}, u32[]{:S(2)}, u32[]{:S(2)}) collective-permute-start(bf16[1,24,768]{2,1,0:T(8,128)(2,1)} %bitcast.13), channel_id=1, source_target_pairs={{0,12},{1,13},{2,14},{3,15},{4,8},{5,9},{6,10},{7,11},{8,4},{9,5},... | collective-permute-start | bytes 110600 | tf_op jit(solution)/shard_map/ppermute | solution.py:1003
  61.1 2.8 %collective-permute-done.1 = bf16[1,24,768]{2,1,0:T(8,128)(2,1)S(1)} collective-permute-done((bf16[1,24,768]{2,1,0:T(8,128)(2,1)}, bf16[1,24,768]{2,1,0:T(8,128)(2,1)S(1)}, u32[]{:S(2)}, u32[]{:S(2)}) %collective-permute-start.1) | collective-permute-done | bytes 36896 | tf_op jit(solution)/shard_map/ppermute | solution.py:1003
  64.7 1.5 collective-permute-start.4
  66.2 1.5 collective-permute-start.3
  67.7 3.7 %collective-permute-done.3.refs_1_ = bf16[4,24,768]{2,1,0:T(8,128)(2,1)S(1)} collective-permute-done((bf16[4,24,768]{2,1,0:T(8,128)(2,1)S(1)}, bf16[4,24,768]{2,1,0:T(8,128)(2,1)S(1)}, u32[]{:S(2)}, u32[]{:S(2)}) %collective-permute-start.3) | collective-permute-done | bytes 147488 | tf_op jit(solution)/shard_map/ppermute | solution.py:1003
  71.3 1.5 collective-permute-start.5
  72.9 4.5 %collective-permute-done.5.refs_3_ = bf16[4,24,768]{2,1,0:T(8,128)(2,1)S(1)} collective-permute-done((bf16[4,24,768]{2,1,0:T(8,128)(2,1)S(1)}, bf16[4,24,768]{2,1,0:T(8,128)(2,1)S(1)}, u32[]{:S(2)}, u32[]{:S(2)}) %collective-permute-start.5) | collective-permute-done | bytes 147488 | tf_op jit(solution)/shard_map/ppermute | solution.py:1003
  78.2 1.3 collective-permute-done.6.refs_4_
  80.6 16.8 %loss.1 = (f32[1,1]{1,0:T(1,128)}, f32[1,1]{1,0:T(1,128)}, bf16[384,768]{1,0:T(8,128)(2,1)}, bf16[384,768]{1,0:T(8,128)(2,1)}, bf16[384,768]{1,0:T(8,128)(2,1)},...) custom-call(s32[36]{0:T(128)} %concatenate.13.scal, ...), custom_call_target="tpu_custom_call" | custom-call | flops 2717908992 | bytes 20000000 | tf_op jit(solution)/shard_map/loss/pallas_call | solution.py:1070
  97.5 1.5 collective-permute-start.10
  99.6 18.9 %middle_back.1 = (f32[384,768]{1,0:T(8,128)}, bf16[384,2304]{1,0:T(8,128)(2,1)}, f32[8,768]{1,0:T(8,128)}) custom-call(s32[36]{0:T(128)} %concatenate.13.scal, f32[384,768]{1,0:T(8,128)} %get-tuple-element.80.dc_any, f32[24,768]{1,0:T(8,128)} %get-tuple-element.81.dy, bf16[384,1536]{1,0:T(8,128)(2,1)} %get-tuple-element.76.gps_any, ...), custom_call_target="tpu_custom_call" | custom-call | flops 3623878656 | bytes 20000000 | tf_op jit(solution)/shard_map/middle_back/pallas_call | solution.py:1070
  119.6 13.8 %weight_grad.1 = (bf16[2,384,768]{2,1,0:T(8,128)(2,1)}, bf16[2,384,896]{2,1,0:T(8,128)(2,1)}, bf16[2,384,768]{2,1,0:T(8,128)(2,1)}, bf16[2,384,896]{2,1,0:T(8,12...) custom-call(s32[36]{0:T(128)} %concatenate.13.scal, ...), custom_call_target="tpu_custom_call" | custom-call | flops 1811939328 | bytes 20000000 | tf_op jit(solution)/shard_map/weight_grad/pallas_call | solution.py:1070
  134.0 1.5 collective-permute-start.14
  136.0 7.2 %collective-permute-done.14.far_a.hop_a = bf16[192,768]{1,0:T(8,128)(2,1)S(1)} collective-permute-done((bf16[192,768]{1,0:T(8,128)(2,1)}, bf16[192,768]{1,0:T(8,128)(2,1)S(1)}, u32[]{:S(2)}, u32[]{:S(2)}) %collective-permute-start.14) | collective-permute-done | bytes 294944 | tf_op jit(solution)/shard_map/ppermute | solution.py:1003
  143.2 1.2 collective-permute-done.15.far_b.hop_b
  146.0 3.1 %wire.1 = (bf16[384,768]{1,0:T(8,128)(2,1)}, bf16[384,896]{1,0:T(8,128)(2,1)}) custom-call(bf16[2,384,768]{2,1,0:T(8,128)(2,1)} %get-tuple-element.94.qa.refs_0_, bf16[2,384,768]{2,1,0:T(8,128)(2,1)} %copy-done.18, bf16[2,384,896]{2,1,0:T(8,128)(2,1)} %get-tuple-element.96.qb.refs_3_, bf16[2,384,896]{2,1,0:T(8,128)(2,1)} %copy-done.17, ...), custom_call_target="tpu_custom_call" | custom-call | flops 1000000 | bytes 4000000 | tf_op jit(solution)/shard_map/wire/pallas_call | solution.py:1070
  153.7 2.4 %collective-permute-start.22 = (bf16[48,1536]{1,0:T(8,128)(2,1)S(1)}, bf16[48,1536]{1,0:T(8,128)(2,1)S(1)}, u32[]{:S(2)}, u32[]{:S(2)}) collective-permute-start(bf16[48,1536]{1,0:T(8,128)(2,1)S(1)} %get-tuple-element.111), channel_id=1, source_target_pairs={{0,8},{1,9},{2,10},{3,11},{4,12},{5,13},{6,14},{7,15},{8,0},{9,1},... | collective-permute-start | bytes 442376 | tf_op jit(solution)/shard_map/ppermute | solution.py:1003
  156.1 1.8 collective-permute-start.23
  157.9 7.0 %input_back.1 = (f32[24,8,768]{2,1,0:T(8,128)}, bf16[24,8,768]{2,1,0:T(8,128)(2,1)}) custom-call(s32[36]{0:T(128)} %concatenate.13.scal, f32[384,768]{1,0:T(8,128)} %get-tuple-element.84.dm_any, bf16[768,768]{1,0:T(8,128)(2,1)} %bitcast.12, bf16[2,768]{1,0:T(2,128)(2,1)} %gains.9, bf16[384,2304]{1,0:T(8,128)(2,1)} %get-tuple-element.85.dqkv_any, ...), custom_call_target="tpu_custom_call" | custom-call | flops 1358954496 | bytes 9000000 | tf_op jit(solution)/shard_map/input_back/pallas_call | solution.py:1070
  165.8 3.5 %turn_qkv.1 = (f32[192,768]{1,0:T(8,128)}, f32[192,832]{1,0:T(8,128)}, bf16[192,768]{1,0:T(8,128)(2,1)}, bf16[192,896]{1,0:T(8,128)(2,1)}) custom-call(bf16[2,384,768]{2,1,0:T(8,128)(2,1)} %get-tuple-element.94.qa.refs_0_, bf16[2,384,768]{2,1,0:T(8,128)(2,1)} %copy-done.18, bf16[384,768]{1,0:T(8,128)(2,1)} %copy-done.1, ...), custom_call_target="tpu_custom_call" | custom-call | flops 1000000 | bytes 4000000 | tf_op jit(solution)/shard_map/turn_qkv/pallas_call | solution.py:1070
  169.3 1.5 collective-permute-start.19
  170.8 1.5 collective-permute-start.20
  173.1 5.1 %collective-permute-done.19.hop_a = bf16[192,768]{1,0:T(8,128)(2,1)S(1)} collective-permute-done((bf16[192,768]{1,0:T(8,128)(2,1)}, bf16[192,768]{1,0:T(8,128)(2,1)S(1)}, u32[]{:S(2)}, u32[]{:S(2)}) %collective-permute-start.19) | collective-permute-done | bytes 294944 | tf_op jit(solution)/shard_map/ppermute | solution.py:1003
  178.2 2.2 %collective-permute-done.20.hop_b = bf16[192,896]{1,0:T(8,128)(2,1)S(1)} collective-permute-done((bf16[192,896]{1,0:T(8,128)(2,1)}, bf16[192,896]{1,0:T(8,128)(2,1)S(1)}, u32[]{:S(2)}, u32[]{:S(2)}) %collective-permute-start.20) | collective-permute-done | bytes 344096 | tf_op jit(solution)/shard_map/ppermute | solution.py:1003
  180.7 2.6 %collective-permute-start.25 = (bf16[48,1664]{1,0:T(8,128)(2,1)S(1)}, bf16[48,1664]{1,0:T(8,128)(2,1)S(1)}, u32[]{:S(2)}, u32[]{:S(2)}) collective-permute-start(bf16[48,1664]{1,0:T(8,128)(2,1)S(1)} %get-tuple-element.115), channel_id=1, source_target_pairs={{0,8},{1,9},{2,10},{3,11},{4,12},{5,13},{6,14},{7,15},{8,0},{9,1},... | collective-permute-start | bytes 479240 | tf_op jit(solution)/shard_map/ppermute | solution.py:1003
  183.3 1.8 collective-permute-start.26
  187.1 6.1 %reduce_grad.1 = (f32[96,768]{1,0:T(8,128)}, f32[8,768]{1,0:T(8,128)S(1)}) custom-call(f32[1]{0:T(128)S(6)} %copy.35.refs_7_.expo, bf16[768,768]{1,0:T(8,128)(2,1)S(1)} %copy-done.7, bf16[768,768]{1,0:T(8,128)(2,1)S(1)} %copy-done.8, bf16[768,768]{1,0:T(8,128)(2,1)S(1)} %copy-done.9, bf16[768,128]{1,0:T(8,128)(2,1)S(1)} %copy-done.15, ...), custom_call_target="tpu_custom_call" | custom-call | flops 905969664 | bytes 6000000 | tf_op jit(solution)/shard_map/reduce_grad/pallas_call | solution.py:1070
  193.2 1.3 collective-permute-done.25.hop_2
  194.5 1.5 finish.1
  (111 shorter events, 18.4 us)
Async XLA Ops:
  17.4 8.6 %copy-start.20 = (bf16[384,1536]{1,0:T(8,128)(2,1)S(1)}, bf16[384,1536]{1,0:T(8,128)(2,1)}, u32[]{:S(2)}) copy-start(bf16[384,1536]{1,0:T(8,128)(2,1)} %get-tuple-element.76.gps_any) | copy-start | bytes 3538948
  17.4 37.5 %all-to-all-start = ((bf16[16,24,1024]{2,1,0:T(8,128)(2,1)}), bf16[16,24,1024]{2,1,0:T(8,128)(2,1)S(1)}, u32[]{:S(2)}, u32[]{:S(2)}) async-start(bf16[16,24,1024]{2,1,0:T(8,128)(2,1)} %get-tuple-element.70), calls=%async_computation | async-start | bytes 1572864 | tf_op jit(solution)/shard_map/all_to_all | solution.py:1133
  25.9 52.2 %collective-permute-start.9 = (bf16[16,48,384]{2,1,0:T(8,128)(2,1)}, bf16[16,48,384]{2,1,0:T(8,128)(2,1)}, u32[]{:S(2)}, u32[]{:S(2)}) collective-permute-start(bf16[16,48,384]{2,1,0:T(8,128)(2,1)} %get-tuple-element.77.refs_12_), channel_id=1, source_target_pairs={{0,16},{16,0},{1,17},{17,1},{2,18},{18,2},{3,19},{19,3},{4,20},{20... | collective-permute-start | bytes 1769480 | tf_op jit(solution)/shard_map/ppermute | solution.py:1003
  26.0 52.1 %collective-permute-start.8 = (bf16[384,1536]{1,0:T(8,128)(2,1)S(1)}, bf16[384,1536]{1,0:T(8,128)(2,1)S(1)}, u32[]{:S(2)}, u32[]{:S(2)}) collective-permute-start(bf16[384,1536]{1,0:T(8,128)(2,1)S(1)} %copy-done.20), channel_id=1, source_target_pairs={{0,16},{16,0},{1,17},{17,1},{2,18},{18,2},{3,19},{19,3},{4,20},{20... | collective-permute-start | bytes 3538952 | tf_op jit(solution)/shard_map/ppermute | solution.py:1003
  55.0 25.6 %copy-start.19 = (bf16[16,24,1024]{2,1,0:T(8,128)(2,1)}, bf16[16,24,1024]{2,1,0:T(8,128)(2,1)S(1)}, u32[]{:S(2)}) copy-start(bf16[16,24,1024]{2,1,0:T(8,128)(2,1)S(1)} %all-to-all-done.refs_5_) | copy-start | bytes 2359300
  55.0 6.1 %collective-permute-start.2 = (bf16[1,24,768]{2,1,0:T(8,128)(2,1)}, bf16[1,24,768]{2,1,0:T(8,128)(2,1)S(1)}, u32[]{:S(2)}, u32[]{:S(2)}) collective-permute-start(bf16[1,24,768]{2,1,0:T(8,128)(2,1)} %bitcast.13), channel_id=1, source_target_pairs={{0,12},{1,13},{2,14},{3,15},{4,8},{5,9},{6,10},{7,11},{8,4},{9,5},... | collective-permute-start | bytes 110600 | tf_op jit(solution)/shard_map/ppermute | solution.py:1003
  58.8 5.1 %collective-permute-start.1 = (bf16[1,24,768]{2,1,0:T(8,128)(2,1)}, bf16[1,24,768]{2,1,0:T(8,128)(2,1)S(1)}, u32[]{:S(2)}, u32[]{:S(2)}) collective-permute-start(bf16[1,24,768]{2,1,0:T(8,128)(2,1)} %bitcast.14), channel_id=1, source_target_pairs={{0,8},{1,9},{2,10},{3,11},{4,12},{5,13},{6,14},{7,15},{8,0},{9,1},... | collective-permute-start | bytes 110600 | tf_op jit(solution)/shard_map/ppermute | solution.py:1003
  58.8 5.1 %collective-permute-start = (bf16[1,24,768]{2,1,0:T(8,128)(2,1)}, bf16[1,24,768]{2,1,0:T(8,128)(2,1)S(1)}, u32[]{:S(2)}, u32[]{:S(2)}) collective-permute-start(bf16[1,24,768]{2,1,0:T(8,128)(2,1)} %bitcast.15), channel_id=1, source_target_pairs={{0,4},{1,5},{2,6},{3,7},{4,0},{5,1},{6,2},{7,3},{8,12},{9,13},{10,... | collective-permute-start | bytes 110600 | tf_op jit(solution)/shard_map/ppermute | solution.py:1003
  61.1 18.4 %collective-permute-start.7 = (bf16[16,24,1024]{2,1,0:T(8,128)(2,1)S(1)}, bf16[16,24,1024]{2,1,0:T(8,128)(2,1)S(1)}, u32[]{:S(2)}, u32[]{:S(2)}) collective-permute-start(bf16[16,24,1024]{2,1,0:T(8,128)(2,1)S(1)} %all-to-all-done.refs_5_), channel_id=1, source_target_pairs={{0,16},{16,0},{1,17},{17,1},{2,18},{18,2},{3,19},{19,3},{4,20},{20... | collective-permute-start | bytes 2359304 | tf_op jit(solution)/shard_map/ppermute | solution.py:1003
  64.7 16.0 %copy-start.27 = (bf16[4,24,768]{2,1,0:T(8,128)(2,1)}, bf16[4,24,768]{2,1,0:T(8,128)(2,1)S(1)}, u32[]{:S(2)}) copy-start(bf16[4,24,768]{2,1,0:T(8,128)(2,1)S(1)} %pad_maximum_fusion.1.refs_0_) | copy-start | bytes 442372
  64.7 8.2 %collective-permute-start.4 = (bf16[4,24,768]{2,1,0:T(8,128)(2,1)S(1)}, bf16[4,24,768]{2,1,0:T(8,128)(2,1)S(1)}, u32[]{:S(2)}, u32[]{:S(2)}) collective-permute-start(bf16[4,24,768]{2,1,0:T(8,128)(2,1)S(1)} %pad_maximum_fusion.1.refs_0_), channel_id=1, source_target_pairs={{0,2},{1,3},{2,0},{3,1},{4,6},{5,7},{6,4},{7,5},{8,10},{9,11},{10,... | collective-permute-start | bytes 442376 | tf_op jit(solution)/shard_map/ppermute | solution.py:1003
  66.2 5.1 %collective-permute-start.3 = (bf16[4,24,768]{2,1,0:T(8,128)(2,1)S(1)}, bf16[4,24,768]{2,1,0:T(8,128)(2,1)S(1)}, u32[]{:S(2)}, u32[]{:S(2)}) collective-permute-start(bf16[4,24,768]{2,1,0:T(8,128)(2,1)S(1)} %pad_maximum_fusion.1.refs_0_), channel_id=1, source_target_pairs={{0,1},{1,0},{2,3},{3,2},{4,5},{5,4},{6,7},{7,6},{8,9},{9,8},{10,11... | collective-permute-start | bytes 442376 | tf_op jit(solution)/shard_map/ppermute | solution.py:1003
  71.3 9.3 %copy-start.29 = (bf16[4,24,768]{2,1,0:T(8,128)(2,1)}, bf16[4,24,768]{2,1,0:T(8,128)(2,1)S(1)}, u32[]{:S(2)}) copy-start(bf16[4,24,768]{2,1,0:T(8,128)(2,1)S(1)} %collective-permute-done.3.refs_1_) | copy-start | bytes 442372
  71.3 6.0 %collective-permute-start.5 = (bf16[4,24,768]{2,1,0:T(8,128)(2,1)S(1)}, bf16[4,24,768]{2,1,0:T(8,128)(2,1)S(1)}, u32[]{:S(2)}, u32[]{:S(2)}) collective-permute-start(bf16[4,24,768]{2,1,0:T(8,128)(2,1)S(1)} %pad_maximum_fusion.1.refs_0_), channel_id=1, source_target_pairs={{0,3},{1,2},{2,1},{3,0},{4,7},{5,6},{6,5},{7,4},{8,11},{9,10},{10,... | collective-permute-start | bytes 442376 | tf_op jit(solution)/shard_map/ppermute | solution.py:1003
  77.4 2.1 %collective-permute-start.6 = (bf16[16,24,768]{2,1,0:T(8,128)(2,1)S(1)}, bf16[16,24,768]{2,1,0:T(8,128)(2,1)S(1)}, u32[]{:S(2)}, u32[]{:S(2)}) collective-permute-start(bf16[16,24,768]{2,1,0:T(8,128)(2,1)S(1)} %constant_dynamic-update-slice_fusion), channel_id=1, source_target_pairs={{0,16},{16,0},{1,17},{17,1},{2,18},{18,2},{3,19},{19,3},{4,20},{20... | collective-permute-start | bytes 1769480 | tf_op jit(solution)/shard_map/ppermute | solution.py:1003
  97.5 21.0 %collective-permute-start.10 = (bf16[384,768]{1,0:T(8,128)(2,1)}, bf16[384,768]{1,0:T(8,128)(2,1)S(1)}, u32[]{:S(2)}, u32[]{:S(2)}) collective-permute-start(bf16[384,768]{1,0:T(8,128)(2,1)} %get-tuple-element.91), channel_id=1, source_target_pairs={{0,1},{1,0},{2,3},{3,2},{4,5},{5,4},{6,7},{7,6},{8,9},{9,8},{10,11... | collective-permute-start | bytes 1769480 | tf_op jit(solution)/shard_map/ppermute | solution.py:1003
  99.0 19.5 %collective-permute-start.11 = (bf16[384,768]{1,0:T(8,128)(2,1)}, bf16[384,768]{1,0:T(8,128)(2,1)S(1)}, u32[]{:S(2)}, u32[]{:S(2)}) collective-permute-start(bf16[384,768]{1,0:T(8,128)(2,1)} %get-tuple-element.93), channel_id=1, source_target_pairs={{0,2},{1,3},{2,0},{3,1},{4,6},{5,7},{6,4},{7,5},{8,10},{9,11},{10,... | collective-permute-start | bytes 1769480 | tf_op jit(solution)/shard_map/ppermute | solution.py:1003
  133.4 11.0 %collective-permute-start.13 = (bf16[2,384,896]{2,1,0:T(8,128)(2,1)}, bf16[2,384,896]{2,1,0:T(8,128)(2,1)S(1)}, u32[]{:S(2)}, u32[]{:S(2)}) collective-permute-start(bf16[2,384,896]{2,1,0:T(8,128)(2,1)} %get-tuple-element.97), channel_id=1, source_target_pairs={{0,16},{16,0},{1,17},{17,1},{2,18},{18,2},{3,19},{19,3},{4,20},{20... | collective-permute-start | bytes 4128776 | tf_op jit(solution)/shard_map/ppermute | solution.py:1003
  133.5 10.9 %collective-permute-start.12 = (bf16[2,384,768]{2,1,0:T(8,128)(2,1)}, bf16[2,384,768]{2,1,0:T(8,128)(2,1)S(1)}, u32[]{:S(2)}, u32[]{:S(2)}) collective-permute-start(bf16[2,384,768]{2,1,0:T(8,128)(2,1)} %get-tuple-element.95), channel_id=1, source_target_pairs={{0,16},{16,0},{1,17},{17,1},{2,18},{18,2},{3,19},{19,3},{4,20},{20... | collective-permute-start | bytes 3538952 | tf_op jit(solution)/shard_map/ppermute | solution.py:1003
  134.0 9.2 %collective-permute-start.14 = (bf16[192,768]{1,0:T(8,128)(2,1)}, bf16[192,768]{1,0:T(8,128)(2,1)S(1)}, u32[]{:S(2)}, u32[]{:S(2)}) collective-permute-start(bf16[192,768]{1,0:T(8,128)(2,1)} %get-tuple-element.98), channel_id=1, source_target_pairs={{0,2},{1,3},{2,0},{3,1},{4,6},{5,7},{6,4},{7,5},{8,10},{9,11},{10,... | collective-permute-start | bytes 884744 | tf_op jit(solution)/shard_map/ppermute | solution.py:1003
  135.4 8.9 %collective-permute-start.15 = (bf16[192,768]{1,0:T(8,128)(2,1)}, bf16[192,768]{1,0:T(8,128)(2,1)S(1)}, u32[]{:S(2)}, u32[]{:S(2)}) collective-permute-start(bf16[192,768]{1,0:T(8,128)(2,1)} %get-tuple-element.99), channel_id=1, source_target_pairs={{0,1},{1,0},{2,3},{3,2},{4,5},{5,4},{6,7},{7,6},{8,9},{9,8},{10,11... | collective-permute-start | bytes 884744 | tf_op jit(solution)/shard_map/ppermute | solution.py:1003
  149.1 16.6 %collective-permute-start.18 = (bf16[384,896]{1,0:T(8,128)(2,1)}, bf16[384,896]{1,0:T(8,128)(2,1)}, u32[]{:S(2)}, u32[]{:S(2)}) collective-permute-start(bf16[384,896]{1,0:T(8,128)(2,1)} %get-tuple-element.100.order_any.rest_0_), channel_id=1, source_target_pairs={{0,2},{1,3},{2,0},{3,1},{4,6},{5,7},{6,4},{7,5},{8,10},{9,11},{10,... | collective-permute-start | bytes 2064392 | tf_op jit(solution)/shard_map/ppermute | solution.py:1003
  149.7 15.2 %collective-permute-start.17 = (bf16[384,768]{1,0:T(8,128)(2,1)}, bf16[384,768]{1,0:T(8,128)(2,1)S(1)}, u32[]{:S(2)}, u32[]{:S(2)}) collective-permute-start(bf16[384,768]{1,0:T(8,128)(2,1)} %get-tuple-element.103), channel_id=1, source_target_pairs={{0,1},{1,0},{2,3},{3,2},{4,5},{5,4},{6,7},{7,6},{8,9},{9,8},{10,11... | collective-permute-start | bytes 1769480 | tf_op jit(solution)/shard_map/ppermute | solution.py:1003
  153.4 17.4 %collective-permute-start.21 = (bf16[48,1536]{1,0:T(8,128)(2,1)S(1)}, bf16[48,1536]{1,0:T(8,128)(2,1)S(1)}, u32[]{:S(2)}, u32[]{:S(2)}) collective-permute-start(bf16[48,1536]{1,0:T(8,128)(2,1)S(1)} %get-tuple-element.110), channel_id=1, source_target_pairs={{0,4},{1,5},{2,6},{3,7},{4,0},{5,1},{6,2},{7,3},{8,12},{9,13},{10,... | collective-permute-start | bytes 442376 | tf_op jit(solution)/shard_map/ppermute | solution.py:1003
  153.7 18.6 %collective-permute-start.22 = (bf16[48,1536]{1,0:T(8,128)(2,1)S(1)}, bf16[48,1536]{1,0:T(8,128)(2,1)S(1)}, u32[]{:S(2)}, u32[]{:S(2)}) collective-permute-start(bf16[48,1536]{1,0:T(8,128)(2,1)S(1)} %get-tuple-element.111), channel_id=1, source_target_pairs={{0,8},{1,9},{2,10},{3,11},{4,12},{5,13},{6,14},{7,15},{8,0},{9,1},... | collective-permute-start | bytes 442376 | tf_op jit(solution)/shard_map/ppermute | solution.py:1003
  156.1 16.1 %collective-permute-start.23 = (bf16[48,1536]{1,0:T(8,128)(2,1)S(1)}, bf16[48,1536]{1,0:T(8,128)(2,1)S(1)}, u32[]{:S(2)}, u32[]{:S(2)}) collective-permute-start(bf16[48,1536]{1,0:T(8,128)(2,1)S(1)} %get-tuple-element.112), channel_id=1, source_target_pairs={{0,12},{1,13},{2,14},{3,15},{4,8},{5,9},{6,10},{7,11},{8,4},{9,5},... | collective-permute-start | bytes 442376 | tf_op jit(solution)/shard_map/ppermute | solution.py:1003
  164.9 8.1 %collective-permute-start.16 = (bf16[24,8,768]{2,1,0:T(8,128)(2,1)}, bf16[24,8,768]{2,1,0:T(8,128)(2,1)S(1)}, u32[]{:S(2)}, u32[]{:S(2)}) collective-permute-start(bf16[24,8,768]{2,1,0:T(8,128)(2,1)} %get-tuple-element.102), channel_id=1, source_target_pairs={{0,16},{16,0},{1,17},{17,1},{2,18},{18,2},{3,19},{19,3},{4,20},{20... | collective-permute-start | bytes 884744 | tf_op jit(solution)/shard_map/ppermute | solution.py:1003
  169.3 8.9 %collective-permute-start.19 = (bf16[192,768]{1,0:T(8,128)(2,1)}, bf16[192,768]{1,0:T(8,128)(2,1)S(1)}, u32[]{:S(2)}, u32[]{:S(2)}) collective-permute-start(bf16[192,768]{1,0:T(8,128)(2,1)} %get-tuple-element.106), channel_id=1, source_target_pairs={{0,2},{1,3},{2,0},{3,1},{4,6},{5,7},{6,4},{7,5},{8,10},{9,11},{10,... | collective-permute-start | bytes 884744 | tf_op jit(solution)/shard_map/ppermute | solution.py:1003
  170.8 9.7 %collective-permute-start.20 = (bf16[192,896]{1,0:T(8,128)(2,1)}, bf16[192,896]{1,0:T(8,128)(2,1)S(1)}, u32[]{:S(2)}, u32[]{:S(2)}) collective-permute-start(bf16[192,896]{1,0:T(8,128)(2,1)} %get-tuple-element.107), channel_id=1, source_target_pairs={{0,1},{1,0},{2,3},{3,2},{4,5},{5,4},{6,7},{7,6},{8,9},{9,8},{10,11... | collective-permute-start | bytes 1032200 | tf_op jit(solution)/shard_map/ppermute | solution.py:1003
  180.6 12.6 %collective-permute-start.24 = (bf16[48,1664]{1,0:T(8,128)(2,1)S(1)}, bf16[48,1664]{1,0:T(8,128)(2,1)S(1)}, u32[]{:S(2)}, u32[]{:S(2)}) collective-permute-start(bf16[48,1664]{1,0:T(8,128)(2,1)S(1)} %get-tuple-element.114), channel_id=1, source_target_pairs={{0,4},{1,5},{2,6},{3,7},{4,0},{5,1},{6,2},{7,3},{8,12},{9,13},{10,... | collective-permute-start | bytes 479240 | tf_op jit(solution)/shard_map/ppermute | solution.py:1003
  180.7 13.8 %collective-permute-start.25 = (bf16[48,1664]{1,0:T(8,128)(2,1)S(1)}, bf16[48,1664]{1,0:T(8,128)(2,1)S(1)}, u32[]{:S(2)}, u32[]{:S(2)}) collective-permute-start(bf16[48,1664]{1,0:T(8,128)(2,1)S(1)} %get-tuple-element.115), channel_id=1, source_target_pairs={{0,8},{1,9},{2,10},{3,11},{4,12},{5,13},{6,14},{7,15},{8,0},{9,1},... | collective-permute-start | bytes 479240 | tf_op jit(solution)/shard_map/ppermute | solution.py:1003
  183.3 11.2 %collective-permute-start.26 = (bf16[48,1664]{1,0:T(8,128)(2,1)S(1)}, bf16[48,1664]{1,0:T(8,128)(2,1)S(1)}, u32[]{:S(2)}, u32[]{:S(2)}) collective-permute-start(bf16[48,1664]{1,0:T(8,128)(2,1)S(1)} %get-tuple-element.116), channel_id=1, source_target_pairs={{0,12},{1,13},{2,14},{3,15},{4,8},{5,9},{6,10},{7,11},{8,4},{9,5},... | collective-permute-start | bytes 479240 | tf_op jit(solution)/shard_map/ppermute | solution.py:1003
  (27 other events, 80.6 us)

commit v3 on v2

--- a/solution.py
+++ b/solution.py
@@ -722,7 +722,6 @@
     load_qkv = load(dqkv_any, dqkv, sems.at[2])
     load_a = load(at_any, at, sems.at[3])
     blocks, block = at.shape[:2]
-    loads_t = [load(src, dst, turn_sems[0].at[i]) for i, (src, dst) in enumerate(zip(turn, held))]
     load_dm.wait()
     dmb[...] = dm[...].astype(BF16)
     load_o.wait()
@@ -738,12 +737,6 @@
         return carry
 
     lax.fori_loop(0, 2, project, 0)
-    for c in loads_t:
-        c.wait()
-    for side in range(len(turned) // 2):
-        total = held[2 * side][...].astype(F32) + held[2 * side + 1][...].astype(F32)
-        turned[side][...] = total[:quarter]
-        turned[2 + side][...] = total[quarter:].astype(BF16)
     load_qkv.wait()
     load_a.wait()
     for c in loads_w:
@@ -761,7 +754,8 @@
         inner_v[...] = acc
         return carry
 
-    lax.fori_loop(0, 6, attend_in, 0)
+    loads_t = [load(src, dst, turn_sems[0].at[i]) for i, (src, dst) in enumerate(zip(turn, held))]
+    lax.fori_loop(0, 6, attend_in, 0, unroll=2)
 
     def move(src, out, side, lanes, slot):
         return [
@@ -779,6 +773,12 @@
         for part in range(4):
             out = (out_a, out_b)[part // 2]
             stores += move(grads.at[hh, part], out, part // 2, (part % 2) * half, 20 * k + 4 * part)
+    for c in loads_t:
+        c.wait()
+    for side in range(len(turned) // 2):
+        total = held[2 * side][...].astype(F32) + held[2 * side + 1][...].astype(F32)
+        turned[side][...] = total[:quarter]
+        turned[2 + side][...] = total[quarter:].astype(BF16)
     inner = inner_v[...]
     inner = jnp.sum(inner, axis=1, keepdims=True)
     sums = jnp.sum(dqkv[...].astype(F32), axis=0, keepdims=True)

time: 197 us -> 195 us (0.990)
  Pallas kernels: 115 us -> 113 us
where the time goes in v3:
time: 195 us; the launch traced here: 194 us
  Pallas kernels  113 us (58%)
  starting transfers between devices  35.6 us (18%)
  waiting for transfers between devices  31.1 us (16%)
  local copies, waits for them, and re-layouts  9.22 us (5%)
  other arithmetic  2.74 us (1%)
  between operations  2.34 us (1%)
    pallas_call x12, Pallas kernels, call(): pl.pallas_call(kernel, name=name, in_specs=in_specs, out_shape=[jax.Shape...  113 us
    ppermute x27, waiting for transfers between devices, xor_permute(): lax.ppermute(x, axis, [(i, i ^ bit) for i in range(lax.axis_size(axis))])  31 us
    ppermute x27, starting transfers between devices, xor_permute(): lax.ppermute(x, axis, [(i, i ^ bit) for i in range(lax.axis_size(axis))])  27.1 us
    unnamed x68, local copies, waits for them, and re-layouts  8.61 us
    all_to_all x1, starting transfers between devices, body(): text_all = lax.all_to_all(text_send, 'dp', 0, 0, tiled=True)  8.46 us
  transfers between devices with their start and end apart: 28, of which 11 were waited for; matrix products, arithmetic and copies ran while one was open for 2% of the time, Pallas kernels for 33%

profile of v3, /device:TPU:0, one launch (start us, length us, event | category | flops | bytes accessed | tf_op | source)
XLA Modules:
  0.0 194.3 jit_solution(16359292446715627133)
XLA Ops:
  1.9 15.5 %text_forward.1 = (bf16[16,48,384]{2,1,0:T(8,128)(2,1)}, bf16[384,2304]{1,0:T(8,128)(2,1)}, bf16[16,48,384]{2,1,0:T(8,128)(2,1)}, f32[384,768]{1,0:T(8,128)}, bf...) custom-call(s32[36]{0:T(128)} %concatenate.13.scal, ...), custom_call_target="tpu_custom_call" | custom-call | flops 3623878656 | bytes 20000000 | tf_op jit(solution)/shard_map/text_forward/pallas_call | solution.py:1070
  17.4 8.5 %all-to-all-start = ((bf16[16,24,1024]{2,1,0:T(8,128)(2,1)}), bf16[16,24,1024]{2,1,0:T(8,128)(2,1)S(1)}, u32[]{:S(2)}, u32[]{:S(2)}) async-start(bf16[16,24,1024]{2,1,0:T(8,128)(2,1)} %get-tuple-element.70), calls=%async_computation | async-start | bytes 1572864 | tf_op jit(solution)/shard_map/all_to_all | solution.py:1133
  26.5 28.7 %image_forward.1 = bf16[24,768]{1,0:T(8,128)(2,1)} custom-call(s32[36]{0:T(128)} %concatenate.13.scal, bf16[50,48,768]{2,1,0:T(8,128)(2,1)} %bitcast.18, bf16[2,768]{1,0:T(2,128)(2,1)} %gains.5, bf16[6,768]{1,0:T(8,128)(2,1)} %biases.3, bf16[24,128]{1,0:T(8,128)(2,1)} %bitcast.19, bf16[768,2304]{1,0:T(8,128)(2,1)} %wq_any.4, bf16[768,768]{1,0:T(8,128)(2,1)} %wp_any.3, ...), custom_call_target="tpu_custom_call" | custom-call | flops 12683575296 | bytes 20000000 | tf_op jit(solution)/shard_map/image_forward/pallas_call | solution.py:1070
  55.2 3.8 %collective-permute-start.2 = (bf16[1,24,768]{2,1,0:T(8,128)(2,1)}, bf16[1,24,768]{2,1,0:T(8,128)(2,1)S(1)}, u32[]{:S(2)}, u32[]{:S(2)}) collective-permute-start(bf16[1,24,768]{2,1,0:T(8,128)(2,1)} %bitcast.13), channel_id=1, source_target_pairs={{0,12},{1,13},{2,14},{3,15},{4,8},{5,9},{6,10},{7,11},{8,4},{9,5},... | collective-permute-start | bytes 110600 | tf_op jit(solution)/shard_map/ppermute | solution.py:1003
  61.3 2.8 %collective-permute-done.1 = bf16[1,24,768]{2,1,0:T(8,128)(2,1)S(1)} collective-permute-done((bf16[1,24,768]{2,1,0:T(8,128)(2,1)}, bf16[1,24,768]{2,1,0:T(8,128)(2,1)S(1)}, u32[]{:S(2)}, u32[]{:S(2)}) %collective-permute-start.1) | collective-permute-done | bytes 36896 | tf_op jit(solution)/shard_map/ppermute | solution.py:1003
  64.9 1.5 collective-permute-start.4
  66.4 1.5 collective-permute-start.3
  67.9 3.7 %collective-permute-done.3.refs_1_ = bf16[4,24,768]{2,1,0:T(8,128)(2,1)S(1)} collective-permute-done((bf16[4,24,768]{2,1,0:T(8,128)(2,1)S(1)}, bf16[4,24,768]{2,1,0:T(8,128)(2,1)S(1)}, u32[]{:S(2)}, u32[]{:S(2)}) %collective-permute-start.3) | collective-permute-done | bytes 147488 | tf_op jit(solution)/shard_map/ppermute | solution.py:1003
  71.6 1.5 collective-permute-start.5
  73.1 4.5 %collective-permute-done.5.refs_3_ = bf16[4,24,768]{2,1,0:T(8,128)(2,1)S(1)} collective-permute-done((bf16[4,24,768]{2,1,0:T(8,128)(2,1)S(1)}, bf16[4,24,768]{2,1,0:T(8,128)(2,1)S(1)}, u32[]{:S(2)}, u32[]{:S(2)}) %collective-permute-start.5) | collective-permute-done | bytes 147488 | tf_op jit(solution)/shard_map/ppermute | solution.py:1003
  78.4 1.3 collective-permute-done.6.refs_4_
  80.9 16.6 %loss.1 = (f32[1,1]{1,0:T(1,128)}, f32[1,1]{1,0:T(1,128)}, bf16[384,768]{1,0:T(8,128)(2,1)}, bf16[384,768]{1,0:T(8,128)(2,1)}, bf16[384,768]{1,0:T(8,128)(2,1)},...) custom-call(s32[36]{0:T(128)} %concatenate.13.scal, ...), custom_call_target="tpu_custom_call" | custom-call | flops 2717908992 | bytes 20000000 | tf_op jit(solution)/shard_map/loss/pallas_call | solution.py:1070
  97.5 1.5 collective-permute-start.10
  99.6 18.9 %middle_back.1 = (f32[384,768]{1,0:T(8,128)}, bf16[384,2304]{1,0:T(8,128)(2,1)}, f32[8,768]{1,0:T(8,128)}) custom-call(s32[36]{0:T(128)} %concatenate.13.scal, f32[384,768]{1,0:T(8,128)} %get-tuple-element.80.dc_any, f32[24,768]{1,0:T(8,128)} %get-tuple-element.81.dy, bf16[384,1536]{1,0:T(8,128)(2,1)} %get-tuple-element.76.gps_any, ...), custom_call_target="tpu_custom_call" | custom-call | flops 3623878656 | bytes 20000000 | tf_op jit(solution)/shard_map/middle_back/pallas_call | solution.py:1070
  119.6 12.5 %weight_grad.1 = (bf16[2,384,768]{2,1,0:T(8,128)(2,1)}, bf16[2,384,896]{2,1,0:T(8,128)(2,1)}, bf16[2,384,768]{2,1,0:T(8,128)(2,1)}, bf16[2,384,896]{2,1,0:T(8,12...) custom-call(s32[36]{0:T(128)} %concatenate.13.scal, ...), custom_call_target="tpu_custom_call" | custom-call | flops 1811939328 | bytes 20000000 | tf_op jit(solution)/shard_map/weight_grad/pallas_call | solution.py:1070
  132.6 1.5 collective-permute-start.14
  134.6 7.2 %collective-permute-done.14.far_a.hop_a = bf16[192,768]{1,0:T(8,128)(2,1)S(1)} collective-permute-done((bf16[192,768]{1,0:T(8,128)(2,1)}, bf16[192,768]{1,0:T(8,128)(2,1)S(1)}, u32[]{:S(2)}, u32[]{:S(2)}) %collective-permute-start.14) | collective-permute-done | bytes 294944 | tf_op jit(solution)/shard_map/ppermute | solution.py:1003
  141.8 1.2 collective-permute-done.15.far_b.hop_b
  144.6 3.1 %wire.1 = (bf16[384,768]{1,0:T(8,128)(2,1)}, bf16[384,896]{1,0:T(8,128)(2,1)}) custom-call(bf16[2,384,768]{2,1,0:T(8,128)(2,1)} %get-tuple-element.94.qa.refs_0_, bf16[2,384,768]{2,1,0:T(8,128)(2,1)} %copy-done.18, bf16[2,384,896]{2,1,0:T(8,128)(2,1)} %get-tuple-element.96.qb.refs_3_, bf16[2,384,896]{2,1,0:T(8,128)(2,1)} %copy-done.17, ...), custom_call_target="tpu_custom_call" | custom-call | flops 1000000 | bytes 4000000 | tf_op jit(solution)/shard_map/wire/pallas_call | solution.py:1070
  152.3 2.4 %collective-permute-start.22 = (bf16[48,1536]{1,0:T(8,128)(2,1)S(1)}, bf16[48,1536]{1,0:T(8,128)(2,1)S(1)}, u32[]{:S(2)}, u32[]{:S(2)}) collective-permute-start(bf16[48,1536]{1,0:T(8,128)(2,1)S(1)} %get-tuple-element.111), channel_id=1, source_target_pairs={{0,8},{1,9},{2,10},{3,11},{4,12},{5,13},{6,14},{7,15},{8,0},{9,1},... | collective-permute-start | bytes 442376 | tf_op jit(solution)/shard_map/ppermute | solution.py:1003
  154.8 1.8 collective-permute-start.23
  156.5 6.7 %input_back.1 = (f32[24,8,768]{2,1,0:T(8,128)}, bf16[24,8,768]{2,1,0:T(8,128)(2,1)}) custom-call(s32[36]{0:T(128)} %concatenate.13.scal, f32[384,768]{1,0:T(8,128)} %get-tuple-element.84.dm_any, bf16[768,768]{1,0:T(8,128)(2,1)} %bitcast.12, bf16[2,768]{1,0:T(2,128)(2,1)} %gains.9, bf16[384,2304]{1,0:T(8,128)(2,1)} %get-tuple-element.85.dqkv_any, ...), custom_call_target="tpu_custom_call" | custom-call | flops 1358954496 | bytes 9000000 | tf_op jit(solution)/shard_map/input_back/pallas_call | solution.py:1070
  164.4 3.5 %turn_qkv.1 = (f32[192,768]{1,0:T(8,128)}, f32[192,832]{1,0:T(8,128)}, bf16[192,768]{1,0:T(8,128)(2,1)}, bf16[192,896]{1,0:T(8,128)(2,1)}) custom-call(bf16[2,384,768]{2,1,0:T(8,128)(2,1)} %get-tuple-element.94.qa.refs_0_, bf16[2,384,768]{2,1,0:T(8,128)(2,1)} %copy-done.18, bf16[384,768]{1,0:T(8,128)(2,1)} %copy-done.1, ...), custom_call_target="tpu_custom_call" | custom-call | flops 1000000 | bytes 4000000 | tf_op jit(solution)/shard_map/turn_qkv/pallas_call | solution.py:1070
  167.9 1.2 collective-permute-start.19
  169.2 1.5 collective-permute-start.20
  171.5 5.1 %collective-permute-done.19.hop_a = bf16[192,768]{1,0:T(8,128)(2,1)S(1)} collective-permute-done((bf16[192,768]{1,0:T(8,128)(2,1)}, bf16[192,768]{1,0:T(8,128)(2,1)S(1)}, u32[]{:S(2)}, u32[]{:S(2)}) %collective-permute-start.19) | collective-permute-done | bytes 294944 | tf_op jit(solution)/shard_map/ppermute | solution.py:1003
  176.6 2.2 %collective-permute-done.20.hop_b = bf16[192,896]{1,0:T(8,128)(2,1)S(1)} collective-permute-done((bf16[192,896]{1,0:T(8,128)(2,1)}, bf16[192,896]{1,0:T(8,128)(2,1)S(1)}, u32[]{:S(2)}, u32[]{:S(2)}) %collective-permute-start.20) | collective-permute-done | bytes 344096 | tf_op jit(solution)/shard_map/ppermute | solution.py:1003
  179.1 2.6 %collective-permute-start.25 = (bf16[48,1664]{1,0:T(8,128)(2,1)S(1)}, bf16[48,1664]{1,0:T(8,128)(2,1)S(1)}, u32[]{:S(2)}, u32[]{:S(2)}) collective-permute-start(bf16[48,1664]{1,0:T(8,128)(2,1)S(1)} %get-tuple-element.115), channel_id=1, source_target_pairs={{0,8},{1,9},{2,10},{3,11},{4,12},{5,13},{6,14},{7,15},{8,0},{9,1},... | collective-permute-start | bytes 479240 | tf_op jit(solution)/shard_map/ppermute | solution.py:1003
  181.7 1.8 collective-permute-start.26
  185.5 6.1 %reduce_grad.1 = (f32[96,768]{1,0:T(8,128)}, f32[8,768]{1,0:T(8,128)S(1)}) custom-call(f32[1]{0:T(128)S(6)} %copy.35.refs_7_.expo, bf16[768,768]{1,0:T(8,128)(2,1)S(1)} %copy-done.7, bf16[768,768]{1,0:T(8,128)(2,1)S(1)} %copy-done.8, bf16[768,768]{1,0:T(8,128)(2,1)S(1)} %copy-done.9, bf16[768,128]{1,0:T(8,128)(2,1)S(1)} %copy-done.15, ...), custom_call_target="tpu_custom_call" | custom-call | flops 905969664 | bytes 6000000 | tf_op jit(solution)/shard_map/reduce_grad/pallas_call | solution.py:1070
  191.6 1.2 collective-permute-done.25.hop_2
  192.8 1.5 finish.1
  (111 shorter events, 18.7 us)
Async XLA Ops:
  17.4 8.6 %copy-start.20 = (bf16[384,1536]{1,0:T(8,128)(2,1)S(1)}, bf16[384,1536]{1,0:T(8,128)(2,1)}, u32[]{:S(2)}) copy-start(bf16[384,1536]{1,0:T(8,128)(2,1)} %get-tuple-element.76.gps_any) | copy-start | bytes 3538948
  17.4 37.8 %all-to-all-start = ((bf16[16,24,1024]{2,1,0:T(8,128)(2,1)}), bf16[16,24,1024]{2,1,0:T(8,128)(2,1)S(1)}, u32[]{:S(2)}, u32[]{:S(2)}) async-start(bf16[16,24,1024]{2,1,0:T(8,128)(2,1)} %get-tuple-element.70), calls=%async_computation | async-start | bytes 1572864 | tf_op jit(solution)/shard_map/all_to_all | solution.py:1133
  25.9 52.4 %collective-permute-start.9 = (bf16[16,48,384]{2,1,0:T(8,128)(2,1)}, bf16[16,48,384]{2,1,0:T(8,128)(2,1)}, u32[]{:S(2)}, u32[]{:S(2)}) collective-permute-start(bf16[16,48,384]{2,1,0:T(8,128)(2,1)} %get-tuple-element.77.refs_12_), channel_id=1, source_target_pairs={{0,16},{16,0},{1,17},{17,1},{2,18},{18,2},{3,19},{19,3},{4,20},{20... | collective-permute-start | bytes 1769480 | tf_op jit(solution)/shard_map/ppermute | solution.py:1003
  26.0 52.3 %collective-permute-start.8 = (bf16[384,1536]{1,0:T(8,128)(2,1)S(1)}, bf16[384,1536]{1,0:T(8,128)(2,1)S(1)}, u32[]{:S(2)}, u32[]{:S(2)}) collective-permute-start(bf16[384,1536]{1,0:T(8,128)(2,1)S(1)} %copy-done.20), channel_id=1, source_target_pairs={{0,16},{16,0},{1,17},{17,1},{2,18},{18,2},{3,19},{19,3},{4,20},{20... | collective-permute-start | bytes 3538952 | tf_op jit(solution)/shard_map/ppermute | solution.py:1003
  55.2 25.6 %copy-start.19 = (bf16[16,24,1024]{2,1,0:T(8,128)(2,1)}, bf16[16,24,1024]{2,1,0:T(8,128)(2,1)S(1)}, u32[]{:S(2)}) copy-start(bf16[16,24,1024]{2,1,0:T(8,128)(2,1)S(1)} %all-to-all-done.refs_5_) | copy-start | bytes 2359300
  55.2 6.1 %collective-permute-start.2 = (bf16[1,24,768]{2,1,0:T(8,128)(2,1)}, bf16[1,24,768]{2,1,0:T(8,128)(2,1)S(1)}, u32[]{:S(2)}, u32[]{:S(2)}) collective-permute-start(bf16[1,24,768]{2,1,0:T(8,128)(2,1)} %bitcast.13), channel_id=1, source_target_pairs={{0,12},{1,13},{2,14},{3,15},{4,8},{5,9},{6,10},{7,11},{8,4},{9,5},... | collective-permute-start | bytes 110600 | tf_op jit(solution)/shard_map/ppermute | solution.py:1003
  59.0 5.1 %collective-permute-start.1 = (bf16[1,24,768]{2,1,0:T(8,128)(2,1)}, bf16[1,24,768]{2,1,0:T(8,128)(2,1)S(1)}, u32[]{:S(2)}, u32[]{:S(2)}) collective-permute-start(bf16[1,24,768]{2,1,0:T(8,128)(2,1)} %bitcast.14), channel_id=1, source_target_pairs={{0,8},{1,9},{2,10},{3,11},{4,12},{5,13},{6,14},{7,15},{8,0},{9,1},... | collective-permute-start | bytes 110600 | tf_op jit(solution)/shard_map/ppermute | solution.py:1003
  59.0 5.1 %collective-permute-start = (bf16[1,24,768]{2,1,0:T(8,128)(2,1)}, bf16[1,24,768]{2,1,0:T(8,128)(2,1)S(1)}, u32[]{:S(2)}, u32[]{:S(2)}) collective-permute-start(bf16[1,24,768]{2,1,0:T(8,128)(2,1)} %bitcast.15), channel_id=1, source_target_pairs={{0,4},{1,5},{2,6},{3,7},{4,0},{5,1},{6,2},{7,3},{8,12},{9,13},{10,... | collective-permute-start | bytes 110600 | tf_op jit(solution)/shard_map/ppermute | solution.py:1003
  61.3 18.4 %collective-permute-start.7 = (bf16[16,24,1024]{2,1,0:T(8,128)(2,1)S(1)}, bf16[16,24,1024]{2,1,0:T(8,128)(2,1)S(1)}, u32[]{:S(2)}, u32[]{:S(2)}) collective-permute-start(bf16[16,24,1024]{2,1,0:T(8,128)(2,1)S(1)} %all-to-all-done.refs_5_), channel_id=1, source_target_pairs={{0,16},{16,0},{1,17},{17,1},{2,18},{18,2},{3,19},{19,3},{4,20},{20... | collective-permute-start | bytes 2359304 | tf_op jit(solution)/shard_map/ppermute | solution.py:1003
  64.9 16.0 %copy-start.27 = (bf16[4,24,768]{2,1,0:T(8,128)(2,1)}, bf16[4,24,768]{2,1,0:T(8,128)(2,1)S(1)}, u32[]{:S(2)}) copy-start(bf16[4,24,768]{2,1,0:T(8,128)(2,1)S(1)} %pad_maximum_fusion.1.refs_0_) | copy-start | bytes 442372
  64.9 8.2 %collective-permute-start.4 = (bf16[4,24,768]{2,1,0:T(8,128)(2,1)S(1)}, bf16[4,24,768]{2,1,0:T(8,128)(2,1)S(1)}, u32[]{:S(2)}, u32[]{:S(2)}) collective-permute-start(bf16[4,24,768]{2,1,0:T(8,128)(2,1)S(1)} %pad_maximum_fusion.1.refs_0_), channel_id=1, source_target_pairs={{0,2},{1,3},{2,0},{3,1},{4,6},{5,7},{6,4},{7,5},{8,10},{9,11},{10,... | collective-permute-start | bytes 442376 | tf_op jit(solution)/shard_map/ppermute | solution.py:1003
  66.4 5.1 %collective-permute-start.3 = (bf16[4,24,768]{2,1,0:T(8,128)(2,1)S(1)}, bf16[4,24,768]{2,1,0:T(8,128)(2,1)S(1)}, u32[]{:S(2)}, u32[]{:S(2)}) collective-permute-start(bf16[4,24,768]{2,1,0:T(8,128)(2,1)S(1)} %pad_maximum_fusion.1.refs_0_), channel_id=1, source_target_pairs={{0,1},{1,0},{2,3},{3,2},{4,5},{5,4},{6,7},{7,6},{8,9},{9,8},{10,11... | collective-permute-start | bytes 442376 | tf_op jit(solution)/shard_map/ppermute | solution.py:1003
  71.6 9.3 %copy-start.29 = (bf16[4,24,768]{2,1,0:T(8,128)(2,1)}, bf16[4,24,768]{2,1,0:T(8,128)(2,1)S(1)}, u32[]{:S(2)}) copy-start(bf16[4,24,768]{2,1,0:T(8,128)(2,1)S(1)} %collective-permute-done.3.refs_1_) | copy-start | bytes 442372
  71.6 6.0 %collective-permute-start.5 = (bf16[4,24,768]{2,1,0:T(8,128)(2,1)S(1)}, bf16[4,24,768]{2,1,0:T(8,128)(2,1)S(1)}, u32[]{:S(2)}, u32[]{:S(2)}) collective-permute-start(bf16[4,24,768]{2,1,0:T(8,128)(2,1)S(1)} %pad_maximum_fusion.1.refs_0_), channel_id=1, source_target_pairs={{0,3},{1,2},{2,1},{3,0},{4,7},{5,6},{6,5},{7,4},{8,11},{9,10},{10,... | collective-permute-start | bytes 442376 | tf_op jit(solution)/shard_map/ppermute | solution.py:1003
  77.6 2.1 %collective-permute-start.6 = (bf16[16,24,768]{2,1,0:T(8,128)(2,1)S(1)}, bf16[16,24,768]{2,1,0:T(8,128)(2,1)S(1)}, u32[]{:S(2)}, u32[]{:S(2)}) collective-permute-start(bf16[16,24,768]{2,1,0:T(8,128)(2,1)S(1)} %constant_dynamic-update-slice_fusion), channel_id=1, source_target_pairs={{0,16},{16,0},{1,17},{17,1},{2,18},{18,2},{3,19},{19,3},{4,20},{20... | collective-permute-start | bytes 1769480 | tf_op jit(solution)/shard_map/ppermute | solution.py:1003
  97.5 21.0 %collective-permute-start.10 = (bf16[384,768]{1,0:T(8,128)(2,1)}, bf16[384,768]{1,0:T(8,128)(2,1)S(1)}, u32[]{:S(2)}, u32[]{:S(2)}) collective-permute-start(bf16[384,768]{1,0:T(8,128)(2,1)} %get-tuple-element.91), channel_id=1, source_target_pairs={{0,1},{1,0},{2,3},{3,2},{4,5},{5,4},{6,7},{7,6},{8,9},{9,8},{10,11... | collective-permute-start | bytes 1769480 | tf_op jit(solution)/shard_map/ppermute | solution.py:1003
  99.0 19.5 %collective-permute-start.11 = (bf16[384,768]{1,0:T(8,128)(2,1)}, bf16[384,768]{1,0:T(8,128)(2,1)S(1)}, u32[]{:S(2)}, u32[]{:S(2)}) collective-permute-start(bf16[384,768]{1,0:T(8,128)(2,1)} %get-tuple-element.93), channel_id=1, source_target_pairs={{0,2},{1,3},{2,0},{3,1},{4,6},{5,7},{6,4},{7,5},{8,10},{9,11},{10,... | collective-permute-start | bytes 1769480 | tf_op jit(solution)/shard_map/ppermute | solution.py:1003
  132.0 11.0 %collective-permute-start.13 = (bf16[2,384,896]{2,1,0:T(8,128)(2,1)}, bf16[2,384,896]{2,1,0:T(8,128)(2,1)S(1)}, u32[]{:S(2)}, u32[]{:S(2)}) collective-permute-start(bf16[2,384,896]{2,1,0:T(8,128)(2,1)} %get-tuple-element.97), channel_id=1, source_target_pairs={{0,16},{16,0},{1,17},{17,1},{2,18},{18,2},{3,19},{19,3},{4,20},{20... | collective-permute-start | bytes 4128776 | tf_op jit(solution)/shard_map/ppermute | solution.py:1003
  132.1 10.9 %collective-permute-start.12 = (bf16[2,384,768]{2,1,0:T(8,128)(2,1)}, bf16[2,384,768]{2,1,0:T(8,128)(2,1)S(1)}, u32[]{:S(2)}, u32[]{:S(2)}) collective-permute-start(bf16[2,384,768]{2,1,0:T(8,128)(2,1)} %get-tuple-element.95), channel_id=1, source_target_pairs={{0,16},{16,0},{1,17},{17,1},{2,18},{18,2},{3,19},{19,3},{4,20},{20... | collective-permute-start | bytes 3538952 | tf_op jit(solution)/shard_map/ppermute | solution.py:1003
  132.6 9.2 %collective-permute-start.14 = (bf16[192,768]{1,0:T(8,128)(2,1)}, bf16[192,768]{1,0:T(8,128)(2,1)S(1)}, u32[]{:S(2)}, u32[]{:S(2)}) collective-permute-start(bf16[192,768]{1,0:T(8,128)(2,1)} %get-tuple-element.98), channel_id=1, source_target_pairs={{0,2},{1,3},{2,0},{3,1},{4,6},{5,7},{6,4},{7,5},{8,10},{9,11},{10,... | collective-permute-start | bytes 884744 | tf_op jit(solution)/shard_map/ppermute | solution.py:1003
  134.1 8.9 %collective-permute-start.15 = (bf16[192,768]{1,0:T(8,128)(2,1)}, bf16[192,768]{1,0:T(8,128)(2,1)S(1)}, u32[]{:S(2)}, u32[]{:S(2)}) collective-permute-start(bf16[192,768]{1,0:T(8,128)(2,1)} %get-tuple-element.99), channel_id=1, source_target_pairs={{0,1},{1,0},{2,3},{3,2},{4,5},{5,4},{6,7},{7,6},{8,9},{9,8},{10,11... | collective-permute-start | bytes 884744 | tf_op jit(solution)/shard_map/ppermute | solution.py:1003
  147.8 16.6 %collective-permute-start.18 = (bf16[384,896]{1,0:T(8,128)(2,1)}, bf16[384,896]{1,0:T(8,128)(2,1)}, u32[]{:S(2)}, u32[]{:S(2)}) collective-permute-start(bf16[384,896]{1,0:T(8,128)(2,1)} %get-tuple-element.100.order_any.rest_0_), channel_id=1, source_target_pairs={{0,2},{1,3},{2,0},{3,1},{4,6},{5,7},{6,4},{7,5},{8,10},{9,11},{10,... | collective-permute-start | bytes 2064392 | tf_op jit(solution)/shard_map/ppermute | solution.py:1003
  148.4 14.9 %collective-permute-start.17 = (bf16[384,768]{1,0:T(8,128)(2,1)}, bf16[384,768]{1,0:T(8,128)(2,1)S(1)}, u32[]{:S(2)}, u32[]{:S(2)}) collective-permute-start(bf16[384,768]{1,0:T(8,128)(2,1)} %get-tuple-element.103), channel_id=1, source_target_pairs={{0,1},{1,0},{2,3},{3,2},{4,5},{5,4},{6,7},{7,6},{8,9},{9,8},{10,11... | collective-permute-start | bytes 1769480 | tf_op jit(solution)/shard_map/ppermute | solution.py:1003
  152.1 17.1 %collective-permute-start.21 = (bf16[48,1536]{1,0:T(8,128)(2,1)S(1)}, bf16[48,1536]{1,0:T(8,128)(2,1)S(1)}, u32[]{:S(2)}, u32[]{:S(2)}) collective-permute-start(bf16[48,1536]{1,0:T(8,128)(2,1)S(1)} %get-tuple-element.110), channel_id=1, source_target_pairs={{0,4},{1,5},{2,6},{3,7},{4,0},{5,1},{6,2},{7,3},{8,12},{9,13},{10,... | collective-permute-start | bytes 442376 | tf_op jit(solution)/shard_map/ppermute | solution.py:1003
  152.3 18.3 %collective-permute-start.22 = (bf16[48,1536]{1,0:T(8,128)(2,1)S(1)}, bf16[48,1536]{1,0:T(8,128)(2,1)S(1)}, u32[]{:S(2)}, u32[]{:S(2)}) collective-permute-start(bf16[48,1536]{1,0:T(8,128)(2,1)S(1)} %get-tuple-element.111), channel_id=1, source_target_pairs={{0,8},{1,9},{2,10},{3,11},{4,12},{5,13},{6,14},{7,15},{8,0},{9,1},... | collective-permute-start | bytes 442376 | tf_op jit(solution)/shard_map/ppermute | solution.py:1003
  154.8 15.9 %collective-permute-start.23 = (bf16[48,1536]{1,0:T(8,128)(2,1)S(1)}, bf16[48,1536]{1,0:T(8,128)(2,1)S(1)}, u32[]{:S(2)}, u32[]{:S(2)}) collective-permute-start(bf16[48,1536]{1,0:T(8,128)(2,1)S(1)} %get-tuple-element.112), channel_id=1, source_target_pairs={{0,12},{1,13},{2,14},{3,15},{4,8},{5,9},{6,10},{7,11},{8,4},{9,5},... | collective-permute-start | bytes 442376 | tf_op jit(solution)/shard_map/ppermute | solution.py:1003
  163.3 8.1 %collective-permute-start.16 = (bf16[24,8,768]{2,1,0:T(8,128)(2,1)}, bf16[24,8,768]{2,1,0:T(8,128)(2,1)S(1)}, u32[]{:S(2)}, u32[]{:S(2)}) collective-permute-start(bf16[24,8,768]{2,1,0:T(8,128)(2,1)} %get-tuple-element.102), channel_id=1, source_target_pairs={{0,16},{16,0},{1,17},{17,1},{2,18},{18,2},{3,19},{19,3},{4,20},{20... | collective-permute-start | bytes 884744 | tf_op jit(solution)/shard_map/ppermute | solution.py:1003
  167.9 8.7 %collective-permute-start.19 = (bf16[192,768]{1,0:T(8,128)(2,1)}, bf16[192,768]{1,0:T(8,128)(2,1)S(1)}, u32[]{:S(2)}, u32[]{:S(2)}) collective-permute-start(bf16[192,768]{1,0:T(8,128)(2,1)} %get-tuple-element.106), channel_id=1, source_target_pairs={{0,2},{1,3},{2,0},{3,1},{4,6},{5,7},{6,4},{7,5},{8,10},{9,11},{10,... | collective-permute-start | bytes 884744 | tf_op jit(solution)/shard_map/ppermute | solution.py:1003
  169.2 9.7 %collective-permute-start.20 = (bf16[192,896]{1,0:T(8,128)(2,1)}, bf16[192,896]{1,0:T(8,128)(2,1)S(1)}, u32[]{:S(2)}, u32[]{:S(2)}) collective-permute-start(bf16[192,896]{1,0:T(8,128)(2,1)} %get-tuple-element.107), channel_id=1, source_target_pairs={{0,1},{1,0},{2,3},{3,2},{4,5},{5,4},{6,7},{7,6},{8,9},{9,8},{10,11... | collective-permute-start | bytes 1032200 | tf_op jit(solution)/shard_map/ppermute | solution.py:1003
  179.0 12.6 %collective-permute-start.24 = (bf16[48,1664]{1,0:T(8,128)(2,1)S(1)}, bf16[48,1664]{1,0:T(8,128)(2,1)S(1)}, u32[]{:S(2)}, u32[]{:S(2)}) collective-permute-start(bf16[48,1664]{1,0:T(8,128)(2,1)S(1)} %get-tuple-element.114), channel_id=1, source_target_pairs={{0,4},{1,5},{2,6},{3,7},{4,0},{5,1},{6,2},{7,3},{8,12},{9,13},{10,... | collective-permute-start | bytes 479240 | tf_op jit(solution)/shard_map/ppermute | solution.py:1003
  179.1 13.7 %collective-permute-start.25 = (bf16[48,1664]{1,0:T(8,128)(2,1)S(1)}, bf16[48,1664]{1,0:T(8,128)(2,1)S(1)}, u32[]{:S(2)}, u32[]{:S(2)}) collective-permute-start(bf16[48,1664]{1,0:T(8,128)(2,1)S(1)} %get-tuple-element.115), channel_id=1, source_target_pairs={{0,8},{1,9},{2,10},{3,11},{4,12},{5,13},{6,14},{7,15},{8,0},{9,1},... | collective-permute-start | bytes 479240 | tf_op jit(solution)/shard_map/ppermute | solution.py:1003
  181.7 11.1 %collective-permute-start.26 = (bf16[48,1664]{1,0:T(8,128)(2,1)S(1)}, bf16[48,1664]{1,0:T(8,128)(2,1)S(1)}, u32[]{:S(2)}, u32[]{:S(2)}) collective-permute-start(bf16[48,1664]{1,0:T(8,128)(2,1)S(1)} %get-tuple-element.116), channel_id=1, source_target_pairs={{0,12},{1,13},{2,14},{3,15},{4,8},{5,9},{6,10},{7,11},{8,4},{9,5},... | collective-permute-start | bytes 479240 | tf_op jit(solution)/shard_map/ppermute | solution.py:1003
  (27 other events, 80.5 us)
